TPU v7x, 32 devices: a whole 2x2x4 slice. The times are simulated.
32 devices in a mesh: groups: 2 (over y), tensor: 8 (over z, x), pool: 2 (over core).
Axes of the slice: x: 2, y: 2, z: 4, core: 2. Of those that a mesh axis runs over, the one named last changes fastest.
Arguments:
- hidden: bfloat16 [2048, 8192], P(('groups', 'tensor')), parts along dimension 0, may hold values from -700 to 700
- norm_gain: bfloat16 [8192], replicated, may hold values from 0.25 to 1.75
- kv_weight: bfloat16 [8192, 1024], P('tensor', 'pool'), may hold values from -0.0625 to 0.0625
- down_panels: bfloat16 [256, 2, 4096, 64], P('groups', 'pool', 'tensor'), parts along dimension 0, may hold values from -0.0625 to 0.0625
- up_panels: bfloat16 [256, 2, 32768], P('groups', 'pool', 'tensor'), parts along dimension 0, may hold values from -0.75 to 0.75
- seg_adapter: int32 [16], P('groups'), parts along dimension 0, may hold values from 0 to 127
- slot_of: int32 [256], P('groups'), parts along dimension 0, may hold values from 0 to 127, each once
Outputs:
- key_value: bfloat16 [2048, 1024], P(('groups', 'tensor'), 'pool'), parts along dimension 0
There are 2 independent parts, one for each index of `groups`. A program takes and returns all parts, laid end to end along the dimension named above; an argument that names none is the same for every part. Nothing has to cross between parts.
Inputs may be any that keep to these rules, and one draw needn't show every extreme that they name: `seg_adapter`: adapter of each segment of 128 tokens, in token order. `slot_of`: every adapter has one slot and every slot one adapter.
All inputs are finite; a program needn't handle non-finite values.
Results may differ from a plain program's by a relative error of at most 0.0054.
Values may be sent and summed in bfloat16 or wider, within the bound.
No kernel may reach another device: no remote copies, remote signals or barrier semaphores. Data moves between devices by JAX's collectives and lax.ppermute only.
A program may use at most 64 MiB of HBM per device.

v0:
```python
import jax
import jax.numpy as jnp
from jax import lax
from jax.sharding import PartitionSpec as P

SEGMENT_TOKENS = 128


def per_device(hidden, norm_gain, kv_weight, down_panels, up_panels, seg_adapter, slot_of):
    tok_rows = hidden.shape[0]
    feature_count = hidden.shape[1]
    half_width = feature_count // 2
    peer_count = lax.axis_size("tensor")
    my_half = lax.axis_index("pool")
    seg_local = tok_rows // SEGMENT_TOKENS
    values = hidden.astype(jnp.float32)
    inv_rms = lax.rsqrt(jnp.mean(values * values, axis=1, keepdims=True) + 1e-05)
    normed_input = (values * inv_rms * norm_gain.astype(jnp.float32)).astype(jnp.bfloat16)
    whole_weight = lax.all_gather(kv_weight, "tensor", axis=0, tiled=True)
    base_output = jnp.dot(normed_input, whole_weight, preferred_element_type=jnp.float32)
    adapter_ids = jnp.arange(slot_of.shape[0], dtype=jnp.int32)
    slot_indices = jnp.sum(
        jnp.where(seg_adapter[:, None] == adapter_ids[None, :], slot_of[None, :], 0), axis=1
    )
    wanted = slot_indices.reshape(peer_count, seg_local).T
    down_store = down_panels[:, 0]
    up_store = up_panels[:, 0]
    block_rows = down_store.shape[1]
    rank_width = down_store.shape[2]
    normed_half = lax.dynamic_slice_in_dim(normed_input, my_half * half_width, half_width, 1)
    got_down, up_mats = (
        lax.all_to_all(down_store[wanted], "tensor", split_axis=1, concat_axis=1, tiled=True),
        lax.all_to_all(up_store[wanted], "tensor", split_axis=1, concat_axis=1, tiled=True),
    )
    panels = got_down.reshape(seg_local, peer_count * block_rows, rank_width)
    partial_value = jnp.einsum(
        "sti,sir->str",
        normed_half.reshape(seg_local, SEGMENT_TOKENS, half_width),
        panels,
        preferred_element_type=jnp.float32,
    ).reshape(tok_rows, rank_width)
    low_rank = lax.psum(partial_value, "pool").astype(jnp.bfloat16)
    up_block = up_mats.reshape(seg_local, rank_width, -1)
    adapter_update = jnp.einsum(
        "str,srh->sth",
        low_rank.reshape(seg_local, SEGMENT_TOKENS, rank_width),
        up_block,
        preferred_element_type=jnp.float32,
    ).reshape(tok_rows, -1)
    return (base_output + adapter_update).astype(jnp.bfloat16)


def solution(mesh):
    placed = (
        P(("groups", "tensor"), None),
        P(),
        P("tensor", "pool"),
        P("groups", "pool", "tensor", None),
        P("groups", "pool", "tensor"),
        P("groups"),
        P("groups"),
    )
    return jax.shard_map(
        per_device,
        mesh=mesh,
        in_specs=placed,
        out_specs=P(("groups", "tensor"), "pool"),
        check_vma=False,
    )
```

profile of v0, /device:TPU:0, one launch (start us, length us, event | category | flops | bytes accessed | tf_op | source)
XLA Modules:
  0.0 160.6 jit_solution(15032315794286832211)
XLA Ops:
  6.5 0.0 copy-start
  6.5 0.0 copy-start.1
  6.5 0.0 all-gather.2.cloned.1.call-start
  6.5 0.7 all-gather.2.cloned.1.call-update
  7.3 1.1 select_reduce_fusion
  8.3 0.0 copy-done
  8.4 0.6 gather_fusion.1
  9.0 0.1 copy.18
  9.1 0.5 broadcast.49
  9.6 1.0 reduce.2
  10.6 0.7 reshape.69
  11.3 7.3 %all-to-all-start.1 = ((bf16[8,2,2048]{2,1,0:T(2,128)(2,1)}), bf16[8,2,2048]{2,1,0:T(2,128)(2,1)S(1)}, u32[]{:S(2)}, u32[]{:S(2)}) async-start(bf16[8,2,2048]{2,1,0:T(2,128)(2,1)} %reshape.69), calls=%async_computation.1 | async-start | bytes 131072 | tf_op jit(solution)/shard_map/all_to_all | solution.py:33
  18.5 0.7 convert_element_type.16
  19.2 5.6 %gather_fusion = bf16[8,512,64]{1,2,0:T(8,128)(2,1)} fusion(bf16[128,512,64]{1,2,0:T(8,128)(2,1)} %bitcast.29, s32[1024]{0:T(1024)S(1)} %pad_clamp_fusion), kind=kCustom, calls=%fused_computation | custom fusion | bytes 1048608 | tf_op jit(solution)/shard_map/gather | solution.py:32
  24.9 0.0 copy-done.1
  24.9 0.5 fusion
  25.4 0.2 all-to-all-done.1
  25.5 5.8 %all-to-all-start = ((bf16[1,8,512,64]{2,3,0,1:T(8,128)(2,1)}), bf16[1,8,512,64]{2,3,0,1:T(8,128)(2,1)}, u32[]{:S(2)}, u32[]{:S(2)}) async-start(bf16[1,8,512,64]{2,3,0,1:T(8,128)(2,1)} %bitcast.25), calls=%async_computation | async-start | bytes 1048576 | tf_op jit(solution)/shard_map/all_to_all | solution.py:32
  31.3 2.2 %fusion.2 = bf16[128,8192]{1,0:T(8,128)(2,1)S(1)} fusion(bf16[128,8192]{1,0:T(8,128)(2,1)} %param.7, f32[8192]{0:T(1024)S(1)} %convert_element_type.16, f32[128]{0:T(128)S(1)} %add_rsqrt_fusion), kind=kLoop, calls=%fused_computation.6 | loop fusion | flops 4194304 | bytes 4227584 | tf_op jit(solution)/shard_map/convert_element_type | solution.py:18
  33.5 0.1 reshape.70
  33.6 0.4 bitcast_reduce_fusion
  34.0 27.2 %all-to-all-done = bf16[1,8,512,64]{2,3,0,1:T(8,128)(2,1)} async-done(((bf16[1,8,512,64]{2,3,0,1:T(8,128)(2,1)}), bf16[1,8,512,64]{2,3,0,1:T(8,128)(2,1)}, u32[]{:S(2)}, u32[]{:S(2)}) %all-to-all-start) | async-done | bytes 524320 | tf_op jit(solution)/shard_map/all_to_all | solution.py:32
  61.3 1.1 copy.15
  62.3 0.5 fusion.4
  62.9 3.4 %psum.7 = bf16[128,64]{0,1:T(8,128)(2,1)S(1)} all-reduce(f32[128,64]{0,1:T(8,128)S(1)} %fusion.4), channel_id=1, replica_groups=mesh['groups'=2,'tensor'=8,'pool'=2] {'pool'}, use_global_device_ids=true, to_apply=%region_2.3 | all-reduce | flops 8192 | bytes 49152 | tf_op jit(solution)/shard_map/psum | solution.py:42
  66.3 82.0 %all-gather.2.cloned.1.call-done = bf16[8192,512]{1,0:T(8,128)(2,1)} async-done(((bf16[1024,512]{1,0:T(8,128)(2,1)}), bf16[8192,512]{1,0:T(8,128)(2,1)}) %all-gather.2.cloned.1.call-update) | async-done | bytes 8388624 | tf_op jit(solution)/shard_map/all_gather | solution.py:19
  148.2 4.6 %fusion.9 = f32[128,512]{1,0:T(8,128)S(1)} fusion(bf16[128,8192]{1,0:T(8,128)(2,1)S(1)} %fusion.2, bf16[8192,512]{1,0:T(8,128)(2,1)} %all-gather.2.cloned.1.call-done), kind=kOutput, calls=%fused_computation.21 | convolution fusion | flops 1073741824 | bytes 10747904 | tf_op jit(solution)/shard_map/dot_general | solution.py:20
  152.9 0.9 fusion.3
  (4 shorter events, 0.1 us)
Async XLA Ops:
  6.5 1.8 %copy-start = (bf16[128,1,4096]{2,0,1:T(8,128)(2,1)S(1)}, bf16[128,1,4096]{2,0,1:T(8,128)(2,1)}, u32[]{:S(2)}) copy-start(bf16[128,1,4096]{2,0,1:T(8,128)(2,1)} %param.11) | copy-start | bytes 3145732
  6.5 18.3 %copy-start.1 = (bf16[128,8192]{1,0:T(8,128)(2,1)S(1)}, bf16[128,8192]{1,0:T(8,128)(2,1)}, u32[]{:S(2)}) copy-start(bf16[128,8192]{1,0:T(8,128)(2,1)} %param.7) | copy-start | bytes 6291460
  6.5 141.7 %all-gather.2.cloned.1.call-start = ((), (), s32[]{:S(2)}) async-start(), calls=%async_computation.2 | async-start | bytes 9437184 | tf_op jit(solution)/shard_map/all_gather | solution.py:19
  11.3 14.3 %all-to-all-start.1 = ((bf16[8,2,2048]{2,1,0:T(2,128)(2,1)}), bf16[8,2,2048]{2,1,0:T(2,128)(2,1)S(1)}, u32[]{:S(2)}, u32[]{:S(2)}) async-start(bf16[8,2,2048]{2,1,0:T(2,128)(2,1)} %reshape.69), calls=%async_computation.1 | async-start | bytes 131072 | tf_op jit(solution)/shard_map/all_to_all | solution.py:33
  25.5 35.7 %all-to-all-start = ((bf16[1,8,512,64]{2,3,0,1:T(8,128)(2,1)}), bf16[1,8,512,64]{2,3,0,1:T(8,128)(2,1)}, u32[]{:S(2)}, u32[]{:S(2)}) async-start(bf16[1,8,512,64]{2,3,0,1:T(8,128)(2,1)} %bitcast.25), calls=%async_computation | async-start | bytes 1048576 | tf_op jit(solution)/shard_map/all_to_all | solution.py:32
Sparse Core Ops, SparseCore 0:
  9.5 138.7 all-gather.1
where the time goes:
time: 161 us
  waiting for transfers between devices  110 us (68%)
  between operations  13.5 us (8%)
  starting transfers between devices  13.1 us (8%)
  local copies, waits for them, and re-layouts  9.03 us (6%)
  matrix products  6.01 us (4%)
  other arithmetic  5.5 us (3%)
  blocking collectives  3.41 us (2%)
    all_gather x1, waiting for transfers between devices, per_device(): whole_weight = lax.all_gather(kv_weight, 'tensor', axis=0, tiled=True)  82 us
    all_to_all x1, waiting for transfers between devices, per_device(): lax.all_to_all(down_store[wanted], 'tensor', split_axis=1, concat_axis=1,...  27.2 us
    all_to_all x1, starting transfers between devices, per_device(): lax.all_to_all(up_store[wanted], 'tensor', split_axis=1, concat_axis=1, t...  7.25 us
    all_to_all x1, starting transfers between devices, per_device(): lax.all_to_all(down_store[wanted], 'tensor', split_axis=1, concat_axis=1,...  5.8 us
    gather x1, local copies, waits for them, and re-layouts, per_device(): down_store[wanted]  5.62 us
    dot_general x1, matrix products, per_device(): jnp.dot(normed_input, whole_weight, preferred_element_type=jnp.float32)  4.63 us
    psum x1, blocking collectives, per_device(): low_rank = lax.psum(partial_value, 'pool').astype(jnp.bfloat16)  3.41 us
  transfers between devices with their start and end apart: 3, of which 3 were waited for; matrix products, arithmetic and copies ran while one was open for 9% of the time, Pallas kernels for 0%

commit v1 on v0

v1 whole, which is shorter than its diff:
```python
import functools

import jax
import jax.numpy as jnp
from jax import lax
from jax.experimental import pallas as pl
from jax.experimental.pallas import tpu as pltpu
from jax.sharding import PartitionSpec as P

SEGMENT_TOKENS = 128
EPS = 1e-05
VMEM_LIMIT = 48 * 1024 * 1024
PAD_ROWS = 16


def params():
    return pltpu.CompilerParams(vmem_limit_bytes=VMEM_LIMIT)


def gather_kernel(peers, place, seg, slot_of, down, up, *rest):
    outs, sem = rest[:peers], rest[peers]
    me = place[0]
    rank, feats = down.shape[1:]
    up_rows = up.shape[1] // feats
    copies = []
    row = lax.broadcasted_iota(jnp.int32, (PAD_ROWS, up.shape[0]), 0)
    col = lax.broadcasted_iota(jnp.int32, (PAD_ROWS, up.shape[0]), 1)
    hot = jnp.zeros((PAD_ROWS, up.shape[0]), jnp.float32)
    for k in range(peers):
        slot = slot_of[seg[me ^ k]]
        copy = pltpu.make_async_copy(down.at[slot], outs[k].at[pl.ds(0, rank)], sem.at[k])
        copy.start()
        copies.append(copy)
        hot = jnp.where((row == k) & (col == slot), 1.0, hot)
    picked = jnp.dot(hot.astype(jnp.bfloat16), up[...], preferred_element_type=jnp.float32)
    for k in range(peers):
        rows = [picked[k : k + 1, r * feats : (r + 1) * feats] for r in range(up_rows)]
        rows.append(jnp.zeros((PAD_ROWS - up_rows, feats), jnp.float32))
        outs[k][pl.ds(rank, PAD_ROWS), :] = jnp.concatenate(rows, axis=0).astype(jnp.bfloat16)
    for copy in copies:
        copy.wait()


def norm_send_kernel(chunks, place, hidden, gain, out):
    side = place[1]
    values = hidden[...].astype(jnp.float32)
    inv = lax.rsqrt(jnp.mean(values * values, axis=1, keepdims=True) + EPS)
    half = hidden.shape[1] // 2
    chunk = half // chunks
    for part in range(2):
        first = (side if part == 0 else 1 - side) * half
        for q in range(chunks):
            at = pl.ds(pl.multiple_of(first + q * chunk, chunk), chunk)
            piece = hidden[:, at].astype(jnp.float32) * inv * gain[:, at].astype(jnp.float32)
            out[q, :, part * chunk : (part + 1) * chunk] = piece.astype(jnp.bfloat16)


def norm_half_kernel(place, hidden, gain, out):
    values = hidden[...].astype(jnp.float32)
    inv = lax.rsqrt(jnp.mean(values * values, axis=1, keepdims=True) + EPS)
    half = hidden.shape[1] // 2
    at = pl.ds(pl.multiple_of(place[2] * half, half), half)
    out[...] = (hidden[:, at].astype(jnp.float32) * inv * gain[:, at].astype(jnp.float32)).astype(jnp.bfloat16)


def partial_kernel(place, mine, other, own_w, far_w, out):
    half = place[2]
    rows = mine.shape[1]
    chunk = own_w.shape[0]
    for part, acts in ((0, mine), (1, other)):
        x = acts[0]
        total = jnp.dot(x[:, :chunk], own_w[...], preferred_element_type=jnp.float32)
        total += jnp.dot(x[:, chunk:], far_w[...], preferred_element_type=jnp.float32)
        at = (half if part == 0 else 1 - half) * rows
        out[0, pl.ds(pl.multiple_of(at, rows), rows), :] = total.astype(jnp.bfloat16)


def rank_kernel(peers, place, acts, *rest):
    pieces, out = rest[:peers], rest[peers]
    me = place[0]
    rank = out.shape[1]
    feats = pieces[0].shape[1]
    total = jnp.zeros(out.shape, jnp.float32)
    for k in range(peers):
        x = acts[:, pl.ds(pl.multiple_of((me ^ k) * feats, feats), feats)]
        total += lax.dot_general(x, pieces[k][:rank, :], (((1,), (1,)), ((), ())), preferred_element_type=jnp.float32)
    out[...] = total


def final_kernel(peers, up_rows, place, parts, low_mine, low_other, *rest):
    pieces, out, up_full = rest[:peers], rest[peers], rest[peers + 1]
    me = place[0]
    rank = low_mine.shape[1]
    for k in range(peers):
        at = pl.ds(pl.multiple_of((me ^ k) * up_rows, up_rows), up_rows)
        up_full[at, :] = pieces[k][rank : rank + PAD_ROWS, :].astype(jnp.float32)[:up_rows]
    low = (low_mine[...] + low_other[...]).astype(jnp.bfloat16)
    total = jnp.dot(low, up_full[...].astype(jnp.bfloat16), preferred_element_type=jnp.float32)
    for q in range(parts.shape[0]):
        total += parts[q].astype(jnp.float32)
    out[...] = total.astype(jnp.bfloat16)


def whole(shape):
    return pl.BlockSpec(shape, lambda *_: (0,) * len(shape))


def call(kernel, prefetch, args, in_specs, outs, out_specs, grid=(1,), scratch=(), name=None, flops=0, nbytes=0):
    return pl.pallas_call(
        kernel,
        grid_spec=pltpu.PrefetchScalarGridSpec(
            num_scalar_prefetch=len(prefetch),
            grid=grid,
            in_specs=in_specs,
            out_specs=out_specs,
            scratch_shapes=scratch,
        ),
        out_shape=outs,
        compiler_params=params(),
        cost_estimate=pl.CostEstimate(flops=flops, bytes_accessed=nbytes, transcendentals=0),
        name=name,
    )(*prefetch, *args)


def cube_device(hidden, norm_gain, kv_weight, down_panels, up_panels, seg_adapter, slot_of):
    tokens, features = hidden.shape
    groups, peers = lax.axis_size("groups"), lax.axis_size("tensor")
    g, t, h = (lax.axis_index(axis) for axis in ("groups", "tensor", "pool"))
    lows = peers // 2
    cube = groups * lows
    chunk = kv_weight.shape[0] // groups
    cols = kv_weight.shape[1]
    rows = tokens // 2
    feats, rank = down_panels.shape[2:]
    bf16, f32 = jnp.bfloat16, jnp.float32
    place = jnp.stack([t, t // lows, h]).astype(jnp.int32)
    swap = [(i, i ^ lows) for i in range(peers)]
    cubes = [[a * peers + s * lows + l for l in range(lows) for a in range(groups)] for s in range(2)]
    gain = norm_gain.reshape(1, features)
    up_rows = up_panels.shape[2] // feats

    own_w = lax.dynamic_slice_in_dim(kv_weight, g * chunk, chunk, 0)
    far_w = lax.ppermute(own_w, "tensor", swap)

    send = call(
        functools.partial(norm_send_kernel, cube), [place], [hidden, gain],
        [pl.BlockSpec((rows, features), lambda i, p: (p[2], 0)), whole((1, features))],
        jax.ShapeDtypeStruct((cube, rows, 2 * chunk), bf16), whole((cube, rows, 2 * chunk)),
        name="norm_send", flops=6 * rows * features, nbytes=4 * rows * features,
    )
    mine = lax.all_to_all(
        send, ("groups", "tensor"), split_axis=0, concat_axis=0, tiled=True, axis_index_groups=cubes
    )

    piece_shape = (rank + PAD_ROWS, feats)
    pieces = call(
        functools.partial(gather_kernel, peers), [place, seg_adapter, slot_of],
        [down_panels[:, 0].transpose(0, 2, 1), up_panels[:, 0]],
        [pl.BlockSpec(memory_space=pl.ANY), whole((up_panels.shape[0], up_panels.shape[2]))],
        [jax.ShapeDtypeStruct(piece_shape, bf16)] * peers, [whole(piece_shape)] * peers,
        scratch=[pltpu.SemaphoreType.DMA((peers,))], name="pick_panels", nbytes=3 << 20,
    )
    pieces = [pieces[0]] + [
        lax.ppermute(pieces[k], "tensor", [(i, i ^ k) for i in range(peers)]) for k in range(1, peers)
    ]
    acts = call(
        norm_half_kernel, [place], [hidden, gain], [whole((tokens, features)), whole((1, features))],
        jax.ShapeDtypeStruct((tokens, features // 2), bf16), whole((tokens, features // 2)),
        name="norm_half", flops=6 * tokens * features, nbytes=4 * tokens * features,
    )

    other = lax.ppermute(mine, "pool", [(0, 1), (1, 0)])
    block = pl.BlockSpec((1, rows, 2 * chunk), lambda i, p: (i, 0, 0))
    partial = call(
        partial_kernel, [place], [mine, other, own_w, far_w],
        [block, block, whole((chunk, cols)), whole((chunk, cols))],
        jax.ShapeDtypeStruct((cube, tokens, cols), bf16),
        pl.BlockSpec((1, tokens, cols), lambda i, p: (i, 0, 0)), grid=(cube,),
        name="partial", flops=4 * cube * tokens * chunk * cols, nbytes=4 << 20,
    )
    parts = lax.all_to_all(
        partial, ("groups", "tensor"), split_axis=0, concat_axis=0, tiled=True, axis_index_groups=cubes
    )

    low_mine = call(
        functools.partial(rank_kernel, peers), [place], [acts, *pieces],
        [whole(acts.shape)] + [whole(piece_shape)] * peers,
        jax.ShapeDtypeStruct((tokens, rank), f32), whole((tokens, rank)),
        name="low_rank", flops=2 * tokens * rank * features // 2, nbytes=2 << 20,
    )
    low_other = lax.ppermute(low_mine, "pool", [(0, 1), (1, 0)])
    return call(
        functools.partial(final_kernel, peers, up_rows), [place], [parts, low_mine, low_other, *pieces],
        [whole(parts.shape), whole((tokens, rank)), whole((tokens, rank))] + [whole(piece_shape)] * peers,
        jax.ShapeDtypeStruct((tokens, cols), bf16), whole((tokens, cols)),
        scratch=[pltpu.VMEM((rank, cols), f32)], name="final", flops=4 * tokens * rank * cols, nbytes=3 << 20,
    )


def gathered_device(hidden, norm_gain, kv_weight, down_panels, up_panels, seg_adapter, slot_of):
    tok_rows = hidden.shape[0]
    half_width = hidden.shape[1] // 2
    peer_count = lax.axis_size("tensor")
    my_half = lax.axis_index("pool")
    seg_local = tok_rows // SEGMENT_TOKENS
    values = hidden.astype(jnp.float32)
    inv_rms = lax.rsqrt(jnp.mean(values * values, axis=1, keepdims=True) + EPS)
    normed = (values * inv_rms * norm_gain.astype(jnp.float32)).astype(jnp.bfloat16)
    weight = lax.all_gather(kv_weight, "tensor", axis=0, tiled=True)
    base = jnp.dot(normed, weight, preferred_element_type=jnp.float32)
    wanted = slot_of[seg_adapter].reshape(peer_count, seg_local).T
    down_store, up_store = down_panels[:, 0], up_panels[:, 0]
    rank_width = down_store.shape[2]
    normed_half = lax.dynamic_slice_in_dim(normed, my_half * half_width, half_width, 1)
    got_down = lax.all_to_all(down_store[wanted], "tensor", split_axis=1, concat_axis=1, tiled=True)
    up_mats = lax.all_to_all(up_store[wanted], "tensor", split_axis=1, concat_axis=1, tiled=True)
    low_rank = jnp.einsum(
        "sti,sir->str",
        normed_half.reshape(seg_local, SEGMENT_TOKENS, half_width),
        got_down.reshape(seg_local, half_width, rank_width),
        preferred_element_type=jnp.float32,
    )
    low_rank = lax.psum(low_rank, "pool").astype(jnp.bfloat16)
    update = jnp.einsum(
        "str,srh->sth",
        low_rank,
        up_mats.reshape(seg_local, rank_width, -1),
        preferred_element_type=jnp.float32,
    )
    return (base + update.reshape(tok_rows, -1)).astype(jnp.bfloat16)


def per_device(hidden, norm_gain, kv_weight, down_panels, up_panels, seg_adapter, slot_of):
    peers, groups = lax.axis_size("tensor"), lax.axis_size("groups")
    feats = down_panels.shape[2]
    fits = (
        hidden.shape[0] == SEGMENT_TOKENS
        and lax.axis_size("pool") == 2
        and peers in (2, 4, 8)
        and kv_weight.shape[0] % (128 * groups) == 0
        and feats == kv_weight.shape[1]
        and up_panels.shape[2] % (8 * feats) == 0
        and up_panels.shape[2] // feats <= PAD_ROWS
    )
    body = cube_device if fits else gathered_device
    return body(hidden, norm_gain, kv_weight, down_panels, up_panels, seg_adapter, slot_of)


def solution(mesh):
    placed = (
        P(("groups", "tensor"), None),
        P(),
        P("tensor", "pool"),
        P("groups", "pool", "tensor", None),
        P("groups", "pool", "tensor"),
        P("groups"),
        P("groups"),
    )
    return jax.shard_map(
        per_device,
        mesh=mesh,
        in_specs=placed,
        out_specs=P(("groups", "tensor"), "pool"),
        check_vma=False,
    )
```

time: 161 us -> 99.7 us (0.62)
  waiting for transfers between devices: 110 us -> 36.5 us
  blocking collectives: 3.41 us -> 21.3 us
  Pallas kernels: 0 us -> 14.9 us
  between operations: 13.5 us -> 0.22 us
  matrix products: 6.01 us -> 0 us
  other arithmetic: 5.5 us -> 0.08 us
  starting transfers between devices: 13.1 us -> 17.5 us
    all_gather x1 -> x0, waiting for transfers between devices: 82 us -> none  [per_device(): whole_weight = lax.all_gather(kv_weight, 'tensor', axis=0, tiled=True)]
    ppermute x0 -> x10, waiting for transfers between devices: none -> 36.5 us  [the longest x1 23.9 us: cube_device(): far_w = lax.ppermute(own_w, 'tensor', swap)]
    all_to_all x2 -> x1, waiting for transfers between devices: 27.4 us -> 0.01 us  [cube_device(): lax.all_to_all(partial, ('groups', 'tensor'), split_axis=0, concat_axis=0...]
    all_to_all x0 -> x1, blocking collectives: none -> 21.3 us  [cube_device(): lax.all_to_all(send, ('groups', 'tensor'), split_axis=0, concat_axis=0, t...]
    pallas_call x0 -> x6, Pallas kernels: none -> 14.9 us  [call(): pl.pallas_call(kernel, grid_spec=pltpu.PrefetchScalarGridSpec(num_scalar_...]
    ppermute x0 -> x10, starting transfers between devices: none -> 13.3 us  [the longest x7 10.5 us: cube_device(): lax.ppermute(pieces[k], 'tensor', [(i, i ^ k) for i in range(peers)])]
    all_to_all x2 -> x1, starting transfers between devices: 13.1 us -> 4.24 us  [cube_device(): lax.all_to_all(partial, ('groups', 'tensor'), split_axis=0, concat_axis=0...]
    gather x3 -> x0, local copies, waits for them, and re-layouts: 6.31 us -> none  [the longest x1 5.62 us: per_device(): down_store[wanted]]
  transfers between devices with their start and end apart: 3 -> 11, of which waited for: 3 -> 6; matrix products, arithmetic and copies ran while one was open for 9% -> 0% of each run, Pallas kernels for 0% -> 4%
where the time goes in v1:
time: 99.7 us; the launch traced here: 99.1 us
  waiting for transfers between devices  36.5 us (37%)
  blocking collectives  21.3 us (21%)
  starting transfers between devices  17.5 us (18%)
  Pallas kernels  14.9 us (15%)
  local copies, waits for them, and re-layouts  8.56 us (9%)
    ppermute x1, waiting for transfers between devices, cube_device(): far_w = lax.ppermute(own_w, 'tensor', swap)  23.9 us
    all_to_all x1, blocking collectives, cube_device(): lax.all_to_all(send, ('groups', 'tensor'), split_axis=0, concat_axis=0, t...  21.3 us
    pallas_call x6, Pallas kernels, call(): pl.pallas_call(kernel, grid_spec=pltpu.PrefetchScalarGridSpec(num_scalar_...  14.9 us
    ppermute x7, waiting for transfers between devices, cube_device(): lax.ppermute(pieces[k], 'tensor', [(i, i ^ k) for i in range(peers)])  11.4 us
    ppermute x7, starting transfers between devices, cube_device(): lax.ppermute(pieces[k], 'tensor', [(i, i ^ k) for i in range(peers)])  10.5 us
    unnamed x36, local copies, waits for them, and re-layouts  7.69 us
    all_to_all x1, starting transfers between devices, cube_device(): lax.all_to_all(partial, ('groups', 'tensor'), split_axis=0, concat_axis=0...  4.24 us
    ppermute x1, starting transfers between devices, cube_device(): far_w = lax.ppermute(own_w, 'tensor', swap)  2.65 us
  transfers between devices with their start and end apart: 11, of which 6 were waited for; matrix products, arithmetic and copies ran while one was open for 0% of the time, Pallas kernels for 4%

profile of v1, /device:TPU:0, one launch (start us, length us, event | category | flops | bytes accessed | tf_op | source)
XLA Modules:
  0.0 99.1 jit_solution(18402271288781817098)
XLA Ops:
  0.0 0.8 reshape.3.gain
  0.9 0.1 pad_add_fusion.place
  0.9 1.6 %copy-done.1 = bf16[128,8192]{1,0:T(8,128)(2,1)S(1)} copy-done((bf16[128,8192]{1,0:T(8,128)(2,1)S(1)}, bf16[128,8192]{1,0:T(8,128)(2,1)}, u32[]{:S(2)}) %copy-start.1) | copy-done | bytes 2097176
  2.5 1.1 %norm_send.1 = bf16[8,64,1024]{2,1,0:T(8,128)(2,1)S(1)} custom-call(s32[3]{0:T(128)S(1)} %pad_add_fusion.place, bf16[128,8192]{1,0:T(8,128)(2,1)S(1)} %copy-done.1, bf16[1,8192]{1,0:T(2,128)(2,1)S(1)} %reshape.3.gain), custom_call_target="tpu_custom_call" | custom-call | flops 3145728 | bytes 2097152 | tf_op jit(solution)/shard_map/norm_send/pallas_call | solution.py:109
  3.6 21.3 %all_to_all.10.mine = bf16[8,64,1024]{2,1,0:T(8,128)(2,1)} all-to-all(bf16[8,64,1024]{2,1,0:T(8,128)(2,1)S(1)} %norm_send.1), channel_id=1, replica_groups={{0,16,2,18,4,20,6,22},{8,24,10,26,12,28,14,30},{1,17,3,19,5,21,7,23},{9..., dimensions={0} | all-to-all | bytes 2097152 | tf_op jit(solution)/shard_map/all_to_all | solution.py:151
  24.9 2.7 %collective-permute-start.1 = (bf16[512,512]{1,0:T(8,128)(2,1)S(1)}, bf16[512,512]{1,0:T(8,128)(2,1)S(1)}, u32[]{:S(2)}, u32[]{:S(2)}) collective-permute-start(bf16[512,512]{1,0:T(8,128)(2,1)S(1)} %constant_dynamic-slice_fusion.own_w), channel_id=1, source_target_pairs={{0,8},{2,10},{4,12},{6,14},{8,0},{10,2},{12,4},{14,6},{1,9},{3,11}... | collective-permute-start | bytes 1572872 | tf_op jit(solution)/shard_map/ppermute | solution.py:143
  27.6 23.9 %collective-permute-done.1.far_w = bf16[512,512]{1,0:T(8,128)(2,1)S(1)} collective-permute-done((bf16[512,512]{1,0:T(8,128)(2,1)S(1)}, bf16[512,512]{1,0:T(8,128)(2,1)S(1)}, u32[]{:S(2)}, u32[]{:S(2)}) %collective-permute-start.1) | collective-permute-done | bytes 524320 | tf_op jit(solution)/shard_map/ppermute | solution.py:143
  51.5 6.9 %partial.1 = bf16[8,128,512]{2,1,0:T(8,128)(2,1)S(1)} custom-call(s32[3]{0:T(128)S(1)} %pad_add_fusion.place, bf16[8,64,1024]{2,1,0:T(8,128)(2,1)} %all_to_all.10.mine, bf16[8,64,1024]{2,1,0:T(8,128)(2,1)} %collective-permute-done.other, bf16[512,512]{1,0:T(8,128)(2,1)S(1)} %constant_dynamic-slice_fusion.own_w, bf16[512,512]{1,0:T(8,128)(2,1)S(1)} %collective-permute-done.1.far_w), custom_call_target="tpu_custom_call" | custom-call | flops 1073741824 | bytes 4194304 | tf_op jit(solution)/shard_map/partial/pallas_call | solution.py:109
  58.4 1.0 copy-done.3
  59.4 4.2 %all-to-all-start.1 = ((bf16[8,128,512]{2,1,0:T(8,128)(2,1)}), bf16[8,128,512]{2,1,0:T(8,128)(2,1)}, u32[]{:S(2)}, u32[]{:S(2)}) async-start(bf16[8,128,512]{2,1,0:T(8,128)(2,1)} %copy-done.3), calls=%async_computation.1 | async-start | bytes 2097152 | tf_op jit(solution)/shard_map/all_to_all | solution.py:181
  63.7 1.2 %copy-done.4 = bf16[128,1,4096]{2,0,1:T(8,128)(2,1)S(1)} copy-done((bf16[128,1,4096]{2,0,1:T(8,128)(2,1)S(1)}, bf16[128,1,4096]{2,0,1:T(8,128)(2,1)}, u32[]{:S(2)}) %copy-start.4) | copy-done | bytes 1048600
  64.9 1.8 %pick_panels.1 = (bf16[80,512]{1,0:T(8,128)(2,1)S(1)}, bf16[80,512]{1,0:T(8,128)(2,1)S(1)}, bf16[80,512]{1,0:T(8,128)(2,1)S(1)}, bf16[80,512]{1,0:T(8,128)(2,1)S...) custom-call(s32[3]{0:T(128)S(1)} %pad_add_fusion.place, ...), custom_call_target="tpu_custom_call" | custom-call | bytes 3145728 | tf_op jit(solution)/shard_map/pick_panels/pallas_call | solution.py:109
  66.7 2.0 %collective-permute-start.2 = (bf16[80,512]{1,0:T(8,128)(2,1)S(1)}, bf16[80,512]{1,0:T(8,128)(2,1)S(1)}, u32[]{:S(2)}, u32[]{:S(2)}) collective-permute-start(bf16[80,512]{1,0:T(8,128)(2,1)S(1)} %get-tuple-element.14), channel_id=1, source_target_pairs={{0,2},{2,0},{4,6},{6,4},{8,10},{10,8},{12,14},{14,12},{1,3},{3,1},... | collective-permute-start | bytes 245768 | tf_op jit(solution)/shard_map/ppermute | solution.py:164
  68.7 1.5 %collective-permute-start.3 = (bf16[80,512]{1,0:T(8,128)(2,1)S(1)}, bf16[80,512]{1,0:T(8,128)(2,1)S(1)}, u32[]{:S(2)}, u32[]{:S(2)}) collective-permute-start(bf16[80,512]{1,0:T(8,128)(2,1)S(1)} %get-tuple-element.15), channel_id=1, source_target_pairs={{0,4},{2,6},{4,0},{6,2},{8,12},{10,14},{12,8},{14,10},{1,5},{3,7},... | collective-permute-start | bytes 245768 | tf_op jit(solution)/shard_map/ppermute | solution.py:164
  70.1 0.1 collective-permute-start.4
  70.3 1.4 %collective-permute-start.5 = (bf16[80,512]{1,0:T(8,128)(2,1)S(1)}, bf16[80,512]{1,0:T(8,128)(2,1)S(1)}, u32[]{:S(2)}, u32[]{:S(2)}) collective-permute-start(bf16[80,512]{1,0:T(8,128)(2,1)S(1)} %get-tuple-element.17), channel_id=1, source_target_pairs={{0,8},{2,10},{4,12},{6,14},{8,0},{10,2},{12,4},{14,6},{1,9},{3,11}... | collective-permute-start | bytes 245768 | tf_op jit(solution)/shard_map/ppermute | solution.py:164
  71.6 2.9 %collective-permute-start.6 = (bf16[80,512]{1,0:T(8,128)(2,1)S(1)}, bf16[80,512]{1,0:T(8,128)(2,1)S(1)}, u32[]{:S(2)}, u32[]{:S(2)}) collective-permute-start(bf16[80,512]{1,0:T(8,128)(2,1)S(1)} %get-tuple-element.18), channel_id=1, source_target_pairs={{0,10},{2,8},{4,14},{6,12},{8,2},{10,0},{12,6},{14,4},{1,11},{3,9}... | collective-permute-start | bytes 245768 | tf_op jit(solution)/shard_map/ppermute | solution.py:164
  74.5 6.4 %collective-permute-done.2.rest_1_ = bf16[80,512]{1,0:T(8,128)(2,1)S(1)} collective-permute-done((bf16[80,512]{1,0:T(8,128)(2,1)S(1)}, bf16[80,512]{1,0:T(8,128)(2,1)S(1)}, u32[]{:S(2)}, u32[]{:S(2)}) %collective-permute-start.2) | collective-permute-done | bytes 81952 | tf_op jit(solution)/shard_map/ppermute | solution.py:164
  80.9 1.6 %collective-permute-start.7 = (bf16[80,512]{1,0:T(8,128)(2,1)S(1)}, bf16[80,512]{1,0:T(8,128)(2,1)S(1)}, u32[]{:S(2)}, u32[]{:S(2)}) collective-permute-start(bf16[80,512]{1,0:T(8,128)(2,1)S(1)} %get-tuple-element.19), channel_id=1, source_target_pairs={{0,12},{2,14},{4,8},{6,10},{8,4},{10,6},{12,0},{14,2},{1,13},{3,15... | collective-permute-start | bytes 245768 | tf_op jit(solution)/shard_map/ppermute | solution.py:164
  82.5 1.1 %collective-permute-done.3.rest_2_ = bf16[80,512]{1,0:T(8,128)(2,1)S(1)} collective-permute-done((bf16[80,512]{1,0:T(8,128)(2,1)S(1)}, bf16[80,512]{1,0:T(8,128)(2,1)S(1)}, u32[]{:S(2)}, u32[]{:S(2)}) %collective-permute-start.3) | collective-permute-done | bytes 81952 | tf_op jit(solution)/shard_map/ppermute | solution.py:164
  83.6 1.1 %collective-permute-start.8 = (bf16[80,512]{1,0:T(8,128)(2,1)S(1)}, bf16[80,512]{1,0:T(8,128)(2,1)S(1)}, u32[]{:S(2)}, u32[]{:S(2)}) collective-permute-start(bf16[80,512]{1,0:T(8,128)(2,1)S(1)} %get-tuple-element.20), channel_id=1, source_target_pairs={{0,14},{2,12},{4,10},{6,8},{8,6},{10,4},{12,2},{14,0},{1,15},{3,13... | collective-permute-start | bytes 245768 | tf_op jit(solution)/shard_map/ppermute | solution.py:164
  84.7 0.6 copy-done.14
  85.3 1.5 %norm_half.1.acts = bf16[128,4096]{1,0:T(8,128)(2,1)S(1)} custom-call(s32[3]{0:T(128)S(1)} %copy-done.14, bf16[128,8192]{1,0:T(8,128)(2,1)S(1)} %copy-done.2, bf16[1,8192]{1,0:T(2,128)(2,1)S(1)} %copy-done.12), custom_call_target="tpu_custom_call" | custom-call | flops 6291456 | bytes 4194304 | tf_op jit(solution)/shard_map/norm_half/pallas_call | solution.py:109
  86.8 0.5 collective-permute-done.7.rest_6_
  87.4 3.4 %collective-permute-done.8.rest_7_ = bf16[80,512]{1,0:T(8,128)(2,1)S(1)} collective-permute-done((bf16[80,512]{1,0:T(8,128)(2,1)S(1)}, bf16[80,512]{1,0:T(8,128)(2,1)S(1)}, u32[]{:S(2)}, u32[]{:S(2)}) %collective-permute-start.8) | collective-permute-done | bytes 81952 | tf_op jit(solution)/shard_map/ppermute | solution.py:164
  90.8 1.0 low_rank.1.low_mine
  91.9 1.2 %collective-permute-done.9.low_other = f32[128,64]{1,0:T(8,128)S(1)} collective-permute-done((f32[128,64]{1,0:T(8,128)S(1)}, f32[128,64]{1,0:T(8,128)S(1)}, u32[]{:S(2)}, u32[]{:S(2)}) %collective-permute-start.9) | collective-permute-done | bytes 32800 | tf_op jit(solution)/shard_map/ppermute | solution.py:191
  93.1 0.9 copy-done.6
  94.0 0.9 copy-done.8
  94.9 0.9 copy-done.10
  95.8 0.6 copy-done.15
  96.4 2.7 %final.1 = bf16[128,512]{1,0:T(8,128)(2,1)} custom-call(s32[3]{0:T(128)S(1)} %copy-done.15, bf16[8,128,512]{2,1,0:T(8,128)(2,1)} %all-to-all-done.1.parts, f32[128,64]{1,0:T(8,128)S(1)} %low_rank.1.low_mine, f32[128,64]{1,0:T(8,128)S(1)} %collective-permute-done.9.low_other, bf16[80,512]{1,0:T(8,128)(2,1)S(1)} %get-tuple-element.13.rest_0_, ...), custom_call_target="tpu_custom_call" | custom-call | flops 16777216 | bytes 3145728 | tf_op jit(solution)/shard_map/final/pallas_call | solution.py:109
  (36 shorter events, 0.2 us)
Async XLA Ops:
  0.0 24.9 %copy-start = (bf16[1024,512]{1,0:T(8,128)(2,1)S(1)}, bf16[1024,512]{1,0:T(8,128)(2,1)}, u32[]{:S(2)}) copy-start(bf16[1024,512]{1,0:T(8,128)(2,1)} %param.9) | copy-start | bytes 3145732
  0.0 63.6 %copy-start.16 = (s32[8]{0:T(128)S(1)}, s32[8]{0:T(128)}, u32[]{:S(2)}) copy-start(s32[8]{0:T(128)} %seg.1) | copy-start | bytes 100
  0.0 63.6 %copy-start.17 = (s32[128]{0:T(128)S(1)}, s32[128]{0:T(128)}, u32[]{:S(2)}) copy-start(s32[128]{0:T(128)} %slot_of.1) | copy-start | bytes 1540
  0.8 24.0 %copy-start.11 = (bf16[1,8192]{1,0:T(2,128)(2,1)}, bf16[1,8192]{1,0:T(2,128)(2,1)S(1)}, u32[]{:S(2)}) copy-start(bf16[1,8192]{1,0:T(2,128)(2,1)S(1)} %reshape.3.gain) | copy-start | bytes 49156
  0.9 1.6 %copy-start.1 = (bf16[128,8192]{1,0:T(8,128)(2,1)S(1)}, bf16[128,8192]{1,0:T(8,128)(2,1)}, u32[]{:S(2)}) copy-start(bf16[128,8192]{1,0:T(8,128)(2,1)} %hidden.3) | copy-start | bytes 6291460
  2.5 64.2 %copy-start.13 = (s32[3]{0:T(128)}, s32[3]{0:T(128)S(1)}, u32[]{:S(2)}) copy-start(s32[3]{0:T(128)S(1)} %pad_add_fusion.place) | copy-start | bytes 40
  24.9 26.6 %collective-permute-start = (bf16[8,64,1024]{2,1,0:T(8,128)(2,1)}, bf16[8,64,1024]{2,1,0:T(8,128)(2,1)}, u32[]{:S(2)}, u32[]{:S(2)}) collective-permute-start(bf16[8,64,1024]{2,1,0:T(8,128)(2,1)} %all_to_all.10.mine), channel_id=1, source_target_pairs={{0,1},{1,0},{2,3},{3,2},{4,5},{5,4},{6,7},{7,6},{8,9},{9,8},{10,11... | collective-permute-start | bytes 3145736 | tf_op jit(solution)/shard_map/ppermute | solution.py:172
  24.9 59.8 %copy-start.2 = (bf16[128,8192]{1,0:T(8,128)(2,1)S(1)}, bf16[128,8192]{1,0:T(8,128)(2,1)}, u32[]{:S(2)}) copy-start(bf16[128,8192]{1,0:T(8,128)(2,1)} %hidden.3) | copy-start | bytes 6291460
  24.9 26.5 %collective-permute-start.1 = (bf16[512,512]{1,0:T(8,128)(2,1)S(1)}, bf16[512,512]{1,0:T(8,128)(2,1)S(1)}, u32[]{:S(2)}, u32[]{:S(2)}) collective-permute-start(bf16[512,512]{1,0:T(8,128)(2,1)S(1)} %constant_dynamic-slice_fusion.own_w), channel_id=1, source_target_pairs={{0,8},{2,10},{4,12},{6,14},{8,0},{10,2},{12,4},{14,6},{1,9},{3,11}... | collective-permute-start | bytes 1572872 | tf_op jit(solution)/shard_map/ppermute | solution.py:143
  58.4 1.0 copy-start.3
  59.4 33.7 %all-to-all-start.1 = ((bf16[8,128,512]{2,1,0:T(8,128)(2,1)}), bf16[8,128,512]{2,1,0:T(8,128)(2,1)}, u32[]{:S(2)}, u32[]{:S(2)}) async-start(bf16[8,128,512]{2,1,0:T(8,128)(2,1)} %copy-done.3), calls=%async_computation.1 | async-start | bytes 2097152 | tf_op jit(solution)/shard_map/all_to_all | solution.py:181
  63.7 1.2 %copy-start.4 = (bf16[128,1,4096]{2,0,1:T(8,128)(2,1)S(1)}, bf16[128,1,4096]{2,0,1:T(8,128)(2,1)}, u32[]{:S(2)}) copy-start(bf16[128,1,4096]{2,0,1:T(8,128)(2,1)} %param.11) | copy-start | bytes 3145732
  64.9 19.8 %copy-start.12 = (bf16[1,8192]{1,0:T(2,128)(2,1)S(1)}, bf16[1,8192]{1,0:T(2,128)(2,1)}, u32[]{:S(2)}) copy-start(bf16[1,8192]{1,0:T(2,128)(2,1)} %copy-done.11) | copy-start | bytes 49156
  66.7 14.2 %collective-permute-start.2 = (bf16[80,512]{1,0:T(8,128)(2,1)S(1)}, bf16[80,512]{1,0:T(8,128)(2,1)S(1)}, u32[]{:S(2)}, u32[]{:S(2)}) collective-permute-start(bf16[80,512]{1,0:T(8,128)(2,1)S(1)} %get-tuple-element.14), channel_id=1, source_target_pairs={{0,2},{2,0},{4,6},{6,4},{8,10},{10,8},{12,14},{14,12},{1,3},{3,1},... | collective-permute-start | bytes 245768 | tf_op jit(solution)/shard_map/ppermute | solution.py:164
  68.7 14.9 %collective-permute-start.3 = (bf16[80,512]{1,0:T(8,128)(2,1)S(1)}, bf16[80,512]{1,0:T(8,128)(2,1)S(1)}, u32[]{:S(2)}, u32[]{:S(2)}) collective-permute-start(bf16[80,512]{1,0:T(8,128)(2,1)S(1)} %get-tuple-element.15), channel_id=1, source_target_pairs={{0,4},{2,6},{4,0},{6,2},{8,12},{10,14},{12,8},{14,10},{1,5},{3,7},... | collective-permute-start | bytes 245768 | tf_op jit(solution)/shard_map/ppermute | solution.py:164
  70.1 16.7 %collective-permute-start.4 = (bf16[80,512]{1,0:T(8,128)(2,1)S(1)}, bf16[80,512]{1,0:T(8,128)(2,1)S(1)}, u32[]{:S(2)}, u32[]{:S(2)}) collective-permute-start(bf16[80,512]{1,0:T(8,128)(2,1)S(1)} %get-tuple-element.16), channel_id=1, source_target_pairs={{0,6},{2,4},{4,2},{6,0},{8,14},{10,12},{12,10},{14,8},{1,7},{3,5},... | collective-permute-start | bytes 245768 | tf_op jit(solution)/shard_map/ppermute | solution.py:164
  70.3 16.6 %collective-permute-start.5 = (bf16[80,512]{1,0:T(8,128)(2,1)S(1)}, bf16[80,512]{1,0:T(8,128)(2,1)S(1)}, u32[]{:S(2)}, u32[]{:S(2)}) collective-permute-start(bf16[80,512]{1,0:T(8,128)(2,1)S(1)} %get-tuple-element.17), channel_id=1, source_target_pairs={{0,8},{2,10},{4,12},{6,14},{8,0},{10,2},{12,4},{14,6},{1,9},{3,11}... | collective-permute-start | bytes 245768 | tf_op jit(solution)/shard_map/ppermute | solution.py:164
  71.6 15.2 %collective-permute-start.6 = (bf16[80,512]{1,0:T(8,128)(2,1)S(1)}, bf16[80,512]{1,0:T(8,128)(2,1)S(1)}, u32[]{:S(2)}, u32[]{:S(2)}) collective-permute-start(bf16[80,512]{1,0:T(8,128)(2,1)S(1)} %get-tuple-element.18), channel_id=1, source_target_pairs={{0,10},{2,8},{4,14},{6,12},{8,2},{10,0},{12,6},{14,4},{1,11},{3,9}... | collective-permute-start | bytes 245768 | tf_op jit(solution)/shard_map/ppermute | solution.py:164
  80.9 6.5 %collective-permute-start.7 = (bf16[80,512]{1,0:T(8,128)(2,1)S(1)}, bf16[80,512]{1,0:T(8,128)(2,1)S(1)}, u32[]{:S(2)}, u32[]{:S(2)}) collective-permute-start(bf16[80,512]{1,0:T(8,128)(2,1)S(1)} %get-tuple-element.19), channel_id=1, source_target_pairs={{0,12},{2,14},{4,8},{6,10},{8,4},{10,6},{12,0},{14,2},{1,13},{3,15... | collective-permute-start | bytes 245768 | tf_op jit(solution)/shard_map/ppermute | solution.py:164
  83.6 7.2 %collective-permute-start.8 = (bf16[80,512]{1,0:T(8,128)(2,1)S(1)}, bf16[80,512]{1,0:T(8,128)(2,1)S(1)}, u32[]{:S(2)}, u32[]{:S(2)}) collective-permute-start(bf16[80,512]{1,0:T(8,128)(2,1)S(1)} %get-tuple-element.20), channel_id=1, source_target_pairs={{0,14},{2,12},{4,10},{6,8},{8,6},{10,4},{12,2},{14,0},{1,15},{3,13... | collective-permute-start | bytes 245768 | tf_op jit(solution)/shard_map/ppermute | solution.py:164
  84.7 0.6 copy-start.14
  86.8 5.0 %copy-start.5 = (bf16[80,512]{1,0:T(8,128)(2,1)}, bf16[80,512]{1,0:T(8,128)(2,1)S(1)}, u32[]{:S(2)}) copy-start(bf16[80,512]{1,0:T(8,128)(2,1)S(1)} %collective-permute-done.6.rest_5_) | copy-start | bytes 245764
  87.4 4.5 %copy-start.7 = (bf16[80,512]{1,0:T(8,128)(2,1)}, bf16[80,512]{1,0:T(8,128)(2,1)S(1)}, u32[]{:S(2)}) copy-start(bf16[80,512]{1,0:T(8,128)(2,1)S(1)} %collective-permute-done.7.rest_6_) | copy-start | bytes 245764
  90.8 1.1 %copy-start.9 = (bf16[80,512]{1,0:T(8,128)(2,1)}, bf16[80,512]{1,0:T(8,128)(2,1)S(1)}, u32[]{:S(2)}) copy-start(bf16[80,512]{1,0:T(8,128)(2,1)S(1)} %collective-permute-done.8.rest_7_) | copy-start | bytes 245764
  91.8 1.3 %collective-permute-start.9 = (f32[128,64]{1,0:T(8,128)S(1)}, f32[128,64]{1,0:T(8,128)S(1)}, u32[]{:S(2)}, u32[]{:S(2)}) collective-permute-start(f32[128,64]{1,0:T(8,128)S(1)} %low_rank.1.low_mine), channel_id=1, source_target_pairs={{0,1},{1,0},{2,3},{3,2},{4,5},{5,4},{6,7},{7,6},{8,9},{9,8},{10,11... | collective-permute-start | bytes 98312 | tf_op jit(solution)/shard_map/ppermute | solution.py:191
  93.1 0.9 copy-start.6
  94.0 0.9 copy-start.8
  94.9 0.9 copy-start.10
  95.8 0.6 copy-start.15

commit v2 on v1

--- a/solution.py
+++ b/solution.py
@@ -9,8 +9,9 @@
 
 SEGMENT_TOKENS = 128
 EPS = 1e-05
-VMEM_LIMIT = 48 * 1024 * 1024
+VMEM_LIMIT = 16 * 1024 * 1024
 PAD_ROWS = 16
+LONG = 1 << 36
 
 
 def params():
@@ -51,7 +52,7 @@
         first = (side if part == 0 else 1 - side) * half
         for q in range(chunks):
             at = pl.ds(pl.multiple_of(first + q * chunk, chunk), chunk)
-            piece = hidden[:, at].astype(jnp.float32) * inv * gain[:, at].astype(jnp.float32)
+            piece = hidden[:, at].astype(jnp.float32) * inv * gain[at].astype(jnp.float32)[None, :]
             out[q, :, part * chunk : (part + 1) * chunk] = piece.astype(jnp.bfloat16)
 
 
@@ -60,19 +61,16 @@
     inv = lax.rsqrt(jnp.mean(values * values, axis=1, keepdims=True) + EPS)
     half = hidden.shape[1] // 2
     at = pl.ds(pl.multiple_of(place[2] * half, half), half)
-    out[...] = (hidden[:, at].astype(jnp.float32) * inv * gain[:, at].astype(jnp.float32)).astype(jnp.bfloat16)
-
-
-def partial_kernel(place, mine, other, own_w, far_w, out):
-    half = place[2]
-    rows = mine.shape[1]
+    out[...] = (hidden[:, at].astype(jnp.float32) * inv * gain[at].astype(jnp.float32)[None, :]).astype(jnp.bfloat16)
+
+
+def partial_kernel(place, acts, own_w, far_w, *rest):
+    out = rest[-1]
+    x = acts[0]
     chunk = own_w.shape[0]
-    for part, acts in ((0, mine), (1, other)):
-        x = acts[0]
-        total = jnp.dot(x[:, :chunk], own_w[...], preferred_element_type=jnp.float32)
-        total += jnp.dot(x[:, chunk:], far_w[...], preferred_element_type=jnp.float32)
-        at = (half if part == 0 else 1 - half) * rows
-        out[0, pl.ds(pl.multiple_of(at, rows), rows), :] = total.astype(jnp.bfloat16)
+    total = jnp.dot(x[:, :chunk], own_w[...], preferred_element_type=jnp.float32)
+    total += jnp.dot(x[:, chunk:], far_w[...], preferred_element_type=jnp.float32)
+    out[0] = total.astype(jnp.bfloat16)
 
 
 def rank_kernel(peers, place, acts, *rest):
@@ -105,7 +103,7 @@
     return pl.BlockSpec(shape, lambda *_: (0,) * len(shape))
 
 
-def call(kernel, prefetch, args, in_specs, outs, out_specs, grid=(1,), scratch=(), name=None, flops=0, nbytes=0):
+def call(kernel, prefetch, args, in_specs, outs, out_specs, grid=(1,), scratch=(), alias=None, name=None, flops=0, nbytes=0):
     return pl.pallas_call(
         kernel,
         grid_spec=pltpu.PrefetchScalarGridSpec(
@@ -117,6 +115,7 @@
         ),
         out_shape=outs,
         compiler_params=params(),
+        input_output_aliases=alias or {},
         cost_estimate=pl.CostEstimate(flops=flops, bytes_accessed=nbytes, transcendentals=0),
         name=name,
     )(*prefetch, *args)
@@ -136,7 +135,7 @@
     place = jnp.stack([t, t // lows, h]).astype(jnp.int32)
     swap = [(i, i ^ lows) for i in range(peers)]
     cubes = [[a * peers + s * lows + l for l in range(lows) for a in range(groups)] for s in range(2)]
-    gain = norm_gain.reshape(1, features)
+    gain = norm_gain
     up_rows = up_panels.shape[2] // feats
 
     own_w = lax.dynamic_slice_in_dim(kv_weight, g * chunk, chunk, 0)
@@ -144,39 +143,49 @@
 
     send = call(
         functools.partial(norm_send_kernel, cube), [place], [hidden, gain],
-        [pl.BlockSpec((rows, features), lambda i, p: (p[2], 0)), whole((1, features))],
+        [pl.BlockSpec((rows, features), lambda i, p: (p[2], 0)), whole((features,))],
         jax.ShapeDtypeStruct((cube, rows, 2 * chunk), bf16), whole((cube, rows, 2 * chunk)),
         name="norm_send", flops=6 * rows * features, nbytes=4 * rows * features,
     )
+    send, later = lax.optimization_barrier((send, place))
     mine = lax.all_to_all(
         send, ("groups", "tensor"), split_axis=0, concat_axis=0, tiled=True, axis_index_groups=cubes
     )
 
     piece_shape = (rank + PAD_ROWS, feats)
     pieces = call(
-        functools.partial(gather_kernel, peers), [place, seg_adapter, slot_of],
+        functools.partial(gather_kernel, peers), [later, seg_adapter, slot_of],
         [down_panels[:, 0].transpose(0, 2, 1), up_panels[:, 0]],
-        [pl.BlockSpec(memory_space=pl.ANY), whole((up_panels.shape[0], up_panels.shape[2]))],
+        [pl.BlockSpec(memory_space=pltpu.HBM), whole((up_panels.shape[0], up_panels.shape[2]))],
         [jax.ShapeDtypeStruct(piece_shape, bf16)] * peers, [whole(piece_shape)] * peers,
-        scratch=[pltpu.SemaphoreType.DMA((peers,))], name="pick_panels", nbytes=3 << 20,
+        scratch=[pltpu.SemaphoreType.DMA((peers,))], name="pick_panels", flops=LONG, nbytes=3 << 20,
     )
     pieces = [pieces[0]] + [
         lax.ppermute(pieces[k], "tensor", [(i, i ^ k) for i in range(peers)]) for k in range(1, peers)
     ]
     acts = call(
-        norm_half_kernel, [place], [hidden, gain], [whole((tokens, features)), whole((1, features))],
+        norm_half_kernel, [later], [hidden, gain], [whole((tokens, features)), whole((features,))],
         jax.ShapeDtypeStruct((tokens, features // 2), bf16), whole((tokens, features // 2)),
         name="norm_half", flops=6 * tokens * features, nbytes=4 * tokens * features,
     )
 
+    near = peers // 2
+    held = lax.optimization_barrier((mine, far_w, acts, *pieces[:near]))
+    mine, far_w, acts = held[:3]
+    pieces[:near] = held[3:]
     other = lax.ppermute(mine, "pool", [(0, 1), (1, 0)])
     block = pl.BlockSpec((1, rows, 2 * chunk), lambda i, p: (i, 0, 0))
+    weights = [whole((chunk, cols))] * 2
+    shape = jax.ShapeDtypeStruct((cube, tokens, cols), bf16)
+    work = dict(grid=(cube,), flops=2 * cube * tokens * chunk * cols, nbytes=3 << 20)
     partial = call(
-        partial_kernel, [place], [mine, other, own_w, far_w],
-        [block, block, whole((chunk, cols)), whole((chunk, cols))],
-        jax.ShapeDtypeStruct((cube, tokens, cols), bf16),
-        pl.BlockSpec((1, tokens, cols), lambda i, p: (i, 0, 0)), grid=(cube,),
-        name="partial", flops=4 * cube * tokens * chunk * cols, nbytes=4 << 20,
+        partial_kernel, [place], [mine, own_w, far_w], [block, *weights], shape,
+        pl.BlockSpec((1, rows, cols), lambda i, p: (i, p[2], 0)), name="partial_mine", **work,
+    )
+    partial = call(
+        partial_kernel, [place], [other, own_w, far_w, partial],
+        [block, *weights, pl.BlockSpec(memory_space=pl.ANY)], shape,
+        pl.BlockSpec((1, rows, cols), lambda i, p: (i, 1 - p[2], 0)), alias={4: 0}, name="partial_other", **work,
     )
     parts = lax.all_to_all(
         partial, ("groups", "tensor"), split_axis=0, concat_axis=0, tiled=True, axis_index_groups=cubes

time: 99.7 us -> 85.6 us (0.86)
  blocking collectives: 21.3 us -> 0 us
  starting transfers between devices: 17.5 us -> 24.6 us
  waiting for transfers between devices: 36.5 us -> 30.7 us
  Pallas kernels: 14.9 us -> 20 us
    ppermute x1, waiting for transfers between devices: 23.9 us -> 0.01 us  [cube_device(): far_w = lax.ppermute(own_w, 'tensor', swap)]
    all_to_all x1 -> x0, blocking collectives: 21.3 us -> none  [cube_device(): lax.all_to_all(send, ('groups', 'tensor'), split_axis=0, concat_axis=0, t...]
    ppermute x7, waiting for transfers between devices: 11.4 us -> 29.5 us  [cube_device(): lax.ppermute(pieces[k], 'tensor', [(i, i ^ k) for i in range(peers)])]
    pallas_call x6 -> x7, Pallas kernels: 14.9 us -> 20 us  [call(): pl.pallas_call(kernel, grid_spec=pltpu.PrefetchScalarGridSpec(num_scalar_...]
    all_to_all x0 -> x1, starting transfers between devices: none -> 4.74 us  [cube_device(): lax.all_to_all(send, ('groups', 'tensor'), split_axis=0, concat_axis=0, t...]
    unnamed x36 -> x26, local copies, waits for them, and re-layouts: 7.69 us -> 9.47 us
    ppermute x1, starting transfers between devices: 2.65 us -> 4.1 us  [cube_device(): far_w = lax.ppermute(own_w, 'tensor', swap)]
  transfers between devices with their start and end apart: 11 -> 12, of which waited for: 6 -> 7; matrix products, arithmetic and copies ran while one was open for 0% -> 0% of each run, Pallas kernels for 4% -> 15%
where the time goes in v2:
time: 85.6 us; the launch traced here: 85 us
  waiting for transfers between devices  30.7 us (36%)
  starting transfers between devices  24.6 us (29%)
  Pallas kernels  20 us (23%)
  local copies, waits for them, and re-layouts  9.51 us (11%)
    ppermute x7, waiting for transfers between devices, cube_device(): lax.ppermute(pieces[k], 'tensor', [(i, i ^ k) for i in range(peers)])  29.5 us
    pallas_call x7, Pallas kernels, call(): pl.pallas_call(kernel, grid_spec=pltpu.PrefetchScalarGridSpec(num_scalar_...  20 us
    ppermute x7, starting transfers between devices, cube_device(): lax.ppermute(pieces[k], 'tensor', [(i, i ^ k) for i in range(peers)])  11.3 us
    unnamed x26, local copies, waits for them, and re-layouts  9.47 us
    all_to_all x1, starting transfers between devices, cube_device(): lax.all_to_all(send, ('groups', 'tensor'), split_axis=0, concat_axis=0, t...  4.74 us
    all_to_all x1, starting transfers between devices, cube_device(): lax.all_to_all(partial, ('groups', 'tensor'), split_axis=0, concat_axis=0...  4.24 us
    ppermute x1, starting transfers between devices, cube_device(): far_w = lax.ppermute(own_w, 'tensor', swap)  4.1 us
  transfers between devices with their start and end apart: 12, of which 7 were waited for; matrix products, arithmetic and copies ran while one was open for 0% of the time, Pallas kernels for 15%

profile of v2, /device:TPU:0, one launch (start us, length us, event | category | flops | bytes accessed | tf_op | source)
XLA Modules:
  0.0 85.0 jit_solution(2118540402308126750)
XLA Ops:
  0.0 1.2 %copy-done = bf16[1024,512]{1,0:T(8,128)(2,1)S(1)} copy-done((bf16[1024,512]{1,0:T(8,128)(2,1)S(1)}, bf16[1024,512]{1,0:T(8,128)(2,1)}, u32[]{:S(2)}) %copy-start) | copy-done | bytes 1048600
  1.3 4.1 %collective-permute-start = (bf16[512,512]{1,0:T(8,128)(2,1)S(1)}, bf16[512,512]{1,0:T(8,128)(2,1)S(1)}, u32[]{:S(2)}, u32[]{:S(2)}) collective-permute-start(bf16[512,512]{1,0:T(8,128)(2,1)S(1)} %constant_dynamic-slice_fusion.own_w), channel_id=1, source_target_pairs={{0,8},{2,10},{4,12},{6,14},{8,0},{10,2},{12,4},{14,6},{1,9},{3,11}... | collective-permute-start | bytes 1572872 | tf_op jit(solution)/shard_map/ppermute | solution.py:142
  5.4 0.1 pad_add_fusion.place
  5.4 1.6 %copy-done.1 = bf16[128,8192]{1,0:T(8,128)(2,1)S(1)} copy-done((bf16[128,8192]{1,0:T(8,128)(2,1)S(1)}, bf16[128,8192]{1,0:T(8,128)(2,1)}, u32[]{:S(2)}) %copy-start.1) | copy-done | bytes 2097176
  7.0 0.7 copy-done.3
  7.8 2.0 %norm_send.1 = bf16[8,64,1024]{2,1,0:T(8,128)(2,1)} custom-call(s32[3]{0:T(128)S(1)} %pad_add_fusion.place, bf16[128,8192]{1,0:T(8,128)(2,1)S(1)} %copy-done.1, bf16[8192]{0:T(1024)(128)(2,1)S(1)} %copy-done.3), custom_call_target="tpu_custom_call" | custom-call | flops 3145728 | bytes 2097152 | tf_op jit(solution)/shard_map/norm_send/pallas_call | solution.py:107
  9.8 4.7 %all-to-all-start = ((bf16[8,64,1024]{2,1,0:T(8,128)(2,1)}), bf16[8,64,1024]{2,1,0:T(8,128)(2,1)}, u32[]{:S(2)}, u32[]{:S(2)}) async-start(bf16[8,64,1024]{2,1,0:T(8,128)(2,1)} %norm_send.1), calls=%async_computation | async-start | bytes 2097152 | tf_op jit(solution)/shard_map/all_to_all | solution.py:151
  14.5 3.4 %copy-done.5 = bf16[128,1,512,64]{2,3,1,0:T(8,128)(2,1)S(1)} copy-done((bf16[128,1,512,64]{2,3,1,0:T(8,128)(2,1)S(1)}, bf16[128,1,512,64]{2,3,1,0:T(8,128)(2,1)}, u32[]{:S(2)}) %copy-start.5) | copy-done | bytes 8388632
  17.9 1.2 %copy-done.6 = bf16[128,1,4096]{2,0,1:T(8,128)(2,1)S(1)} copy-done((bf16[128,1,4096]{2,0,1:T(8,128)(2,1)S(1)}, bf16[128,1,4096]{2,0,1:T(8,128)(2,1)}, u32[]{:S(2)}) %copy-start.6) | copy-done | bytes 1048600
  19.1 0.7 copy-done.11
  19.8 0.7 copy-done.12
  20.4 1.6 %pick_panels.1 = (bf16[80,512]{1,0:T(8,128)(2,1)S(1)}, bf16[80,512]{1,0:T(8,128)(2,1)S(1)}, bf16[80,512]{1,0:T(8,128)(2,1)S(1)}, bf16[80,512]{1,0:T(8,128)(2,1)S...) custom-call(s32[3]{0:T(128)S(1)} %pad_add_fusion.place, ...), custom_call_target="tpu_custom_call" | custom-call | flops 68719476736 | bytes 3145728 | tf_op jit(solution)/shard_map/pick_panels/pallas_call | solution.py:107
  22.1 2.1 %collective-permute-start.1 = (bf16[80,512]{1,0:T(8,128)(2,1)S(1)}, bf16[80,512]{1,0:T(8,128)(2,1)S(1)}, u32[]{:S(2)}, u32[]{:S(2)}) collective-permute-start(bf16[80,512]{1,0:T(8,128)(2,1)S(1)} %get-tuple-element.25), channel_id=1, source_target_pairs={{0,2},{2,0},{4,6},{6,4},{8,10},{10,8},{12,14},{14,12},{1,3},{3,1},... | collective-permute-start | bytes 245768 | tf_op jit(solution)/shard_map/ppermute | solution.py:164
  24.2 1.5 %collective-permute-start.2 = (bf16[80,512]{1,0:T(8,128)(2,1)S(1)}, bf16[80,512]{1,0:T(8,128)(2,1)S(1)}, u32[]{:S(2)}, u32[]{:S(2)}) collective-permute-start(bf16[80,512]{1,0:T(8,128)(2,1)S(1)} %get-tuple-element.26), channel_id=1, source_target_pairs={{0,4},{2,6},{4,0},{6,2},{8,12},{10,14},{12,8},{14,10},{1,5},{3,7},... | collective-permute-start | bytes 245768 | tf_op jit(solution)/shard_map/ppermute | solution.py:164
  25.6 0.1 collective-permute-start.3
  25.7 1.5 %norm_half.1.acts = bf16[128,4096]{1,0:T(8,128)(2,1)S(1)} custom-call(s32[3]{0:T(128)S(1)} %pad_add_fusion.place, bf16[128,8192]{1,0:T(8,128)(2,1)S(1)} %copy-done.2, bf16[8192]{0:T(1024)(128)(2,1)S(1)} %copy-done.4), custom_call_target="tpu_custom_call" | custom-call | flops 6291456 | bytes 4194304 | tf_op jit(solution)/shard_map/norm_half/pallas_call | solution.py:107
  27.2 13.3 %collective-permute-done.2.rest_2_ = bf16[80,512]{1,0:T(8,128)(2,1)S(1)} collective-permute-done((bf16[80,512]{1,0:T(8,128)(2,1)S(1)}, bf16[80,512]{1,0:T(8,128)(2,1)S(1)}, u32[]{:S(2)}, u32[]{:S(2)}) %collective-permute-start.2) | collective-permute-done | bytes 81952 | tf_op jit(solution)/shard_map/ppermute | solution.py:164
  40.5 1.8 %collective-permute-done.3.rest_3_ = bf16[80,512]{1,0:T(8,128)(2,1)S(1)} collective-permute-done((bf16[80,512]{1,0:T(8,128)(2,1)S(1)}, bf16[80,512]{1,0:T(8,128)(2,1)S(1)}, u32[]{:S(2)}, u32[]{:S(2)}) %collective-permute-start.3) | collective-permute-done | bytes 81952 | tf_op jit(solution)/shard_map/ppermute | solution.py:164
  42.5 6.7 %partial_mine.1.rest_0_ = bf16[8,128,512]{2,1,0:T(8,128)(2,1)} custom-call(s32[3]{0:T(128)S(1)} %pad_add_fusion.place, bf16[8,64,1024]{2,1,0:T(8,128)(2,1)} %all-to-all-done.acts, bf16[512,512]{1,0:T(8,128)(2,1)S(1)} %constant_dynamic-slice_fusion.own_w, bf16[512,512]{1,0:T(8,128)(2,1)S(1)} %collective-permute-done.far_w), custom_call_target="tpu_custom_call" | custom-call | flops 536870912 | bytes 3145728 | tf_op jit(solution)/shard_map/partial_mine/pallas_call | solution.py:107
  49.2 4.5 %partial_other.1 = bf16[8,128,512]{2,1,0:T(8,128)(2,1)} custom-call(s32[3]{0:T(128)S(1)} %pad_add_fusion.place, bf16[8,64,1024]{2,1,0:T(8,128)(2,1)S(1)} %collective-permute-done.4.acts, bf16[512,512]{1,0:T(8,128)(2,1)S(1)} %constant_dynamic-slice_fusion.own_w, bf16[512,512]{1,0:T(8,128)(2,1)S(1)} %collective-permute-done.far_w, ...), custom_call_target="tpu_custom_call", output_to_operand_aliasing={{}: (4, {})} | custom-call | flops 536870912 | bytes 3145728 | tf_op jit(solution)/shard_map/partial_other/pallas_call | solution.py:107
  53.7 4.2 %all-to-all-start.1 = ((bf16[8,128,512]{2,1,0:T(8,128)(2,1)}), bf16[8,128,512]{2,1,0:T(8,128)(2,1)}, u32[]{:S(2)}, u32[]{:S(2)}) async-start(bf16[8,128,512]{2,1,0:T(8,128)(2,1)} %partial_other.1), calls=%async_computation.1 | async-start | bytes 2097152 | tf_op jit(solution)/shard_map/all_to_all | solution.py:190
  58.0 4.2 %collective-permute-start.6 = (bf16[80,512]{1,0:T(8,128)(2,1)}, bf16[80,512]{1,0:T(8,128)(2,1)S(1)}, u32[]{:S(2)}, u32[]{:S(2)}) collective-permute-start(bf16[80,512]{1,0:T(8,128)(2,1)} %copy-done.9), channel_id=1, source_target_pairs={{0,10},{2,8},{4,14},{6,12},{8,2},{10,0},{12,6},{14,4},{1,11},{3,9}... | collective-permute-start | bytes 245768 | tf_op jit(solution)/shard_map/ppermute | solution.py:164
  62.2 0.9 %collective-permute-start.7 = (bf16[80,512]{1,0:T(8,128)(2,1)}, bf16[80,512]{1,0:T(8,128)(2,1)S(1)}, u32[]{:S(2)}, u32[]{:S(2)}) collective-permute-start(bf16[80,512]{1,0:T(8,128)(2,1)} %copy-done.8), channel_id=1, source_target_pairs={{0,12},{2,14},{4,8},{6,10},{8,4},{10,6},{12,0},{14,2},{1,13},{3,15... | collective-permute-start | bytes 245768 | tf_op jit(solution)/shard_map/ppermute | solution.py:164
  63.1 2.5 %collective-permute-start.8 = (bf16[80,512]{1,0:T(8,128)(2,1)}, bf16[80,512]{1,0:T(8,128)(2,1)S(1)}, u32[]{:S(2)}, u32[]{:S(2)}) collective-permute-start(bf16[80,512]{1,0:T(8,128)(2,1)} %copy-done.7), channel_id=1, source_target_pairs={{0,14},{2,12},{4,10},{6,8},{8,6},{10,4},{12,2},{14,0},{1,15},{3,13... | collective-permute-start | bytes 245768 | tf_op jit(solution)/shard_map/ppermute | solution.py:164
  65.7 7.0 %collective-permute-done.5.rest_4_ = bf16[80,512]{1,0:T(8,128)(2,1)S(1)} collective-permute-done((bf16[80,512]{1,0:T(8,128)(2,1)}, bf16[80,512]{1,0:T(8,128)(2,1)S(1)}, u32[]{:S(2)}, u32[]{:S(2)}) %collective-permute-start.5) | collective-permute-done | bytes 81952 | tf_op jit(solution)/shard_map/ppermute | solution.py:164
  72.7 1.8 %collective-permute-done.6.rest_5_ = bf16[80,512]{1,0:T(8,128)(2,1)S(1)} collective-permute-done((bf16[80,512]{1,0:T(8,128)(2,1)}, bf16[80,512]{1,0:T(8,128)(2,1)S(1)}, u32[]{:S(2)}, u32[]{:S(2)}) %collective-permute-start.6) | collective-permute-done | bytes 81952 | tf_op jit(solution)/shard_map/ppermute | solution.py:164
  74.4 4.0 %collective-permute-done.7.rest_6_ = bf16[80,512]{1,0:T(8,128)(2,1)S(1)} collective-permute-done((bf16[80,512]{1,0:T(8,128)(2,1)}, bf16[80,512]{1,0:T(8,128)(2,1)S(1)}, u32[]{:S(2)}, u32[]{:S(2)}) %collective-permute-start.7) | collective-permute-done | bytes 81952 | tf_op jit(solution)/shard_map/ppermute | solution.py:164
  78.4 1.6 %collective-permute-done.8.rest_7_ = bf16[80,512]{1,0:T(8,128)(2,1)S(1)} collective-permute-done((bf16[80,512]{1,0:T(8,128)(2,1)}, bf16[80,512]{1,0:T(8,128)(2,1)S(1)}, u32[]{:S(2)}, u32[]{:S(2)}) %collective-permute-start.8) | collective-permute-done | bytes 81952 | tf_op jit(solution)/shard_map/ppermute | solution.py:164
  80.0 1.0 %low_rank.1.low_mine = f32[128,64]{1,0:T(8,128)S(1)} custom-call(s32[3]{0:T(128)S(1)} %pad_add_fusion.place, bf16[128,4096]{1,0:T(8,128)(2,1)S(1)} %norm_half.1.acts, bf16[80,512]{1,0:T(8,128)(2,1)S(1)} %get-tuple-element.31.rest_0_, bf16[80,512]{1,0:T(8,128)(2,1)S(1)} %collective-permute-done.1.rest_1_, bf16[80,512]{1,0:T(8,128)(2,1)S(1)} %collective-permute-done.2.rest_2_, ...), custom_call_target="tpu_custom_call" | custom-call | flops 67108864 | bytes 2097152 | tf_op jit(solution)/shard_map/low_rank/pallas_call | solution.py:107
  81.0 0.1 collective-permute-start.9
  81.1 1.2 %collective-permute-done.9.low_other = f32[128,64]{1,0:T(8,128)S(1)} collective-permute-done((f32[128,64]{1,0:T(8,128)S(1)}, f32[128,64]{1,0:T(8,128)S(1)}, u32[]{:S(2)}, u32[]{:S(2)}) %collective-permute-start.9) | collective-permute-done | bytes 32800 | tf_op jit(solution)/shard_map/ppermute | solution.py:200
  82.3 2.7 %final.1 = bf16[128,512]{1,0:T(8,128)(2,1)} custom-call(s32[3]{0:T(128)S(1)} %pad_add_fusion.place, bf16[8,128,512]{2,1,0:T(8,128)(2,1)} %all-to-all-done.1.parts, f32[128,64]{1,0:T(8,128)S(1)} %low_rank.1.low_mine, f32[128,64]{1,0:T(8,128)S(1)} %collective-permute-done.9.low_other, bf16[80,512]{1,0:T(8,128)(2,1)S(1)} %get-tuple-element.31.rest_0_, ...), custom_call_target="tpu_custom_call" | custom-call | flops 16777216 | bytes 3145728 | tf_op jit(solution)/shard_map/final/pallas_call | solution.py:107
  (27 shorter events, 0.2 us)
Async XLA Ops:
  0.0 1.2 %copy-start = (bf16[1024,512]{1,0:T(8,128)(2,1)S(1)}, bf16[1024,512]{1,0:T(8,128)(2,1)}, u32[]{:S(2)}) copy-start(bf16[1024,512]{1,0:T(8,128)(2,1)} %param.9) | copy-start | bytes 3145732
  1.3 41.1 %collective-permute-start = (bf16[512,512]{1,0:T(8,128)(2,1)S(1)}, bf16[512,512]{1,0:T(8,128)(2,1)S(1)}, u32[]{:S(2)}, u32[]{:S(2)}) collective-permute-start(bf16[512,512]{1,0:T(8,128)(2,1)S(1)} %constant_dynamic-slice_fusion.own_w), channel_id=1, source_target_pairs={{0,8},{2,10},{4,12},{6,14},{8,0},{10,2},{12,4},{14,6},{1,9},{3,11}... | collective-permute-start | bytes 1572872 | tf_op jit(solution)/shard_map/ppermute | solution.py:142
  5.4 1.6 %copy-start.1 = (bf16[128,8192]{1,0:T(8,128)(2,1)S(1)}, bf16[128,8192]{1,0:T(8,128)(2,1)}, u32[]{:S(2)}) copy-start(bf16[128,8192]{1,0:T(8,128)(2,1)} %hidden.3) | copy-start | bytes 6291460
  7.0 0.7 copy-start.3
  9.8 32.6 %all-to-all-start = ((bf16[8,64,1024]{2,1,0:T(8,128)(2,1)}), bf16[8,64,1024]{2,1,0:T(8,128)(2,1)}, u32[]{:S(2)}, u32[]{:S(2)}) async-start(bf16[8,64,1024]{2,1,0:T(8,128)(2,1)} %norm_send.1), calls=%async_computation | async-start | bytes 2097152 | tf_op jit(solution)/shard_map/all_to_all | solution.py:151
  14.5 3.4 %copy-start.5 = (bf16[128,1,512,64]{2,3,1,0:T(8,128)(2,1)S(1)}, bf16[128,1,512,64]{2,3,1,0:T(8,128)(2,1)}, u32[]{:S(2)}) copy-start(bf16[128,1,512,64]{2,3,1,0:T(8,128)(2,1)} %param.10) | copy-start | bytes 25165828
  17.9 1.2 %copy-start.6 = (bf16[128,1,4096]{2,0,1:T(8,128)(2,1)S(1)}, bf16[128,1,4096]{2,0,1:T(8,128)(2,1)}, u32[]{:S(2)}) copy-start(bf16[128,1,4096]{2,0,1:T(8,128)(2,1)} %param.11) | copy-start | bytes 3145732
  19.1 0.7 copy-start.11
  19.8 0.7 copy-start.12
  20.4 5.3 %copy-start.2 = (bf16[128,8192]{1,0:T(8,128)(2,1)S(1)}, bf16[128,8192]{1,0:T(8,128)(2,1)}, u32[]{:S(2)}) copy-start(bf16[128,8192]{1,0:T(8,128)(2,1)} %hidden.3) | copy-start | bytes 6291460
  20.4 5.3 %copy-start.4 = (bf16[8192]{0:T(1024)(128)(2,1)S(1)}, bf16[8192]{0:T(1024)(128)(2,1)}, u32[]{:S(2)}) copy-start(bf16[8192]{0:T(1024)(128)(2,1)} %gain.3) | copy-start | bytes 49156
  22.1 20.3 %copy-start.7 = (bf16[80,512]{1,0:T(8,128)(2,1)}, bf16[80,512]{1,0:T(8,128)(2,1)S(1)}, u32[]{:S(2)}) copy-start(bf16[80,512]{1,0:T(8,128)(2,1)S(1)} %get-tuple-element.38) | copy-start | bytes 245764
  22.1 20.3 %copy-start.8 = (bf16[80,512]{1,0:T(8,128)(2,1)}, bf16[80,512]{1,0:T(8,128)(2,1)S(1)}, u32[]{:S(2)}) copy-start(bf16[80,512]{1,0:T(8,128)(2,1)S(1)} %get-tuple-element.37) | copy-start | bytes 245764
  22.1 20.3 %copy-start.9 = (bf16[80,512]{1,0:T(8,128)(2,1)}, bf16[80,512]{1,0:T(8,128)(2,1)S(1)}, u32[]{:S(2)}) copy-start(bf16[80,512]{1,0:T(8,128)(2,1)S(1)} %get-tuple-element.36) | copy-start | bytes 245764
  22.1 20.3 %copy-start.10 = (bf16[80,512]{1,0:T(8,128)(2,1)}, bf16[80,512]{1,0:T(8,128)(2,1)S(1)}, u32[]{:S(2)}) copy-start(bf16[80,512]{1,0:T(8,128)(2,1)S(1)} %get-tuple-element.35) | copy-start | bytes 245764
  22.1 5.1 %collective-permute-start.1 = (bf16[80,512]{1,0:T(8,128)(2,1)S(1)}, bf16[80,512]{1,0:T(8,128)(2,1)S(1)}, u32[]{:S(2)}, u32[]{:S(2)}) collective-permute-start(bf16[80,512]{1,0:T(8,128)(2,1)S(1)} %get-tuple-element.25), channel_id=1, source_target_pairs={{0,2},{2,0},{4,6},{6,4},{8,10},{10,8},{12,14},{14,12},{1,3},{3,1},... | collective-permute-start | bytes 245768 | tf_op jit(solution)/shard_map/ppermute | solution.py:164
  24.2 16.3 %collective-permute-start.2 = (bf16[80,512]{1,0:T(8,128)(2,1)S(1)}, bf16[80,512]{1,0:T(8,128)(2,1)S(1)}, u32[]{:S(2)}, u32[]{:S(2)}) collective-permute-start(bf16[80,512]{1,0:T(8,128)(2,1)S(1)} %get-tuple-element.26), channel_id=1, source_target_pairs={{0,4},{2,6},{4,0},{6,2},{8,12},{10,14},{12,8},{14,10},{1,5},{3,7},... | collective-permute-start | bytes 245768 | tf_op jit(solution)/shard_map/ppermute | solution.py:164
  25.6 16.7 %collective-permute-start.3 = (bf16[80,512]{1,0:T(8,128)(2,1)S(1)}, bf16[80,512]{1,0:T(8,128)(2,1)S(1)}, u32[]{:S(2)}, u32[]{:S(2)}) collective-permute-start(bf16[80,512]{1,0:T(8,128)(2,1)S(1)} %get-tuple-element.27), channel_id=1, source_target_pairs={{0,6},{2,4},{4,2},{6,0},{8,14},{10,12},{12,10},{14,8},{1,7},{3,5},... | collective-permute-start | bytes 245768 | tf_op jit(solution)/shard_map/ppermute | solution.py:164
  42.4 6.8 %collective-permute-start.4 = (bf16[8,64,1024]{2,1,0:T(8,128)(2,1)}, bf16[8,64,1024]{2,1,0:T(8,128)(2,1)S(1)}, u32[]{:S(2)}, u32[]{:S(2)}) collective-permute-start(bf16[8,64,1024]{2,1,0:T(8,128)(2,1)} %all-to-all-done.acts), channel_id=1, source_target_pairs={{0,1},{1,0},{2,3},{3,2},{4,5},{5,4},{6,7},{7,6},{8,9},{9,8},{10,11... | collective-permute-start | bytes 3145736 | tf_op jit(solution)/shard_map/ppermute | solution.py:176
  53.7 28.6 %all-to-all-start.1 = ((bf16[8,128,512]{2,1,0:T(8,128)(2,1)}), bf16[8,128,512]{2,1,0:T(8,128)(2,1)}, u32[]{:S(2)}, u32[]{:S(2)}) async-start(bf16[8,128,512]{2,1,0:T(8,128)(2,1)} %partial_other.1), calls=%async_computation.1 | async-start | bytes 2097152 | tf_op jit(solution)/shard_map/all_to_all | solution.py:190
  57.9 14.7 %collective-permute-start.5 = (bf16[80,512]{1,0:T(8,128)(2,1)}, bf16[80,512]{1,0:T(8,128)(2,1)S(1)}, u32[]{:S(2)}, u32[]{:S(2)}) collective-permute-start(bf16[80,512]{1,0:T(8,128)(2,1)} %copy-done.10), channel_id=1, source_target_pairs={{0,8},{2,10},{4,12},{6,14},{8,0},{10,2},{12,4},{14,6},{1,9},{3,11}... | collective-permute-start | bytes 245768 | tf_op jit(solution)/shard_map/ppermute | solution.py:164
  58.0 16.4 %collective-permute-start.6 = (bf16[80,512]{1,0:T(8,128)(2,1)}, bf16[80,512]{1,0:T(8,128)(2,1)S(1)}, u32[]{:S(2)}, u32[]{:S(2)}) collective-permute-start(bf16[80,512]{1,0:T(8,128)(2,1)} %copy-done.9), channel_id=1, source_target_pairs={{0,10},{2,8},{4,14},{6,12},{8,2},{10,0},{12,6},{14,4},{1,11},{3,9}... | collective-permute-start | bytes 245768 | tf_op jit(solution)/shard_map/ppermute | solution.py:164
  62.2 16.2 %collective-permute-start.7 = (bf16[80,512]{1,0:T(8,128)(2,1)}, bf16[80,512]{1,0:T(8,128)(2,1)S(1)}, u32[]{:S(2)}, u32[]{:S(2)}) collective-permute-start(bf16[80,512]{1,0:T(8,128)(2,1)} %copy-done.8), channel_id=1, source_target_pairs={{0,12},{2,14},{4,8},{6,10},{8,4},{10,6},{12,0},{14,2},{1,13},{3,15... | collective-permute-start | bytes 245768 | tf_op jit(solution)/shard_map/ppermute | solution.py:164
  63.1 16.9 %collective-permute-start.8 = (bf16[80,512]{1,0:T(8,128)(2,1)}, bf16[80,512]{1,0:T(8,128)(2,1)S(1)}, u32[]{:S(2)}, u32[]{:S(2)}) collective-permute-start(bf16[80,512]{1,0:T(8,128)(2,1)} %copy-done.7), channel_id=1, source_target_pairs={{0,14},{2,12},{4,10},{6,8},{8,6},{10,4},{12,2},{14,0},{1,15},{3,13... | collective-permute-start | bytes 245768 | tf_op jit(solution)/shard_map/ppermute | solution.py:164
  81.0 1.3 %collective-permute-start.9 = (f32[128,64]{1,0:T(8,128)S(1)}, f32[128,64]{1,0:T(8,128)S(1)}, u32[]{:S(2)}, u32[]{:S(2)}) collective-permute-start(f32[128,64]{1,0:T(8,128)S(1)} %low_rank.1.low_mine), channel_id=1, source_target_pairs={{0,1},{1,0},{2,3},{3,2},{4,5},{5,4},{6,7},{7,6},{8,9},{9,8},{10,11... | collective-permute-start | bytes 98312 | tf_op jit(solution)/shard_map/ppermute | solution.py:200

commit v3 on v2

v3 whole, which is shorter than its diff:
```python
import functools

import jax
import jax.numpy as jnp
from jax import lax
from jax.experimental import pallas as pl
from jax.experimental.pallas import tpu as pltpu
from jax.sharding import PartitionSpec as P

SEGMENT_TOKENS = 128
EPS = 1e-05
VMEM_LIMIT = 16 * 1024 * 1024
PAD_ROWS = 16
LONG = 1 << 36
PEERS = ((1, 0), (0, 1), (1, 1))


def params():
    return pltpu.CompilerParams(vmem_limit_bytes=VMEM_LIMIT)


def gather_kernel(place, seg, slot_of, down, up, out, sem):
    peers = out.shape[0]
    rank, feats = down.shape[1:]
    up_rows = up.shape[1] // feats
    copies = []
    row = lax.broadcasted_iota(jnp.int32, (PAD_ROWS, up.shape[0]), 0)
    col = lax.broadcasted_iota(jnp.int32, (PAD_ROWS, up.shape[0]), 1)
    hot = jnp.zeros((PAD_ROWS, up.shape[0]), jnp.float32)
    for k in range(peers):
        slot = slot_of[seg[k]]
        copy = pltpu.make_async_copy(down.at[slot], out.at[k, pl.ds(0, rank)], sem.at[k])
        copy.start()
        copies.append(copy)
        hot = jnp.where((row == k) & (col == slot), 1.0, hot)
    picked = jnp.dot(hot.astype(jnp.bfloat16), up[...], preferred_element_type=jnp.float32)
    for k in range(peers):
        rows = [picked[k : k + 1, r * feats : (r + 1) * feats] for r in range(up_rows)]
        rows.append(jnp.zeros((PAD_ROWS - up_rows, feats), jnp.float32))
        out[k, pl.ds(rank, PAD_ROWS), :] = jnp.concatenate(rows, axis=0).astype(jnp.bfloat16)
    for copy in copies:
        copy.wait()


def wanted(place, peer, step, row_count, chunk):
    shard = (place[1] * 2 + peer % 2) ^ (2 * step)
    return pl.multiple_of(shard * row_count + (peer // 2) * chunk, chunk)


def normed_piece(rows, gain, inv, at):
    return (rows[:, at].astype(jnp.float32) * inv * gain[at].astype(jnp.float32)[None, :]).astype(jnp.bfloat16)


def inv_rms(rows):
    values = rows[...].astype(jnp.float32)
    return lax.rsqrt(jnp.mean(values * values, axis=1, keepdims=True) + EPS)


def norm_send_kernel(steps, row_count, chunk, place, hidden, gain_hbm, out, held, gain, sem):
    rows = held.shape[0]
    cut = rows // 4
    first = place[2] * rows
    copies = [pltpu.make_async_copy(gain_hbm, gain, sem.at[4])]
    for i in range(4):
        at = pl.ds(pl.multiple_of(first + i * cut, cut), cut)
        copies.append(pltpu.make_async_copy(hidden.at[at], held.at[pl.ds(i * cut, cut)], sem.at[i]))
    for copy in copies:
        copy.start()
    copies[0].wait()
    for i in range(4):
        copies[1 + i].wait()
        part = held.at[pl.ds(i * cut, cut)]
        inv = inv_rms(part)
        for peer in range(4):
            for step in range(steps):
                at = pl.ds(wanted(place, peer, step, row_count, chunk), chunk)
                out[peer, pl.ds(i * cut, cut), step * chunk : (step + 1) * chunk] = normed_piece(part, gain, inv, at)


def norm_half_kernel(place, hidden, gain, out, held, sem):
    half = hidden.shape[1] // 2
    at = pl.ds(pl.multiple_of(place[2] * half, half), half)
    held[...] = normed_piece(hidden, gain, inv_rms(hidden), at)
    copy = pltpu.make_async_copy(held, out, sem)
    copy.start()
    copy.wait()


def in_order(place, mine, other):
    me = place[3] * 2 + place[0] % 2
    quarters = [me ^ 1, me ^ 2, me ^ 3, me]
    return jnp.concatenate([mine[q] for q in quarters] + [other[q] for q in quarters], axis=0)


def early_kernel(place, mine, other, *rest):
    weights, out = rest[:-1], rest[-1]
    x = in_order(place, mine, other)
    total = jnp.zeros(out.shape, jnp.float32)
    first = 0
    for w in weights:
        total += jnp.dot(x[:, first : first + w.shape[0]], w[...], preferred_element_type=jnp.float32)
        first += w.shape[0]
    out[...] = total


def late_kernel(place, mine, other, weight, early, out0, out1, out2, own):
    rows = mine.shape[1]
    x = in_order(place, mine, other)
    total = early[...] + jnp.dot(x, weight[...], preferred_element_type=jnp.float32)
    half = place[2]
    for part in range(2):
        at = pl.ds(pl.multiple_of((half if part == 0 else 1 - half) * rows, rows), rows)
        for k, out in enumerate((out0, out1, out2, own)):
            first = (4 * part + k) * rows
            out[at, :] = total[first : first + rows].astype(out.dtype)


def rank_kernel(place, acts, pieces, out):
    rank = out.shape[1]
    feats = pieces.shape[2]
    total = jnp.zeros(out.shape, jnp.float32)
    for k in range(pieces.shape[0]):
        x = acts[:, k * feats : (k + 1) * feats]
        total += lax.dot_general(x, pieces[k, :rank, :], (((1,), (1,)), ((), ())), preferred_element_type=jnp.float32)
    out[...] = total


def final_kernel(up_rows, place, own, far0, far1, far2, low_mine, low_other, pieces, out):
    rank = low_mine.shape[1]
    up = [pieces[k, rank : rank + PAD_ROWS, :].astype(jnp.float32)[:up_rows] for k in range(pieces.shape[0])]
    low = (low_mine[...] + low_other[...]).astype(jnp.bfloat16)
    up = jnp.concatenate(up, axis=0).astype(jnp.bfloat16)
    total = jnp.dot(low, up, preferred_element_type=jnp.float32) + own[...]
    for part in (far0, far1, far2):
        total += part[...].astype(jnp.float32)
    out[...] = total.astype(jnp.bfloat16)


def whole(shape):
    return pl.BlockSpec(shape, lambda *_: (0,) * len(shape))


def call(kernel, prefetch, args, in_specs, outs, out_specs, grid=(1,), scratch=(), alias=None, name=None, flops=0, nbytes=0):
    return pl.pallas_call(
        kernel,
        grid_spec=pltpu.PrefetchScalarGridSpec(
            num_scalar_prefetch=len(prefetch),
            grid=grid,
            in_specs=in_specs,
            out_specs=out_specs,
            scratch_shapes=scratch,
        ),
        out_shape=outs,
        compiler_params=params(),
        input_output_aliases=alias or {},
        cost_estimate=pl.CostEstimate(flops=flops, bytes_accessed=nbytes, transcendentals=0),
        name=name,
    )(*prefetch, *args)


def square_device(hidden, norm_gain, kv_weight, down_panels, up_panels, seg_adapter, slot_of):
    tokens, features = hidden.shape
    groups, peers = lax.axis_size("groups"), lax.axis_size("tensor")
    g, t, h = (lax.axis_index(axis) for axis in ("groups", "tensor", "pool"))
    steps = peers // 2
    row_count, cols = kv_weight.shape
    chunk = row_count // groups
    rows = tokens // 2
    span = steps * chunk
    feats, rank = down_panels.shape[2:]
    bf16, f32 = jnp.bfloat16, jnp.float32
    place = jnp.stack([t, t // 2, h, g]).astype(jnp.int32)
    up_rows = up_panels.shape[2] // feats
    hbm = pl.BlockSpec(memory_space=pltpu.HBM)
    cores = [(0, 1), (1, 0)]

    def to_peer(x, flip_x, flip_g):
        pairs = [(i, i ^ flip_x ^ (flip_g * peers)) for i in range(groups * peers)]
        return lax.ppermute(x, ("groups", "tensor"), pairs)

    own_w = lax.dynamic_slice_in_dim(kv_weight, g * chunk, chunk, 0)


    def along_z(x, step):
        return lax.ppermute(x, "tensor", [(i, i ^ (2 * step)) for i in range(peers)])

    second = along_z(own_w, 2)
    first = along_z(own_w, 1)
    squares = [[a * peers + z * 2 + x for a in range(groups) for x in range(2)] for z in range(steps)]
    send = call(
        functools.partial(norm_send_kernel, steps, row_count, chunk), [place], [hidden, norm_gain], [hbm, hbm],
        jax.ShapeDtypeStruct((4, rows, span), bf16), whole((4, rows, span)),
        scratch=[pltpu.VMEM((rows, features), bf16), pltpu.VMEM((features,), bf16), pltpu.SemaphoreType.DMA((5,))],
        name="norm_send", flops=6 * rows * features, nbytes=4 * rows * features,
    )
    send, later = lax.optimization_barrier((send, place))
    mine = lax.all_to_all(
        send, ("groups", "tensor"), split_axis=0, concat_axis=0, tiled=True, axis_index_groups=squares
    )

    piece_shape = (peers, rank + PAD_ROWS, feats)
    pieces = call(
        gather_kernel, [later, seg_adapter, slot_of],
        [down_panels[:, 0].transpose(0, 2, 1), up_panels[:, 0]],
        [hbm, whole((up_panels.shape[0], up_panels.shape[2]))],
        jax.ShapeDtypeStruct(piece_shape, bf16), whole(piece_shape),
        scratch=[pltpu.SemaphoreType.DMA((peers,))], name="pick_panels", flops=LONG, nbytes=3 << 20,
    )
    mine, pieces, later, second = lax.optimization_barrier((mine, pieces, later, second))
    third = along_z(second, 1)
    acts = call(
        norm_half_kernel, [later], [hidden, norm_gain], [whole((tokens, features)), whole((features,))],
        jax.ShapeDtypeStruct((tokens, features // 2), bf16), hbm,
        scratch=[pltpu.VMEM((tokens, features // 2), bf16), pltpu.SemaphoreType.DMA], name="norm_half", flops=LONG, nbytes=4 * tokens * features,
    )
    others = [lax.ppermute(mine, "pool", cores)]
    weight = whole((chunk, cols))
    early = call(
        early_kernel, [place], [mine, *others, own_w, first, second],
        [pl.BlockSpec((4, rows, span - chunk), lambda i, p: (0, 0, 0))] * 2 + [weight] * 3,
        jax.ShapeDtypeStruct((4 * tokens, cols), f32), whole((4 * tokens, cols)),
        name="early_rows", flops=24 * tokens * chunk * cols, nbytes=4 << 20,
    )
    acts, early, third = lax.optimization_barrier((acts, early, third))
    late = call(
        late_kernel, [place], [mine, *others, third, early],
        [pl.BlockSpec((4, rows, chunk), lambda i, p: (0, 0, steps - 1))] * 2 + [weight, whole(early.shape)],
        [jax.ShapeDtypeStruct((tokens, cols), bf16)] * 3 + [jax.ShapeDtypeStruct((tokens, cols), f32)],
        [whole((tokens, cols))] * 4,
        name="late_rows", flops=8 * tokens * chunk * cols, nbytes=4 << 20,
    )
    parts = [to_peer(x, *peer) for x, peer in zip(late[:3], PEERS)]

    pieces = lax.all_to_all(pieces, "tensor", split_axis=0, concat_axis=0, tiled=True)
    low_mine = call(
        rank_kernel, [place], [acts, pieces], [whole(acts.shape), whole(piece_shape)],
        jax.ShapeDtypeStruct((tokens, rank), f32), whole((tokens, rank)),
        name="low_rank", flops=2 * tokens * rank * features // 2, nbytes=2 << 20,
    )
    low_other = lax.ppermute(low_mine, "pool", cores)
    return call(
        functools.partial(final_kernel, up_rows), [place],
        [late[3], *parts, low_mine, low_other, pieces],
        [whole((tokens, cols))] * 4 + [whole((tokens, rank))] * 2 + [whole(piece_shape)],
        jax.ShapeDtypeStruct((tokens, cols), bf16), whole((tokens, cols)),
        name="final", flops=4 * tokens * rank * cols, nbytes=3 << 20,
    )


def gathered_device(hidden, norm_gain, kv_weight, down_panels, up_panels, seg_adapter, slot_of):
    tok_rows = hidden.shape[0]
    half_width = hidden.shape[1] // 2
    peer_count = lax.axis_size("tensor")
    my_half = lax.axis_index("pool")
    seg_local = tok_rows // SEGMENT_TOKENS
    values = hidden.astype(jnp.float32)
    inv_rms = lax.rsqrt(jnp.mean(values * values, axis=1, keepdims=True) + EPS)
    normed = (values * inv_rms * norm_gain.astype(jnp.float32)).astype(jnp.bfloat16)
    weight = lax.all_gather(kv_weight, "tensor", axis=0, tiled=True)
    base = jnp.dot(normed, weight, preferred_element_type=jnp.float32)
    wanted = slot_of[seg_adapter].reshape(peer_count, seg_local).T
    down_store, up_store = down_panels[:, 0], up_panels[:, 0]
    rank_width = down_store.shape[2]
    normed_half = lax.dynamic_slice_in_dim(normed, my_half * half_width, half_width, 1)
    got_down = lax.all_to_all(down_store[wanted], "tensor", split_axis=1, concat_axis=1, tiled=True)
    up_mats = lax.all_to_all(up_store[wanted], "tensor", split_axis=1, concat_axis=1, tiled=True)
    low_rank = jnp.einsum(
        "sti,sir->str",
        normed_half.reshape(seg_local, SEGMENT_TOKENS, half_width),
        got_down.reshape(seg_local, half_width, rank_width),
        preferred_element_type=jnp.float32,
    )
    low_rank = lax.psum(low_rank, "pool").astype(jnp.bfloat16)
    update = jnp.einsum(
        "str,srh->sth",
        low_rank,
        up_mats.reshape(seg_local, rank_width, -1),
        preferred_element_type=jnp.float32,
    )
    return (base + update.reshape(tok_rows, -1)).astype(jnp.bfloat16)


def per_device(hidden, norm_gain, kv_weight, down_panels, up_panels, seg_adapter, slot_of):
    peers, groups = lax.axis_size("tensor"), lax.axis_size("groups")
    feats = down_panels.shape[2]
    fits = (
        hidden.shape[0] == SEGMENT_TOKENS
        and lax.axis_size("pool") == 2
        and peers == 8
        and groups == 2
        and kv_weight.shape[0] % (128 * groups) == 0
        and feats == kv_weight.shape[1]
        and up_panels.shape[2] % (8 * feats) == 0
        and up_panels.shape[2] // feats <= PAD_ROWS
    )
    body = square_device if fits else gathered_device
    return body(hidden, norm_gain, kv_weight, down_panels, up_panels, seg_adapter, slot_of)


def solution(mesh):
    placed = (
        P(("groups", "tensor"), None),
        P(),
        P("tensor", "pool"),
        P("groups", "pool", "tensor", None),
        P("groups", "pool", "tensor"),
        P("groups"),
        P("groups"),
    )
    return jax.shard_map(
        per_device,
        mesh=mesh,
        in_specs=placed,
        out_specs=P(("groups", "tensor"), "pool"),
        check_vma=False,
    )
```

time: 85.6 us -> 63.5 us (0.74)
  waiting for transfers between devices: 30.7 us -> 15.5 us
  Pallas kernels: 20 us -> 13.8 us
  starting transfers between devices: 24.6 us -> 19.2 us
  local copies, waits for them, and re-layouts: 9.51 us -> 14.1 us
    ppermute x10 -> x8, waiting for transfers between devices: 30.7 us -> 15.5 us  [the longest x3 11.7 us: along_z(): return lax.ppermute(x, 'tensor', [(i, i ^ 2 * step) for i in range(peers)])]
    pallas_call x7, Pallas kernels: 20 us -> 13.8 us  [call(): pl.pallas_call(kernel, grid_spec=pltpu.PrefetchScalarGridSpec(num_scalar_...]
    ppermute x10 -> x8, starting transfers between devices: 15.6 us -> 9.77 us  [the longest x3 6.2 us: along_z(): return lax.ppermute(x, 'tensor', [(i, i ^ 2 * step) for i in range(peers)])]
    unnamed x26 -> x24, local copies, waits for them, and re-layouts: 9.47 us -> 14.1 us
  transfers between devices with their start and end apart: 12 -> 10, of which waited for: 7 -> 4; matrix products, arithmetic and copies ran while one was open for 0% -> 0% of each run, Pallas kernels for 15% -> 20%
where the time goes in v3:
time: 63.5 us; the launch traced here: 62.8 us
  starting transfers between devices  19.2 us (30%)
  waiting for transfers between devices  15.5 us (24%)
  local copies, waits for them, and re-layouts  14.1 us (22%)
  Pallas kernels  13.8 us (22%)
    unnamed x24, local copies, waits for them, and re-layouts  14.1 us
    pallas_call x7, Pallas kernels, call(): pl.pallas_call(kernel, grid_spec=pltpu.PrefetchScalarGridSpec(num_scalar_...  13.8 us
    ppermute x3, waiting for transfers between devices, along_z(): return lax.ppermute(x, 'tensor', [(i, i ^ 2 * step) for i in range(peers)])  11.7 us
    ppermute x3, starting transfers between devices, along_z(): return lax.ppermute(x, 'tensor', [(i, i ^ 2 * step) for i in range(peers)])  6.2 us
    all_to_all x1, starting transfers between devices, square_device(): lax.all_to_all(pieces, 'tensor', split_axis=0, concat_axis=0, tiled=True)  5.69 us
    all_to_all x1, starting transfers between devices, square_device(): lax.all_to_all(send, ('groups', 'tensor'), split_axis=0, concat_axis=0, t...  3.73 us
    ppermute x3, starting transfers between devices, to_peer(): return lax.ppermute(x, ('groups', 'tensor'), pairs)  3.49 us
    ppermute x3, waiting for transfers between devices, to_peer(): return lax.ppermute(x, ('groups', 'tensor'), pairs)  2.53 us
  transfers between devices with their start and end apart: 10, of which 4 were waited for; matrix products, arithmetic and copies ran while one was open for 0% of the time, Pallas kernels for 20%

profile of v3, /device:TPU:0, one launch (start us, length us, event | category | flops | bytes accessed | tf_op | source)
XLA Modules:
  0.0 62.8 jit_solution(2543438885782530535)
XLA Ops:
  0.0 1.2 %copy-done = bf16[1024,512]{1,0:T(8,128)(2,1)S(1)} copy-done((bf16[1024,512]{1,0:T(8,128)(2,1)S(1)}, bf16[1024,512]{1,0:T(8,128)(2,1)}, u32[]{:S(2)}) %copy-start) | copy-done | bytes 1048600
  1.3 4.1 %collective-permute-start = (bf16[512,512]{1,0:T(8,128)(2,1)S(1)}, bf16[512,512]{1,0:T(8,128)(2,1)}, u32[]{:S(2)}, u32[]{:S(2)}) collective-permute-start(bf16[512,512]{1,0:T(8,128)(2,1)S(1)} %constant_dynamic-slice_fusion.rest_0_), channel_id=1, source_target_pairs={{0,8},{2,10},{4,12},{6,14},{8,0},{10,2},{12,4},{14,6},{1,9},{3,11}... | collective-permute-start | bytes 1572872 | tf_op jit(solution)/shard_map/ppermute | solution.py:185
  5.4 1.6 %collective-permute-start.2 = (bf16[512,512]{1,0:T(8,128)(2,1)S(1)}, bf16[512,512]{1,0:T(8,128)(2,1)}, u32[]{:S(2)}, u32[]{:S(2)}) collective-permute-start(bf16[512,512]{1,0:T(8,128)(2,1)S(1)} %constant_dynamic-slice_fusion.rest_0_), channel_id=1, source_target_pairs={{0,4},{2,6},{4,0},{6,2},{8,12},{10,14},{12,8},{14,10},{1,5},{3,7},... | collective-permute-start | bytes 1572872 | tf_op jit(solution)/shard_map/ppermute | solution.py:185
  6.9 0.1 pad_add_fusion.place
  7.0 1.6 %copy-done.1 = bf16[128,8192]{1,0:T(8,128)(2,1)S(1)} copy-done((bf16[128,8192]{1,0:T(8,128)(2,1)S(1)}, bf16[128,8192]{1,0:T(8,128)(2,1)}, u32[]{:S(2)}) %copy-start.1) | copy-done | bytes 2097176
  8.6 0.7 %copy-done.6 = bf16[8192]{0:T(1024)(128)(2,1)S(1)} copy-done((bf16[8192]{0:T(1024)(128)(2,1)S(1)}, bf16[8192]{0:T(1024)(128)(2,1)}, u32[]{:S(2)}) %copy-start.6) | copy-done | bytes 16408
  9.3 2.5 %norm_send.1 = bf16[4,64,2048]{2,1,0:T(8,128)(2,1)} custom-call(s32[4]{0:T(128)S(1)} %pad_add_fusion.place, bf16[128,8192]{1,0:T(8,128)(2,1)S(1)} %copy-done.1, bf16[8192]{0:T(1024)(128)(2,1)S(1)} %copy-done.6), custom_call_target="tpu_custom_call" | custom-call | flops 3145728 | bytes 2097152 | tf_op jit(solution)/shard_map/norm_send/pallas_call | solution.py:144
  11.8 3.7 %all-to-all-start = ((bf16[4,64,2048]{2,1,0:T(8,128)(2,1)}), bf16[4,64,2048]{2,1,0:T(8,128)(2,1)S(1)}, u32[]{:S(2)}, u32[]{:S(2)}) async-start(bf16[4,64,2048]{2,1,0:T(8,128)(2,1)} %norm_send.1), calls=%async_computation | async-start | bytes 2097152 | tf_op jit(solution)/shard_map/all_to_all | solution.py:197
  15.5 3.4 %copy-done.8 = bf16[128,1,512,64]{2,3,1,0:T(8,128)(2,1)S(1)} copy-done((bf16[128,1,512,64]{2,3,1,0:T(8,128)(2,1)S(1)}, bf16[128,1,512,64]{2,3,1,0:T(8,128)(2,1)}, u32[]{:S(2)}) %copy-start.8) | copy-done | bytes 8388632
  18.9 1.2 %copy-done.9 = bf16[128,1,4096]{2,0,1:T(8,128)(2,1)S(1)} copy-done((bf16[128,1,4096]{2,0,1:T(8,128)(2,1)S(1)}, bf16[128,1,4096]{2,0,1:T(8,128)(2,1)}, u32[]{:S(2)}) %copy-start.9) | copy-done | bytes 1048600
  20.1 0.7 %copy-done.10 = s32[8]{0:T(128)S(1)} copy-done((s32[8]{0:T(128)S(1)}, s32[8]{0:T(128)}, u32[]{:S(2)}) %copy-start.10) | copy-done | bytes 56
  20.8 0.7 %copy-done.11 = s32[128]{0:T(128)S(1)} copy-done((s32[128]{0:T(128)S(1)}, s32[128]{0:T(128)}, u32[]{:S(2)}) %copy-start.11) | copy-done | bytes 536
  21.5 1.6 %pick_panels.1 = bf16[8,80,512]{2,1,0:T(8,128)(2,1)S(1)} custom-call(s32[4]{0:T(128)S(1)} %pad_add_fusion.place, s32[8]{0:T(128)S(1)} %copy-done.10, s32[128]{0:T(128)S(1)} %copy-done.11, bf16[128,64,512]{2,1,0:T(8,128)(2,1)S(1)} %bitcast.8, bf16[128,4096]{1,0:T(8,128)(2,1)S(1)} %bitcast.9), custom_call_target="tpu_custom_call" | custom-call | flops 68719476736 | bytes 3145728 | tf_op jit(solution)/shard_map/pick_panels/pallas_call | solution.py:144
  23.1 0.8 %copy-done.5 = bf16[8,80,512]{2,1,0:T(8,128)(2,1)} copy-done((bf16[8,80,512]{2,1,0:T(8,128)(2,1)}, bf16[8,80,512]{2,1,0:T(8,128)(2,1)S(1)}, u32[]{:S(2)}) %copy-start.5) | copy-done | bytes 655384
  23.9 4.8 %collective-permute-done.rest_2_ = bf16[512,512]{1,0:T(8,128)(2,1)} collective-permute-done((bf16[512,512]{1,0:T(8,128)(2,1)S(1)}, bf16[512,512]{1,0:T(8,128)(2,1)}, u32[]{:S(2)}, u32[]{:S(2)}) %collective-permute-start) | collective-permute-done | bytes 524320 | tf_op jit(solution)/shard_map/ppermute | solution.py:185
  28.7 0.5 collective-permute-start.3
  29.3 5.7 %all-to-all-start.1 = ((bf16[8,80,512]{2,1,0:T(8,128)(2,1)}), bf16[8,80,512]{2,1,0:T(8,128)(2,1)S(1)}, u32[]{:S(2)}, u32[]{:S(2)}) async-start(bf16[8,80,512]{2,1,0:T(8,128)(2,1)} %copy-done.5), calls=%async_computation.1 | async-start | bytes 1310720 | tf_op jit(solution)/shard_map/all_to_all | solution.py:234
  35.0 0.0 copy-start.2
  35.0 1.6 %copy-done.2 = bf16[128,8192]{1,0:T(8,128)(2,1)S(1)} copy-done((bf16[128,8192]{1,0:T(8,128)(2,1)S(1)}, bf16[128,8192]{1,0:T(8,128)(2,1)}, u32[]{:S(2)}) %copy-start.2) | copy-done | bytes 2097176
  36.6 1.6 %norm_half.1.acts = bf16[128,4096]{1,0:T(8,128)(2,1)S(1)} custom-call(s32[4]{0:T(128)S(1)} %pad_add_fusion.place, bf16[128,8192]{1,0:T(8,128)(2,1)S(1)} %copy-done.2, bf16[8192]{0:T(1024)(128)(2,1)S(1)} %copy-done.7), custom_call_target="tpu_custom_call" | custom-call | flops 68719476736 | bytes 4194304 | tf_op jit(solution)/shard_map/norm_half/pallas_call | solution.py:144
  38.2 1.0 %copy-done.3 = bf16[128,4096]{1,0:T(8,128)(2,1)} copy-done((bf16[128,4096]{1,0:T(8,128)(2,1)}, bf16[128,4096]{1,0:T(8,128)(2,1)S(1)}, u32[]{:S(2)}) %copy-start.3) | copy-done | bytes 1048600
  39.1 3.0 %early_rows.1.early = f32[512,512]{1,0:T(8,128)S(1)} custom-call(s32[4]{0:T(128)S(1)} %pad_add_fusion.place, bf16[4,64,2048]{2,1,0:T(8,128)(2,1)S(1)} %all-to-all-done.mine, bf16[4,64,2048]{2,1,0:T(8,128)(2,1)} %collective-permute-done.1.other, bf16[512,512]{1,0:T(8,128)(2,1)S(1)} %constant_dynamic-slice_fusion.rest_0_, ...), custom_call_target="tpu_custom_call" | custom-call | flops 805306368 | bytes 4194304 | tf_op jit(solution)/shard_map/early_rows/pallas_call | solution.py:144
  42.1 6.9 %collective-permute-done.3.weight = bf16[512,512]{1,0:T(8,128)(2,1)} collective-permute-done((bf16[512,512]{1,0:T(8,128)(2,1)}, bf16[512,512]{1,0:T(8,128)(2,1)}, u32[]{:S(2)}, u32[]{:S(2)}) %collective-permute-start.3) | collective-permute-done | bytes 524320 | tf_op jit(solution)/shard_map/ppermute | solution.py:185
  49.0 2.8 %late_rows.1 = (bf16[128,512]{1,0:T(8,128)(2,1)}, bf16[128,512]{1,0:T(8,128)(2,1)}, bf16[128,512]{1,0:T(8,128)(2,1)}, f32[128,512]{1,0:T(8,128)S(1)}) custom-call(s32[4]{0:T(128)S(1)} %pad_add_fusion.place, bf16[4,64,2048]{2,1,0:T(8,128)(2,1)S(1)} %all-to-all-done.mine, bf16[4,64,2048]{2,1,0:T(8,128)(2,1)} %collective-permute-done.1.other, ...), custom_call_target="tpu_custom_call" | custom-call | flops 268435456 | bytes 4194304 | tf_op jit(solution)/shard_map/late_rows/pallas_call | solution.py:144
  51.9 1.6 %collective-permute-start.5 = (bf16[128,512]{1,0:T(8,128)(2,1)}, bf16[128,512]{1,0:T(8,128)(2,1)S(1)}, u32[]{:S(2)}, u32[]{:S(2)}) collective-permute-start(bf16[128,512]{1,0:T(8,128)(2,1)} %get-tuple-element.27), channel_id=1, source_target_pairs={{0,16},{2,18},{4,20},{6,22},{8,24},{10,26},{12,28},{14,30},{16,0},... | collective-permute-start | bytes 393224 | tf_op jit(solution)/shard_map/ppermute | solution.py:179
  53.4 1.9 %collective-permute-start.6 = (bf16[128,512]{1,0:T(8,128)(2,1)}, bf16[128,512]{1,0:T(8,128)(2,1)S(1)}, u32[]{:S(2)}, u32[]{:S(2)}) collective-permute-start(bf16[128,512]{1,0:T(8,128)(2,1)} %get-tuple-element.28), channel_id=1, source_target_pairs={{0,18},{2,16},{4,22},{6,20},{8,26},{10,24},{12,30},{14,28},{16,2},... | collective-permute-start | bytes 393224 | tf_op jit(solution)/shard_map/ppermute | solution.py:179
  55.3 1.2 %copy-done.4 = bf16[128,4096]{1,0:T(8,128)(2,1)S(1)} copy-done((bf16[128,4096]{1,0:T(8,128)(2,1)S(1)}, bf16[128,4096]{1,0:T(8,128)(2,1)}, u32[]{:S(2)}) %copy-start.4) | copy-done | bytes 1048600
  56.6 0.9 %low_rank.1.low_mine = f32[128,64]{1,0:T(8,128)S(1)} custom-call(s32[4]{0:T(128)S(1)} %pad_add_fusion.place, bf16[128,4096]{1,0:T(8,128)(2,1)S(1)} %copy-done.4, bf16[8,80,512]{2,1,0:T(8,128)(2,1)S(1)} %all-to-all-done.1.pieces), custom_call_target="tpu_custom_call" | custom-call | flops 67108864 | bytes 2097152 | tf_op jit(solution)/shard_map/low_rank/pallas_call | solution.py:144
  57.5 0.1 collective-permute-start.7
  57.6 1.2 %collective-permute-done.7.low_other = f32[128,64]{1,0:T(8,128)S(1)} collective-permute-done((f32[128,64]{1,0:T(8,128)S(1)}, f32[128,64]{1,0:T(8,128)S(1)}, u32[]{:S(2)}, u32[]{:S(2)}) %collective-permute-start.7) | collective-permute-done | bytes 32800 | tf_op jit(solution)/shard_map/ppermute | solution.py:240
  58.9 2.5 %collective-permute-done.6.far2 = bf16[128,512]{1,0:T(8,128)(2,1)S(1)} collective-permute-done((bf16[128,512]{1,0:T(8,128)(2,1)}, bf16[128,512]{1,0:T(8,128)(2,1)S(1)}, u32[]{:S(2)}, u32[]{:S(2)}) %collective-permute-start.6) | collective-permute-done | bytes 131104 | tf_op jit(solution)/shard_map/ppermute | solution.py:179
  61.4 1.4 %final.1 = bf16[128,512]{1,0:T(8,128)(2,1)} custom-call(s32[4]{0:T(128)S(1)} %pad_add_fusion.place, f32[128,512]{1,0:T(8,128)S(1)} %get-tuple-element.25.own, bf16[128,512]{1,0:T(8,128)(2,1)S(1)} %collective-permute-done.4.far0, bf16[128,512]{1,0:T(8,128)(2,1)S(1)} %collective-permute-done.5.far1, bf16[128,512]{1,0:T(8,128)(2,1)S(1)} %collective-permute-done.6.far2, ...), custom_call_target="tpu_custom_call" | custom-call | flops 16777216 | bytes 3145728 | tf_op jit(solution)/shard_map/final/pallas_call | solution.py:144
  (21 shorter events, 0.1 us)
Async XLA Ops:
  0.0 1.2 %copy-start = (bf16[1024,512]{1,0:T(8,128)(2,1)S(1)}, bf16[1024,512]{1,0:T(8,128)(2,1)}, u32[]{:S(2)}) copy-start(bf16[1024,512]{1,0:T(8,128)(2,1)} %param.9) | copy-start | bytes 3145732
  1.3 27.5 %collective-permute-start = (bf16[512,512]{1,0:T(8,128)(2,1)S(1)}, bf16[512,512]{1,0:T(8,128)(2,1)}, u32[]{:S(2)}, u32[]{:S(2)}) collective-permute-start(bf16[512,512]{1,0:T(8,128)(2,1)S(1)} %constant_dynamic-slice_fusion.rest_0_), channel_id=1, source_target_pairs={{0,8},{2,10},{4,12},{6,14},{8,0},{10,2},{12,4},{14,6},{1,9},{3,11}... | collective-permute-start | bytes 1572872 | tf_op jit(solution)/shard_map/ppermute | solution.py:185
  5.4 33.8 %collective-permute-start.2 = (bf16[512,512]{1,0:T(8,128)(2,1)S(1)}, bf16[512,512]{1,0:T(8,128)(2,1)}, u32[]{:S(2)}, u32[]{:S(2)}) collective-permute-start(bf16[512,512]{1,0:T(8,128)(2,1)S(1)} %constant_dynamic-slice_fusion.rest_0_), channel_id=1, source_target_pairs={{0,4},{2,6},{4,0},{6,2},{8,12},{10,14},{12,8},{14,10},{1,5},{3,7},... | collective-permute-start | bytes 1572872 | tf_op jit(solution)/shard_map/ppermute | solution.py:185
  7.0 1.6 %copy-start.1 = (bf16[128,8192]{1,0:T(8,128)(2,1)S(1)}, bf16[128,8192]{1,0:T(8,128)(2,1)}, u32[]{:S(2)}) copy-start(bf16[128,8192]{1,0:T(8,128)(2,1)} %hidden.3) | copy-start | bytes 6291460
  8.6 0.7 %copy-start.6 = (bf16[8192]{0:T(1024)(128)(2,1)S(1)}, bf16[8192]{0:T(1024)(128)(2,1)}, u32[]{:S(2)}) copy-start(bf16[8192]{0:T(1024)(128)(2,1)} %gain.1) | copy-start | bytes 49156
  11.8 16.9 %all-to-all-start = ((bf16[4,64,2048]{2,1,0:T(8,128)(2,1)}), bf16[4,64,2048]{2,1,0:T(8,128)(2,1)S(1)}, u32[]{:S(2)}, u32[]{:S(2)}) async-start(bf16[4,64,2048]{2,1,0:T(8,128)(2,1)} %norm_send.1), calls=%async_computation | async-start | bytes 2097152 | tf_op jit(solution)/shard_map/all_to_all | solution.py:197
  15.5 3.4 %copy-start.8 = (bf16[128,1,512,64]{2,3,1,0:T(8,128)(2,1)S(1)}, bf16[128,1,512,64]{2,3,1,0:T(8,128)(2,1)}, u32[]{:S(2)}) copy-start(bf16[128,1,512,64]{2,3,1,0:T(8,128)(2,1)} %param.10) | copy-start | bytes 25165828
  18.9 1.2 %copy-start.9 = (bf16[128,1,4096]{2,0,1:T(8,128)(2,1)S(1)}, bf16[128,1,4096]{2,0,1:T(8,128)(2,1)}, u32[]{:S(2)}) copy-start(bf16[128,1,4096]{2,0,1:T(8,128)(2,1)} %param.11) | copy-start | bytes 3145732
  20.1 0.7 %copy-start.10 = (s32[8]{0:T(128)S(1)}, s32[8]{0:T(128)}, u32[]{:S(2)}) copy-start(s32[8]{0:T(128)} %seg.1) | copy-start | bytes 100
  20.8 0.7 %copy-start.11 = (s32[128]{0:T(128)S(1)}, s32[128]{0:T(128)}, u32[]{:S(2)}) copy-start(s32[128]{0:T(128)} %slot_of.1) | copy-start | bytes 1540
  21.5 13.5 %copy-start.7 = (bf16[8192]{0:T(1024)(128)(2,1)S(1)}, bf16[8192]{0:T(1024)(128)(2,1)}, u32[]{:S(2)}) copy-start(bf16[8192]{0:T(1024)(128)(2,1)} %gain.1) | copy-start | bytes 49156
  23.1 0.9 %copy-start.5 = (bf16[8,80,512]{2,1,0:T(8,128)(2,1)}, bf16[8,80,512]{2,1,0:T(8,128)(2,1)S(1)}, u32[]{:S(2)}) copy-start(bf16[8,80,512]{2,1,0:T(8,128)(2,1)S(1)} %pick_panels.1) | copy-start | bytes 1966084
  28.7 10.4 %collective-permute-start.1 = (bf16[4,64,2048]{2,1,0:T(8,128)(2,1)S(1)}, bf16[4,64,2048]{2,1,0:T(8,128)(2,1)}, u32[]{:S(2)}, u32[]{:S(2)}) collective-permute-start(bf16[4,64,2048]{2,1,0:T(8,128)(2,1)S(1)} %all-to-all-done.mine), channel_id=1, source_target_pairs={{0,1},{1,0},{2,3},{3,2},{4,5},{5,4},{6,7},{7,6},{8,9},{9,8},{10,11... | collective-permute-start | bytes 3145736 | tf_op jit(solution)/shard_map/ppermute | solution.py:216
  28.7 20.3 %collective-permute-start.3 = (bf16[512,512]{1,0:T(8,128)(2,1)}, bf16[512,512]{1,0:T(8,128)(2,1)}, u32[]{:S(2)}, u32[]{:S(2)}) collective-permute-start(bf16[512,512]{1,0:T(8,128)(2,1)} %collective-permute-done.rest_2_), channel_id=1, source_target_pairs={{0,4},{2,6},{4,0},{6,2},{8,12},{10,14},{12,8},{14,10},{1,5},{3,7},... | collective-permute-start | bytes 1572872 | tf_op jit(solution)/shard_map/ppermute | solution.py:185
  29.3 26.1 %all-to-all-start.1 = ((bf16[8,80,512]{2,1,0:T(8,128)(2,1)}), bf16[8,80,512]{2,1,0:T(8,128)(2,1)S(1)}, u32[]{:S(2)}, u32[]{:S(2)}) async-start(bf16[8,80,512]{2,1,0:T(8,128)(2,1)} %copy-done.5), calls=%async_computation.1 | async-start | bytes 1310720 | tf_op jit(solution)/shard_map/all_to_all | solution.py:234
  35.0 1.6 %copy-start.2 = (bf16[128,8192]{1,0:T(8,128)(2,1)S(1)}, bf16[128,8192]{1,0:T(8,128)(2,1)}, u32[]{:S(2)}) copy-start(bf16[128,8192]{1,0:T(8,128)(2,1)} %hidden.3) | copy-start | bytes 6291460
  38.1 1.0 %copy-start.3 = (bf16[128,4096]{1,0:T(8,128)(2,1)}, bf16[128,4096]{1,0:T(8,128)(2,1)S(1)}, u32[]{:S(2)}) copy-start(bf16[128,4096]{1,0:T(8,128)(2,1)S(1)} %norm_half.1.acts) | copy-start | bytes 3145732
  51.9 7.0 %collective-permute-start.4 = (bf16[128,512]{1,0:T(8,128)(2,1)}, bf16[128,512]{1,0:T(8,128)(2,1)S(1)}, u32[]{:S(2)}, u32[]{:S(2)}) collective-permute-start(bf16[128,512]{1,0:T(8,128)(2,1)} %get-tuple-element.26), channel_id=1, source_target_pairs={{0,2},{2,0},{4,6},{6,4},{8,10},{10,8},{12,14},{14,12},{16,18},{18,... | collective-permute-start | bytes 393224 | tf_op jit(solution)/shard_map/ppermute | solution.py:179
  51.9 7.0 %collective-permute-start.5 = (bf16[128,512]{1,0:T(8,128)(2,1)}, bf16[128,512]{1,0:T(8,128)(2,1)S(1)}, u32[]{:S(2)}, u32[]{:S(2)}) collective-permute-start(bf16[128,512]{1,0:T(8,128)(2,1)} %get-tuple-element.27), channel_id=1, source_target_pairs={{0,16},{2,18},{4,20},{6,22},{8,24},{10,26},{12,28},{14,30},{16,0},... | collective-permute-start | bytes 393224 | tf_op jit(solution)/shard_map/ppermute | solution.py:179
  53.4 7.9 %collective-permute-start.6 = (bf16[128,512]{1,0:T(8,128)(2,1)}, bf16[128,512]{1,0:T(8,128)(2,1)S(1)}, u32[]{:S(2)}, u32[]{:S(2)}) collective-permute-start(bf16[128,512]{1,0:T(8,128)(2,1)} %get-tuple-element.28), channel_id=1, source_target_pairs={{0,18},{2,16},{4,22},{6,20},{8,26},{10,24},{12,30},{14,28},{16,2},... | collective-permute-start | bytes 393224 | tf_op jit(solution)/shard_map/ppermute | solution.py:179
  55.3 1.2 %copy-start.4 = (bf16[128,4096]{1,0:T(8,128)(2,1)S(1)}, bf16[128,4096]{1,0:T(8,128)(2,1)}, u32[]{:S(2)}) copy-start(bf16[128,4096]{1,0:T(8,128)(2,1)} %copy-done.3) | copy-start | bytes 3145732
  57.5 1.3 %collective-permute-start.7 = (f32[128,64]{1,0:T(8,128)S(1)}, f32[128,64]{1,0:T(8,128)S(1)}, u32[]{:S(2)}, u32[]{:S(2)}) collective-permute-start(f32[128,64]{1,0:T(8,128)S(1)} %low_rank.1.low_mine), channel_id=1, source_target_pairs={{0,1},{1,0},{2,3},{3,2},{4,5},{5,4},{6,7},{7,6},{8,9},{9,8},{10,11... | collective-permute-start | bytes 98312 | tf_op jit(solution)/shard_map/ppermute | solution.py:240

commit v4 on v3

--- a/solution.py
+++ b/solution.py
@@ -10,23 +10,23 @@
 SEGMENT_TOKENS = 128
 EPS = 1e-05
 VMEM_LIMIT = 16 * 1024 * 1024
-PAD_ROWS = 16
+PAD_ROWS = 8
 LONG = 1 << 36
-PEERS = ((1, 0), (0, 1), (1, 1))
+PEERS = ((1, 1), (1, 0), (0, 1))
 
 
 def params():
     return pltpu.CompilerParams(vmem_limit_bytes=VMEM_LIMIT)
 
 
-def gather_kernel(place, seg, slot_of, down, up, out, sem):
+def gather_kernel(seg, slot_of, down, up, out, sem):
     peers = out.shape[0]
     rank, feats = down.shape[1:]
     up_rows = up.shape[1] // feats
     copies = []
-    row = lax.broadcasted_iota(jnp.int32, (PAD_ROWS, up.shape[0]), 0)
-    col = lax.broadcasted_iota(jnp.int32, (PAD_ROWS, up.shape[0]), 1)
-    hot = jnp.zeros((PAD_ROWS, up.shape[0]), jnp.float32)
+    row = lax.broadcasted_iota(jnp.int32, (2 * PAD_ROWS, up.shape[0]), 0)
+    col = lax.broadcasted_iota(jnp.int32, (2 * PAD_ROWS, up.shape[0]), 1)
+    hot = jnp.zeros((2 * PAD_ROWS, up.shape[0]), jnp.float32)
     for k in range(peers):
         slot = slot_of[seg[k]]
         copy = pltpu.make_async_copy(down.at[slot], out.at[k, pl.ds(0, rank)], sem.at[k])
@@ -36,14 +36,13 @@
     picked = jnp.dot(hot.astype(jnp.bfloat16), up[...], preferred_element_type=jnp.float32)
     for k in range(peers):
         rows = [picked[k : k + 1, r * feats : (r + 1) * feats] for r in range(up_rows)]
-        rows.append(jnp.zeros((PAD_ROWS - up_rows, feats), jnp.float32))
         out[k, pl.ds(rank, PAD_ROWS), :] = jnp.concatenate(rows, axis=0).astype(jnp.bfloat16)
     for copy in copies:
         copy.wait()
 
 
-def wanted(place, peer, step, row_count, chunk):
-    shard = (place[1] * 2 + peer % 2) ^ (2 * step)
+def wanted(peer, step, row_count, chunk):
+    shard = (lax.axis_index("tensor") // 2 * 2 + peer % 2) ^ (2 * step)
     return pl.multiple_of(shard * row_count + (peer // 2) * chunk, chunk)
 
 
@@ -56,10 +55,10 @@
     return lax.rsqrt(jnp.mean(values * values, axis=1, keepdims=True) + EPS)
 
 
-def norm_send_kernel(steps, row_count, chunk, place, hidden, gain_hbm, out, held, gain, sem):
+def norm_send_kernel(steps, row_count, chunk, hidden, gain_hbm, out, held, gain, sem):
     rows = held.shape[0]
     cut = rows // 4
-    first = place[2] * rows
+    first = lax.axis_index("pool") * rows
     copies = [pltpu.make_async_copy(gain_hbm, gain, sem.at[4])]
     for i in range(4):
         at = pl.ds(pl.multiple_of(first + i * cut, cut), cut)
@@ -73,41 +72,42 @@
         inv = inv_rms(part)
         for peer in range(4):
             for step in range(steps):
-                at = pl.ds(wanted(place, peer, step, row_count, chunk), chunk)
+                at = pl.ds(wanted(peer, step, row_count, chunk), chunk)
                 out[peer, pl.ds(i * cut, cut), step * chunk : (step + 1) * chunk] = normed_piece(part, gain, inv, at)
 
 
-def norm_half_kernel(place, hidden, gain, out, held, sem):
+def norm_half_kernel(token, hidden, gain, out):
     half = hidden.shape[1] // 2
-    at = pl.ds(pl.multiple_of(place[2] * half, half), half)
-    held[...] = normed_piece(hidden, gain, inv_rms(hidden), at)
-    copy = pltpu.make_async_copy(held, out, sem)
-    copy.start()
-    copy.wait()
-
-
-def in_order(place, mine, other):
-    me = place[3] * 2 + place[0] % 2
-    quarters = [me ^ 1, me ^ 2, me ^ 3, me]
-    return jnp.concatenate([mine[q] for q in quarters] + [other[q] for q in quarters], axis=0)
-
-
-def early_kernel(place, mine, other, *rest):
+    at = pl.ds(pl.multiple_of(lax.axis_index("pool") * half, half), half)
+    out[...] = normed_piece(hidden, gain, inv_rms(hidden), at)
+
+
+def tick_kernel(token, out):
+    out[...] = token[...]
+
+
+def in_order(mine, other, cols):
+    me = lax.axis_index("groups") * 2 + lax.axis_index("tensor") % 2
+    quarters = [me ^ 3, me ^ 1, me ^ 2, me]
+    return jnp.concatenate([half[q, :, cols] for half in (mine, other) for q in quarters], axis=0)
+
+
+def early_kernel(mine, other, *rest):
     weights, out = rest[:-1], rest[-1]
-    x = in_order(place, mine, other)
     total = jnp.zeros(out.shape, jnp.float32)
     first = 0
     for w in weights:
-        total += jnp.dot(x[:, first : first + w.shape[0]], w[...], preferred_element_type=jnp.float32)
+        x = in_order(mine, other, slice(first, first + w.shape[0]))
+        total += jnp.dot(x, w[...], preferred_element_type=jnp.float32)
         first += w.shape[0]
     out[...] = total
 
 
-def late_kernel(place, mine, other, weight, early, out0, out1, out2, own):
+def late_kernel(mine, other, weight, early, out0, out1, out2, own):
     rows = mine.shape[1]
-    x = in_order(place, mine, other)
+    x = in_order(mine, other, slice(mine.shape[2] - weight.shape[0], mine.shape[2]))
     total = early[...] + jnp.dot(x, weight[...], preferred_element_type=jnp.float32)
-    half = place[2]
+    half = lax.axis_index("pool")
     for part in range(2):
         at = pl.ds(pl.multiple_of((half if part == 0 else 1 - half) * rows, rows), rows)
         for k, out in enumerate((out0, out1, out2, own)):
@@ -115,7 +115,7 @@
             out[at, :] = total[first : first + rows].astype(out.dtype)
 
 
-def rank_kernel(place, acts, pieces, out):
+def rank_kernel(acts, pieces, out):
     rank = out.shape[1]
     feats = pieces.shape[2]
     total = jnp.zeros(out.shape, jnp.float32)
@@ -125,7 +125,7 @@
     out[...] = total
 
 
-def final_kernel(up_rows, place, own, far0, far1, far2, low_mine, low_other, pieces, out):
+def final_kernel(up_rows, own, far0, far1, far2, low_mine, low_other, pieces, out):
     rank = low_mine.shape[1]
     up = [pieces[k, rank : rank + PAD_ROWS, :].astype(jnp.float32)[:up_rows] for k in range(pieces.shape[0])]
     low = (low_mine[...] + low_other[...]).astype(jnp.bfloat16)
@@ -137,10 +137,10 @@
 
 
 def whole(shape):
-    return pl.BlockSpec(shape, lambda *_: (0,) * len(shape))
-
-
-def call(kernel, prefetch, args, in_specs, outs, out_specs, grid=(1,), scratch=(), alias=None, name=None, flops=0, nbytes=0):
+    return pl.BlockSpec(memory_space=pltpu.VMEM)
+
+
+def call(kernel, prefetch, args, in_specs, outs, out_specs, grid=(), scratch=(), alias=None, name=None, flops=0, nbytes=0):
     return pl.pallas_call(
         kernel,
         grid_spec=pltpu.PrefetchScalarGridSpec(
@@ -161,7 +161,7 @@
 def square_device(hidden, norm_gain, kv_weight, down_panels, up_panels, seg_adapter, slot_of):
     tokens, features = hidden.shape
     groups, peers = lax.axis_size("groups"), lax.axis_size("tensor")
-    g, t, h = (lax.axis_index(axis) for axis in ("groups", "tensor", "pool"))
+    g = lax.axis_index("groups")
     steps = peers // 2
     row_count, cols = kv_weight.shape
     chunk = row_count // groups
@@ -169,7 +169,6 @@
     span = steps * chunk
     feats, rank = down_panels.shape[2:]
     bf16, f32 = jnp.bfloat16, jnp.float32
-    place = jnp.stack([t, t // 2, h, g]).astype(jnp.int32)
     up_rows = up_panels.shape[2] // feats
     hbm = pl.BlockSpec(memory_space=pltpu.HBM)
     cores = [(0, 1), (1, 0)]
@@ -184,62 +183,68 @@
     def along_z(x, step):
         return lax.ppermute(x, "tensor", [(i, i ^ (2 * step)) for i in range(peers)])
 
-    second = along_z(own_w, 2)
-    first = along_z(own_w, 1)
+    second, first = along_z(own_w, 2), along_z(own_w, 1)
     squares = [[a * peers + z * 2 + x for a in range(groups) for x in range(2)] for z in range(steps)]
     send = call(
-        functools.partial(norm_send_kernel, steps, row_count, chunk), [place], [hidden, norm_gain], [hbm, hbm],
+        functools.partial(norm_send_kernel, steps, row_count, chunk), [], [hidden, norm_gain], [hbm, hbm],
         jax.ShapeDtypeStruct((4, rows, span), bf16), whole((4, rows, span)),
         scratch=[pltpu.VMEM((rows, features), bf16), pltpu.VMEM((features,), bf16), pltpu.SemaphoreType.DMA((5,))],
         name="norm_send", flops=6 * rows * features, nbytes=4 * rows * features,
     )
-    send, later = lax.optimization_barrier((send, place))
+    send, later = lax.optimization_barrier((send, slot_of))
     mine = lax.all_to_all(
         send, ("groups", "tensor"), split_axis=0, concat_axis=0, tiled=True, axis_index_groups=squares
     )
 
     piece_shape = (peers, rank + PAD_ROWS, feats)
     pieces = call(
-        gather_kernel, [later, seg_adapter, slot_of],
+        gather_kernel, [seg_adapter, later],
         [down_panels[:, 0].transpose(0, 2, 1), up_panels[:, 0]],
         [hbm, whole((up_panels.shape[0], up_panels.shape[2]))],
         jax.ShapeDtypeStruct(piece_shape, bf16), whole(piece_shape),
         scratch=[pltpu.SemaphoreType.DMA((peers,))], name="pick_panels", flops=LONG, nbytes=3 << 20,
     )
-    mine, pieces, later, second = lax.optimization_barrier((mine, pieces, later, second))
+    mine, pieces, later, second, first = lax.optimization_barrier((mine, pieces, later, second, first))
     third = along_z(second, 1)
-    acts = call(
-        norm_half_kernel, [later], [hidden, norm_gain], [whole((tokens, features)), whole((features,))],
-        jax.ShapeDtypeStruct((tokens, features // 2), bf16), hbm,
-        scratch=[pltpu.VMEM((tokens, features // 2), bf16), pltpu.SemaphoreType.DMA], name="norm_half", flops=LONG, nbytes=4 * tokens * features,
+    tick = call(
+        tick_kernel, [], [later], [whole(later.shape)], jax.ShapeDtypeStruct(later.shape, jnp.int32),
+        whole(later.shape), name="tick", flops=LONG,
     )
     others = [lax.ppermute(mine, "pool", cores)]
     weight = whole((chunk, cols))
     early = call(
-        early_kernel, [place], [mine, *others, own_w, first, second],
-        [pl.BlockSpec((4, rows, span - chunk), lambda i, p: (0, 0, 0))] * 2 + [weight] * 3,
+        early_kernel, [], [mine, *others, own_w, first, second],
+        [weight] * 5,
         jax.ShapeDtypeStruct((4 * tokens, cols), f32), whole((4 * tokens, cols)),
         name="early_rows", flops=24 * tokens * chunk * cols, nbytes=4 << 20,
     )
-    acts, early, third = lax.optimization_barrier((acts, early, third))
+    early, pieces = lax.optimization_barrier((early, pieces))
+    tick, early, third = lax.optimization_barrier((tick, early, third))
     late = call(
-        late_kernel, [place], [mine, *others, third, early],
-        [pl.BlockSpec((4, rows, chunk), lambda i, p: (0, 0, steps - 1))] * 2 + [weight, whole(early.shape)],
+        late_kernel, [], [mine, *others, third, early],
+        [weight] * 4,
         [jax.ShapeDtypeStruct((tokens, cols), bf16)] * 3 + [jax.ShapeDtypeStruct((tokens, cols), f32)],
         [whole((tokens, cols))] * 4,
         name="late_rows", flops=8 * tokens * chunk * cols, nbytes=4 << 20,
     )
+    *late, last = lax.optimization_barrier((*late, tick))
+    acts = call(
+        norm_half_kernel, [], [last, hidden, norm_gain],
+        [pl.BlockSpec(memory_space=pl.ANY), whole((tokens, features)), whole((features,))],
+        jax.ShapeDtypeStruct((tokens, features // 2), bf16), whole((tokens, features // 2)),
+        name="norm_half", flops=6 * tokens * features, nbytes=4 * tokens * features,
+    )
     parts = [to_peer(x, *peer) for x, peer in zip(late[:3], PEERS)]
 
     pieces = lax.all_to_all(pieces, "tensor", split_axis=0, concat_axis=0, tiled=True)
     low_mine = call(
-        rank_kernel, [place], [acts, pieces], [whole(acts.shape), whole(piece_shape)],
+        rank_kernel, [], [acts, pieces], [whole(acts.shape), whole(piece_shape)],
         jax.ShapeDtypeStruct((tokens, rank), f32), whole((tokens, rank)),
         name="low_rank", flops=2 * tokens * rank * features // 2, nbytes=2 << 20,
     )
     low_other = lax.ppermute(low_mine, "pool", cores)
     return call(
-        functools.partial(final_kernel, up_rows), [place],
+        functools.partial(final_kernel, up_rows), [],
         [late[3], *parts, low_mine, low_other, pieces],
         [whole((tokens, cols))] * 4 + [whole((tokens, rank))] * 2 + [whole(piece_shape)],
         jax.ShapeDtypeStruct((tokens, cols), bf16), whole((tokens, cols)),
@@ -291,7 +296,7 @@
         and kv_weight.shape[0] % (128 * groups) == 0
         and feats == kv_weight.shape[1]
         and up_panels.shape[2] % (8 * feats) == 0
-        and up_panels.shape[2] // feats <= PAD_ROWS
+        and up_panels.shape[2] // feats == PAD_ROWS
     )
     body = square_device if fits else gathered_device
     return body(hidden, norm_gain, kv_weight, down_panels, up_panels, seg_adapter, slot_of)

time: 63.5 us -> 60.3 us (0.950)
  Pallas kernels: 13.8 us -> 10.7 us
  local copies, waits for them, and re-layouts: 14.1 us -> 11.5 us
  waiting for transfers between devices: 15.5 us -> 17.6 us
    all_to_all x1, waiting for transfers between devices: 0.01 us -> 7.17 us  [square_device(): lax.all_to_all(pieces, 'tensor', split_axis=0, concat_axis=0, tiled=True)]
    ppermute x3, waiting for transfers between devices: 11.7 us -> 7.99 us  [along_z(): return lax.ppermute(x, 'tensor', [(i, i ^ 2 * step) for i in range(peers)])]
    pallas_call x7 -> x8, Pallas kernels: 13.8 us -> 10.7 us  [call(): pl.pallas_call(kernel, grid_spec=pltpu.PrefetchScalarGridSpec(num_scalar_...]
    unnamed x24 -> x28, local copies, waits for them, and re-layouts: 14.1 us -> 11.4 us
    ppermute x3, waiting for transfers between devices: 2.53 us -> 0.01 us  [to_peer(): return lax.ppermute(x, ('groups', 'tensor'), pairs)]
    ppermute x1, waiting for transfers between devices: 0.01 us -> 1.17 us  [square_device(): others = [lax.ppermute(mine, 'pool', cores)]]
    ppermute x3, starting transfers between devices: 6.2 us -> 7.17 us  [along_z(): return lax.ppermute(x, 'tensor', [(i, i ^ 2 * step) for i in range(peers)])]
  transfers between devices with their start and end apart: 10 -> 10, of which waited for: 4 -> 6; matrix products, arithmetic and copies ran while one was open for 0% -> 0% of each run, Pallas kernels for 20% -> 17%
where the time goes in v4:
time: 60.3 us; the launch traced here: 59.7 us
  starting transfers between devices  19.8 us (33%)
  waiting for transfers between devices  17.6 us (29%)
  local copies, waits for them, and re-layouts  11.5 us (19%)
  Pallas kernels  10.7 us (18%)
    unnamed x28, local copies, waits for them, and re-layouts  11.4 us
    pallas_call x8, Pallas kernels, call(): pl.pallas_call(kernel, grid_spec=pltpu.PrefetchScalarGridSpec(num_scalar_...  10.7 us
    ppermute x3, waiting for transfers between devices, along_z(): return lax.ppermute(x, 'tensor', [(i, i ^ 2 * step) for i in range(peers)])  7.99 us
    all_to_all x1, waiting for transfers between devices, square_device(): lax.all_to_all(pieces, 'tensor', split_axis=0, concat_axis=0, tiled=True)  7.17 us
    ppermute x3, starting transfers between devices, along_z(): return lax.ppermute(x, 'tensor', [(i, i ^ 2 * step) for i in range(peers)])  7.17 us
    all_to_all x1, starting transfers between devices, square_device(): lax.all_to_all(pieces, 'tensor', split_axis=0, concat_axis=0, tiled=True)  5.34 us
    all_to_all x1, starting transfers between devices, square_device(): lax.all_to_all(send, ('groups', 'tensor'), split_axis=0, concat_axis=0, t...  3.73 us
    ppermute x3, starting transfers between devices, to_peer(): return lax.ppermute(x, ('groups', 'tensor'), pairs)  3.49 us
  transfers between devices with their start and end apart: 10, of which 6 were waited for; matrix products, arithmetic and copies ran while one was open for 0% of the time, Pallas kernels for 17%

profile of v4, /device:TPU:0, one launch (start us, length us, event | category | flops | bytes accessed | tf_op | source)
XLA Modules:
  0.0 59.7 jit_solution(8352702886520364606)
XLA Ops:
  0.0 1.2 %copy-done = bf16[1024,512]{1,0:T(8,128)(2,1)S(1)} copy-done((bf16[1024,512]{1,0:T(8,128)(2,1)S(1)}, bf16[1024,512]{1,0:T(8,128)(2,1)}, u32[]{:S(2)}) %copy-start) | copy-done | bytes 1048600
  1.3 4.1 %collective-permute-start = (bf16[512,512]{1,0:T(8,128)(2,1)S(1)}, bf16[512,512]{1,0:T(8,128)(2,1)S(1)}, u32[]{:S(2)}, u32[]{:S(2)}) collective-permute-start(bf16[512,512]{1,0:T(8,128)(2,1)S(1)} %constant_dynamic-slice_fusion.rest_0_), channel_id=1, source_target_pairs={{0,8},{2,10},{4,12},{6,14},{8,0},{10,2},{12,4},{14,6},{1,9},{3,11}... | collective-permute-start | bytes 1572872 | tf_op jit(solution)/shard_map/ppermute | solution.py:184
  5.4 1.6 %collective-permute-start.1 = (bf16[512,512]{1,0:T(8,128)(2,1)S(1)}, bf16[512,512]{1,0:T(8,128)(2,1)}, u32[]{:S(2)}, u32[]{:S(2)}) collective-permute-start(bf16[512,512]{1,0:T(8,128)(2,1)S(1)} %constant_dynamic-slice_fusion.rest_0_), channel_id=1, source_target_pairs={{0,4},{2,6},{4,0},{6,2},{8,12},{10,14},{12,8},{14,10},{1,5},{3,7},... | collective-permute-start | bytes 1572872 | tf_op jit(solution)/shard_map/ppermute | solution.py:184
  6.9 1.6 %copy-done.1 = bf16[128,8192]{1,0:T(8,128)(2,1)S(1)} copy-done((bf16[128,8192]{1,0:T(8,128)(2,1)S(1)}, bf16[128,8192]{1,0:T(8,128)(2,1)}, u32[]{:S(2)}) %copy-start.1) | copy-done | bytes 2097176
  8.5 0.7 %copy-done.7 = bf16[8192]{0:T(1024)(128)(2,1)S(1)} copy-done((bf16[8192]{0:T(1024)(128)(2,1)S(1)}, bf16[8192]{0:T(1024)(128)(2,1)}, u32[]{:S(2)}) %copy-start.7) | copy-done | bytes 16408
  9.3 1.9 %norm_send.1 = bf16[4,64,2048]{2,1,0:T(8,128)(2,1)} custom-call(bf16[128,8192]{1,0:T(8,128)(2,1)S(1)} %copy-done.1, bf16[8192]{0:T(1024)(128)(2,1)S(1)} %copy-done.7), custom_call_target="tpu_custom_call" | custom-call | flops 3145728 | bytes 2097152 | tf_op jit(solution)/shard_map/norm_send/pallas_call | solution.py:144
  11.2 3.7 %all-to-all-start = ((bf16[4,64,2048]{2,1,0:T(8,128)(2,1)}), bf16[4,64,2048]{2,1,0:T(8,128)(2,1)S(1)}, u32[]{:S(2)}, u32[]{:S(2)}) async-start(bf16[4,64,2048]{2,1,0:T(8,128)(2,1)} %norm_send.1), calls=%async_computation | async-start | bytes 2097152 | tf_op jit(solution)/shard_map/all_to_all | solution.py:195
  14.9 3.4 %copy-done.9 = bf16[128,1,512,64]{2,3,1,0:T(8,128)(2,1)S(1)} copy-done((bf16[128,1,512,64]{2,3,1,0:T(8,128)(2,1)S(1)}, bf16[128,1,512,64]{2,3,1,0:T(8,128)(2,1)}, u32[]{:S(2)}) %copy-start.9) | copy-done | bytes 8388632
  18.3 1.2 %copy-done.10 = bf16[128,1,4096]{2,0,1:T(8,128)(2,1)S(1)} copy-done((bf16[128,1,4096]{2,0,1:T(8,128)(2,1)S(1)}, bf16[128,1,4096]{2,0,1:T(8,128)(2,1)}, u32[]{:S(2)}) %copy-start.10) | copy-done | bytes 1048600
  19.5 0.7 %copy-done.11 = s32[8]{0:T(128)S(1)} copy-done((s32[8]{0:T(128)S(1)}, s32[8]{0:T(128)}, u32[]{:S(2)}) %copy-start.11) | copy-done | bytes 56
  20.2 0.7 %copy-done.12 = s32[128]{0:T(128)S(1)} copy-done((s32[128]{0:T(128)S(1)}, s32[128]{0:T(128)}, u32[]{:S(2)}) %copy-start.12) | copy-done | bytes 536
  20.8 2.5 %pick_panels.1 = bf16[8,72,512]{2,1,0:T(8,128)(2,1)} custom-call(s32[8]{0:T(128)S(1)} %copy-done.11, s32[128]{0:T(128)S(1)} %copy-done.12, bf16[128,64,512]{2,1,0:T(8,128)(2,1)S(1)} %bitcast.4, bf16[128,4096]{1,0:T(8,128)(2,1)S(1)} %bitcast.5), custom_call_target="tpu_custom_call" | custom-call | flops 68719476736 | bytes 3145728 | tf_op jit(solution)/shard_map/pick_panels/pallas_call | solution.py:144
  23.3 5.3 %collective-permute-done.rest_2_ = bf16[512,512]{1,0:T(8,128)(2,1)S(1)} collective-permute-done((bf16[512,512]{1,0:T(8,128)(2,1)S(1)}, bf16[512,512]{1,0:T(8,128)(2,1)S(1)}, u32[]{:S(2)}, u32[]{:S(2)}) %collective-permute-start) | collective-permute-done | bytes 524320 | tf_op jit(solution)/shard_map/ppermute | solution.py:184
  28.6 0.3 collective-permute-done.1.rest_1_
  28.9 1.5 %collective-permute-start.3 = (bf16[512,512]{1,0:T(8,128)(2,1)S(1)}, bf16[512,512]{1,0:T(8,128)(2,1)}, u32[]{:S(2)}, u32[]{:S(2)}) collective-permute-start(bf16[512,512]{1,0:T(8,128)(2,1)S(1)} %collective-permute-done.rest_2_), channel_id=1, source_target_pairs={{0,4},{2,6},{4,0},{6,2},{8,12},{10,14},{12,8},{14,10},{1,5},{3,7},... | collective-permute-start | bytes 1572872 | tf_op jit(solution)/shard_map/ppermute | solution.py:184
  30.4 1.2 %collective-permute-done.2.other = bf16[4,64,2048]{2,1,0:T(8,128)(2,1)S(1)} collective-permute-done((bf16[4,64,2048]{2,1,0:T(8,128)(2,1)S(1)}, bf16[4,64,2048]{2,1,0:T(8,128)(2,1)S(1)}, u32[]{:S(2)}, u32[]{:S(2)}) %collective-permute-start.2) | collective-permute-done | bytes 1048608 | tf_op jit(solution)/shard_map/ppermute | solution.py:213
  31.6 2.0 %early_rows.1.early = f32[512,512]{1,0:T(8,128)S(1)} custom-call(bf16[4,64,2048]{2,1,0:T(8,128)(2,1)S(1)} %all-to-all-done.mine, bf16[4,64,2048]{2,1,0:T(8,128)(2,1)S(1)} %collective-permute-done.2.other, bf16[512,512]{1,0:T(8,128)(2,1)S(1)} %constant_dynamic-slice_fusion.rest_0_, bf16[512,512]{1,0:T(8,128)(2,1)} %collective-permute-done.1.rest_1_, ...), custom_call_target="tpu_custom_call" | custom-call | flops 805306368 | bytes 4194304 | tf_op jit(solution)/shard_map/early_rows/pallas_call | solution.py:144
  33.6 1.0 %copy-done.3 = bf16[4,64,2048]{2,1,0:T(8,128)(2,1)} copy-done((bf16[4,64,2048]{2,1,0:T(8,128)(2,1)}, bf16[4,64,2048]{2,1,0:T(8,128)(2,1)S(1)}, u32[]{:S(2)}) %copy-start.3) | copy-done | bytes 1048600
  34.6 1.0 %copy-done.5 = f32[512,512]{1,0:T(8,128)} copy-done((f32[512,512]{1,0:T(8,128)}, f32[512,512]{1,0:T(8,128)S(1)}, u32[]{:S(2)}) %copy-start.5) | copy-done | bytes 1048600
  35.6 5.3 %all-to-all-start.1 = ((bf16[8,72,512]{2,1,0:T(8,128)(2,1)}), bf16[8,72,512]{2,1,0:T(8,128)(2,1)S(1)}, u32[]{:S(2)}, u32[]{:S(2)}) async-start(bf16[8,72,512]{2,1,0:T(8,128)(2,1)} %pick_panels.1), calls=%async_computation.1 | async-start | bytes 1179648 | tf_op jit(solution)/shard_map/all_to_all | solution.py:239
  41.0 0.0 copy-start.8
  41.0 2.4 %collective-permute-done.3.weight = bf16[512,512]{1,0:T(8,128)(2,1)} collective-permute-done((bf16[512,512]{1,0:T(8,128)(2,1)S(1)}, bf16[512,512]{1,0:T(8,128)(2,1)}, u32[]{:S(2)}, u32[]{:S(2)}) %collective-permute-start.3) | collective-permute-done | bytes 524320 | tf_op jit(solution)/shard_map/ppermute | solution.py:184
  43.4 2.1 %late_rows.1 = (bf16[128,512]{1,0:T(8,128)(2,1)}, bf16[128,512]{1,0:T(8,128)(2,1)}, bf16[128,512]{1,0:T(8,128)(2,1)S(1)}, f32[128,512]{1,0:T(8,128)S(1)}) custom-call(bf16[4,64,2048]{2,1,0:T(8,128)(2,1)S(1)} %all-to-all-done.mine, bf16[4,64,2048]{2,1,0:T(8,128)(2,1)S(1)} %copy-done.4, bf16[512,512]{1,0:T(8,128)(2,1)} %collective-permute-done.3.weight, ...), custom_call_target="tpu_custom_call" | custom-call | flops 268435456 | bytes 4194304 | tf_op jit(solution)/shard_map/late_rows/pallas_call | solution.py:144
  45.5 2.5 %collective-permute-start.4 = (bf16[128,512]{1,0:T(8,128)(2,1)}, bf16[128,512]{1,0:T(8,128)(2,1)S(1)}, u32[]{:S(2)}, u32[]{:S(2)}) collective-permute-start(bf16[128,512]{1,0:T(8,128)(2,1)} %get-tuple-element.42), channel_id=1, source_target_pairs={{0,18},{2,16},{4,22},{6,20},{8,26},{10,24},{12,30},{14,28},{16,2},... | collective-permute-start | bytes 393224 | tf_op jit(solution)/shard_map/ppermute | solution.py:178
  48.0 0.5 collective-permute-start.5
  48.5 0.5 collective-permute-start.6
  49.0 0.9 %norm_half.1.acts = bf16[128,4096]{1,0:T(8,128)(2,1)S(1)} custom-call(s32[128]{0:T(128)S(1)} %tick.1.token, bf16[128,8192]{1,0:T(8,128)(2,1)S(1)} %copy-done.2, bf16[8192]{0:T(1024)(128)(2,1)S(1)} %copy-done.8), custom_call_target="tpu_custom_call" | custom-call | flops 6291456 | bytes 4194304 | tf_op jit(solution)/shard_map/norm_half/pallas_call | solution.py:144
  50.0 7.2 %all-to-all-done.1.pieces = bf16[8,72,512]{2,1,0:T(8,128)(2,1)S(1)} async-done(((bf16[8,72,512]{2,1,0:T(8,128)(2,1)}), bf16[8,72,512]{2,1,0:T(8,128)(2,1)S(1)}, u32[]{:S(2)}, u32[]{:S(2)}) %all-to-all-start.1) | async-done | bytes 589856 | tf_op jit(solution)/shard_map/all_to_all | solution.py:239
  57.1 0.4 low_rank.1.low_mine
  57.6 0.1 collective-permute-start.7
  57.7 1.2 %collective-permute-done.7.low_other = f32[128,64]{1,0:T(8,128)S(1)} collective-permute-done((f32[128,64]{1,0:T(8,128)S(1)}, f32[128,64]{1,0:T(8,128)S(1)}, u32[]{:S(2)}, u32[]{:S(2)}) %collective-permute-start.7) | collective-permute-done | bytes 32800 | tf_op jit(solution)/shard_map/ppermute | solution.py:245
  58.9 0.9 %final.1 = bf16[128,512]{1,0:T(8,128)(2,1)} custom-call(f32[128,512]{1,0:T(8,128)S(1)} %get-tuple-element.41.own, bf16[128,512]{1,0:T(8,128)(2,1)S(1)} %collective-permute-done.4.far0, bf16[128,512]{1,0:T(8,128)(2,1)S(1)} %collective-permute-done.5.far1, bf16[128,512]{1,0:T(8,128)(2,1)S(1)} %collective-permute-done.6.far2, f32[128,64]{1,0:T(8,128)S(1)} %low_rank.1.low_mine, ...), custom_call_target="tpu_custom_call" | custom-call | flops 16777216 | bytes 3145728 | tf_op jit(solution)/shard_map/final/pallas_call | solution.py:144
  (25 shorter events, 0.1 us)
Async XLA Ops:
  0.0 1.2 %copy-start = (bf16[1024,512]{1,0:T(8,128)(2,1)S(1)}, bf16[1024,512]{1,0:T(8,128)(2,1)}, u32[]{:S(2)}) copy-start(bf16[1024,512]{1,0:T(8,128)(2,1)} %param.9) | copy-start | bytes 3145732
  1.3 27.4 %collective-permute-start = (bf16[512,512]{1,0:T(8,128)(2,1)S(1)}, bf16[512,512]{1,0:T(8,128)(2,1)S(1)}, u32[]{:S(2)}, u32[]{:S(2)}) collective-permute-start(bf16[512,512]{1,0:T(8,128)(2,1)S(1)} %constant_dynamic-slice_fusion.rest_0_), channel_id=1, source_target_pairs={{0,8},{2,10},{4,12},{6,14},{8,0},{10,2},{12,4},{14,6},{1,9},{3,11}... | collective-permute-start | bytes 1572872 | tf_op jit(solution)/shard_map/ppermute | solution.py:184
  5.4 23.6 %collective-permute-start.1 = (bf16[512,512]{1,0:T(8,128)(2,1)S(1)}, bf16[512,512]{1,0:T(8,128)(2,1)}, u32[]{:S(2)}, u32[]{:S(2)}) collective-permute-start(bf16[512,512]{1,0:T(8,128)(2,1)S(1)} %constant_dynamic-slice_fusion.rest_0_), channel_id=1, source_target_pairs={{0,4},{2,6},{4,0},{6,2},{8,12},{10,14},{12,8},{14,10},{1,5},{3,7},... | collective-permute-start | bytes 1572872 | tf_op jit(solution)/shard_map/ppermute | solution.py:184
  6.9 1.6 %copy-start.1 = (bf16[128,8192]{1,0:T(8,128)(2,1)S(1)}, bf16[128,8192]{1,0:T(8,128)(2,1)}, u32[]{:S(2)}) copy-start(bf16[128,8192]{1,0:T(8,128)(2,1)} %hidden.3) | copy-start | bytes 6291460
  8.5 0.7 %copy-start.7 = (bf16[8192]{0:T(1024)(128)(2,1)S(1)}, bf16[8192]{0:T(1024)(128)(2,1)}, u32[]{:S(2)}) copy-start(bf16[8192]{0:T(1024)(128)(2,1)} %gain.1) | copy-start | bytes 49156
  11.2 17.7 %all-to-all-start = ((bf16[4,64,2048]{2,1,0:T(8,128)(2,1)}), bf16[4,64,2048]{2,1,0:T(8,128)(2,1)S(1)}, u32[]{:S(2)}, u32[]{:S(2)}) async-start(bf16[4,64,2048]{2,1,0:T(8,128)(2,1)} %norm_send.1), calls=%async_computation | async-start | bytes 2097152 | tf_op jit(solution)/shard_map/all_to_all | solution.py:195
  14.9 3.4 %copy-start.9 = (bf16[128,1,512,64]{2,3,1,0:T(8,128)(2,1)S(1)}, bf16[128,1,512,64]{2,3,1,0:T(8,128)(2,1)}, u32[]{:S(2)}) copy-start(bf16[128,1,512,64]{2,3,1,0:T(8,128)(2,1)} %param.10) | copy-start | bytes 25165828
  18.3 1.2 %copy-start.10 = (bf16[128,1,4096]{2,0,1:T(8,128)(2,1)S(1)}, bf16[128,1,4096]{2,0,1:T(8,128)(2,1)}, u32[]{:S(2)}) copy-start(bf16[128,1,4096]{2,0,1:T(8,128)(2,1)} %param.11) | copy-start | bytes 3145732
  19.5 0.7 %copy-start.11 = (s32[8]{0:T(128)S(1)}, s32[8]{0:T(128)}, u32[]{:S(2)}) copy-start(s32[8]{0:T(128)} %seg.1) | copy-start | bytes 100
  20.2 0.7 %copy-start.12 = (s32[128]{0:T(128)S(1)}, s32[128]{0:T(128)}, u32[]{:S(2)}) copy-start(s32[128]{0:T(128)} %token_) | copy-start | bytes 1540
  20.8 20.1 %copy-start.13 = (s32[128]{0:T(128)S(1)}, s32[128]{0:T(128)}, u32[]{:S(2)}) copy-start(s32[128]{0:T(128)} %token_) | copy-start | bytes 1540
  28.9 2.7 %collective-permute-start.2 = (bf16[4,64,2048]{2,1,0:T(8,128)(2,1)S(1)}, bf16[4,64,2048]{2,1,0:T(8,128)(2,1)S(1)}, u32[]{:S(2)}, u32[]{:S(2)}) collective-permute-start(bf16[4,64,2048]{2,1,0:T(8,128)(2,1)S(1)} %all-to-all-done.mine), channel_id=1, source_target_pairs={{0,1},{1,0},{2,3},{3,2},{4,5},{5,4},{6,7},{7,6},{8,9},{9,8},{10,11... | collective-permute-start | bytes 3145736 | tf_op jit(solution)/shard_map/ppermute | solution.py:213
  28.9 14.4 %collective-permute-start.3 = (bf16[512,512]{1,0:T(8,128)(2,1)S(1)}, bf16[512,512]{1,0:T(8,128)(2,1)}, u32[]{:S(2)}, u32[]{:S(2)}) collective-permute-start(bf16[512,512]{1,0:T(8,128)(2,1)S(1)} %collective-permute-done.rest_2_), channel_id=1, source_target_pairs={{0,4},{2,6},{4,0},{6,2},{8,12},{10,14},{12,8},{14,10},{1,5},{3,7},... | collective-permute-start | bytes 1572872 | tf_op jit(solution)/shard_map/ppermute | solution.py:184
  33.6 1.0 %copy-start.3 = (bf16[4,64,2048]{2,1,0:T(8,128)(2,1)}, bf16[4,64,2048]{2,1,0:T(8,128)(2,1)S(1)}, u32[]{:S(2)}) copy-start(bf16[4,64,2048]{2,1,0:T(8,128)(2,1)S(1)} %collective-permute-done.2.other) | copy-start | bytes 3145732
  34.6 1.0 %copy-start.5 = (f32[512,512]{1,0:T(8,128)}, f32[512,512]{1,0:T(8,128)S(1)}, u32[]{:S(2)}) copy-start(f32[512,512]{1,0:T(8,128)S(1)} %early_rows.1.early) | copy-start | bytes 3145732
  35.6 21.5 %all-to-all-start.1 = ((bf16[8,72,512]{2,1,0:T(8,128)(2,1)}), bf16[8,72,512]{2,1,0:T(8,128)(2,1)S(1)}, u32[]{:S(2)}, u32[]{:S(2)}) async-start(bf16[8,72,512]{2,1,0:T(8,128)(2,1)} %pick_panels.1), calls=%async_computation.1 | async-start | bytes 1179648 | tf_op jit(solution)/shard_map/all_to_all | solution.py:239
  40.9 2.4 %copy-start.4 = (bf16[4,64,2048]{2,1,0:T(8,128)(2,1)S(1)}, bf16[4,64,2048]{2,1,0:T(8,128)(2,1)}, u32[]{:S(2)}) copy-start(bf16[4,64,2048]{2,1,0:T(8,128)(2,1)} %copy-done.3) | copy-start | bytes 3145732
  41.0 2.4 %copy-start.6 = (f32[512,512]{1,0:T(8,128)S(1)}, f32[512,512]{1,0:T(8,128)}, u32[]{:S(2)}) copy-start(f32[512,512]{1,0:T(8,128)} %copy-done.5) | copy-start | bytes 3145732
  41.0 8.0 %copy-start.2 = (bf16[128,8192]{1,0:T(8,128)(2,1)S(1)}, bf16[128,8192]{1,0:T(8,128)(2,1)}, u32[]{:S(2)}) copy-start(bf16[128,8192]{1,0:T(8,128)(2,1)} %hidden.3) | copy-start | bytes 6291460
  41.0 8.0 %copy-start.8 = (bf16[8192]{0:T(1024)(128)(2,1)S(1)}, bf16[8192]{0:T(1024)(128)(2,1)}, u32[]{:S(2)}) copy-start(bf16[8192]{0:T(1024)(128)(2,1)} %gain.1) | copy-start | bytes 49156
  45.5 12.1 %collective-permute-start.4 = (bf16[128,512]{1,0:T(8,128)(2,1)}, bf16[128,512]{1,0:T(8,128)(2,1)S(1)}, u32[]{:S(2)}, u32[]{:S(2)}) collective-permute-start(bf16[128,512]{1,0:T(8,128)(2,1)} %get-tuple-element.42), channel_id=1, source_target_pairs={{0,18},{2,16},{4,22},{6,20},{8,26},{10,24},{12,30},{14,28},{16,2},... | collective-permute-start | bytes 393224 | tf_op jit(solution)/shard_map/ppermute | solution.py:178
  48.0 9.6 %collective-permute-start.5 = (bf16[128,512]{1,0:T(8,128)(2,1)}, bf16[128,512]{1,0:T(8,128)(2,1)S(1)}, u32[]{:S(2)}, u32[]{:S(2)}) collective-permute-start(bf16[128,512]{1,0:T(8,128)(2,1)} %get-tuple-element.43), channel_id=1, source_target_pairs={{0,2},{2,0},{4,6},{6,4},{8,10},{10,8},{12,14},{14,12},{16,18},{18,... | collective-permute-start | bytes 393224 | tf_op jit(solution)/shard_map/ppermute | solution.py:178
  48.5 9.1 %collective-permute-start.6 = (bf16[128,512]{1,0:T(8,128)(2,1)S(1)}, bf16[128,512]{1,0:T(8,128)(2,1)S(1)}, u32[]{:S(2)}, u32[]{:S(2)}) collective-permute-start(bf16[128,512]{1,0:T(8,128)(2,1)S(1)} %get-tuple-element.44), channel_id=1, source_target_pairs={{0,16},{2,18},{4,20},{6,22},{8,24},{10,26},{12,28},{14,30},{16,0},... | collective-permute-start | bytes 393224 | tf_op jit(solution)/shard_map/ppermute | solution.py:178
  57.6 1.3 %collective-permute-start.7 = (f32[128,64]{1,0:T(8,128)S(1)}, f32[128,64]{1,0:T(8,128)S(1)}, u32[]{:S(2)}, u32[]{:S(2)}) collective-permute-start(f32[128,64]{1,0:T(8,128)S(1)} %low_rank.1.low_mine), channel_id=1, source_target_pairs={{0,1},{1,0},{2,3},{3,2},{4,5},{5,4},{6,7},{7,6},{8,9},{9,8},{10,11... | collective-permute-start | bytes 98312 | tf_op jit(solution)/shard_map/ppermute | solution.py:245

commit v5 on v4

--- a/solution.py
+++ b/solution.py
@@ -15,8 +15,10 @@
 PEERS = ((1, 1), (1, 0), (0, 1))
 
 
-def params():
-    return pltpu.CompilerParams(vmem_limit_bytes=VMEM_LIMIT)
+def panel_order(peers):
+    planes = peers // 2
+    inner = [*range(planes // 2, -1, -1), *range(planes // 2 + 1, planes)]
+    return [2 * z + x for z in inner for x in range(2)]
 
 
 def gather_kernel(seg, slot_of, down, up, out, sem):
@@ -28,7 +30,7 @@
     col = lax.broadcasted_iota(jnp.int32, (2 * PAD_ROWS, up.shape[0]), 1)
     hot = jnp.zeros((2 * PAD_ROWS, up.shape[0]), jnp.float32)
     for k in range(peers):
-        slot = slot_of[seg[k]]
+        slot = slot_of[seg[panel_order(peers)[k]]]
         copy = pltpu.make_async_copy(down.at[slot], out.at[k, pl.ds(0, rank)], sem.at[k])
         copy.start()
         copies.append(copy)
@@ -93,7 +95,7 @@
 
 
 def early_kernel(mine, other, *rest):
-    weights, out = rest[:-1], rest[-1]
+    weights, out, last = rest[:-2], rest[-2], rest[-1]
     total = jnp.zeros(out.shape, jnp.float32)
     first = 0
     for w in weights:
@@ -101,12 +103,12 @@
         total += jnp.dot(x, w[...], preferred_element_type=jnp.float32)
         first += w.shape[0]
     out[...] = total
-
-
-def late_kernel(mine, other, weight, early, out0, out1, out2, own):
-    rows = mine.shape[1]
-    x = in_order(mine, other, slice(mine.shape[2] - weight.shape[0], mine.shape[2]))
-    total = early[...] + jnp.dot(x, weight[...], preferred_element_type=jnp.float32)
+    last[...] = in_order(mine, other, slice(first, mine.shape[2]))
+
+
+def late_kernel(last, weight, early, out0, out1, out2, own):
+    rows = own.shape[0] // 2
+    total = early[...] + jnp.dot(last[...], weight[...], preferred_element_type=jnp.float32)
     half = lax.axis_index("pool")
     for part in range(2):
         at = pl.ds(pl.multiple_of((half if part == 0 else 1 - half) * rows, rows), rows)
@@ -119,15 +121,16 @@
     rank = out.shape[1]
     feats = pieces.shape[2]
     total = jnp.zeros(out.shape, jnp.float32)
-    for k in range(pieces.shape[0]):
-        x = acts[:, k * feats : (k + 1) * feats]
+    for k, t in enumerate(panel_order(pieces.shape[0])):
+        x = acts[:, t * feats : (t + 1) * feats]
         total += lax.dot_general(x, pieces[k, :rank, :], (((1,), (1,)), ((), ())), preferred_element_type=jnp.float32)
     out[...] = total
 
 
 def final_kernel(up_rows, own, far0, far1, far2, low_mine, low_other, pieces, out):
     rank = low_mine.shape[1]
-    up = [pieces[k, rank : rank + PAD_ROWS, :].astype(jnp.float32)[:up_rows] for k in range(pieces.shape[0])]
+    order = panel_order(pieces.shape[0])
+    up = [pieces[order.index(t), rank : rank + up_rows, :].astype(jnp.float32) for t in range(len(order))]
     low = (low_mine[...] + low_other[...]).astype(jnp.bfloat16)
     up = jnp.concatenate(up, axis=0).astype(jnp.bfloat16)
     total = jnp.dot(low, up, preferred_element_type=jnp.float32) + own[...]
@@ -140,7 +143,7 @@
     return pl.BlockSpec(memory_space=pltpu.VMEM)
 
 
-def call(kernel, prefetch, args, in_specs, outs, out_specs, grid=(), scratch=(), alias=None, name=None, flops=0, nbytes=0):
+def call(kernel, prefetch, args, in_specs, outs, out_specs, grid=(), scratch=(), alias=None, limit=VMEM_LIMIT, name=None, flops=0, nbytes=0):
     return pl.pallas_call(
         kernel,
         grid_spec=pltpu.PrefetchScalarGridSpec(
@@ -151,7 +154,7 @@
             scratch_shapes=scratch,
         ),
         out_shape=outs,
-        compiler_params=params(),
+        compiler_params=pltpu.CompilerParams(vmem_limit_bytes=limit),
         input_output_aliases=alias or {},
         cost_estimate=pl.CostEstimate(flops=flops, bytes_accessed=nbytes, transcendentals=0),
         name=name,
@@ -212,17 +215,18 @@
     )
     others = [lax.ppermute(mine, "pool", cores)]
     weight = whole((chunk, cols))
-    early = call(
+    early, x_last = call(
         early_kernel, [], [mine, *others, own_w, first, second],
         [weight] * 5,
-        jax.ShapeDtypeStruct((4 * tokens, cols), f32), whole((4 * tokens, cols)),
+        [jax.ShapeDtypeStruct((4 * tokens, cols), f32), jax.ShapeDtypeStruct((4 * tokens, chunk), bf16)],
+        [weight] * 2,
         name="early_rows", flops=24 * tokens * chunk * cols, nbytes=4 << 20,
     )
     early, pieces = lax.optimization_barrier((early, pieces))
     tick, early, third = lax.optimization_barrier((tick, early, third))
     late = call(
-        late_kernel, [], [mine, *others, third, early],
-        [weight] * 4,
+        late_kernel, [], [x_last, third, early],
+        [weight] * 3,
         [jax.ShapeDtypeStruct((tokens, cols), bf16)] * 3 + [jax.ShapeDtypeStruct((tokens, cols), f32)],
         [whole((tokens, cols))] * 4,
         name="late_rows", flops=8 * tokens * chunk * cols, nbytes=4 << 20,
@@ -236,7 +240,9 @@
     )
     parts = [to_peer(x, *peer) for x, peer in zip(late[:3], PEERS)]
 
-    pieces = lax.all_to_all(pieces, "tensor", split_axis=0, concat_axis=0, tiled=True)
+    pieces = lax.all_to_all(
+        pieces, "tensor", split_axis=0, concat_axis=0, tiled=True, axis_index_groups=[panel_order(peers)]
+    )
     low_mine = call(
         rank_kernel, [], [acts, pieces], [whole(acts.shape), whole(piece_shape)],
         jax.ShapeDtypeStruct((tokens, rank), f32), whole((tokens, rank)),

time: 60.3 us -> 59.1 us (0.980)
  waiting for transfers between devices: 17.6 us -> 15.1 us
  starting transfers between devices: 19.8 us -> 21.3 us
    all_to_all x1, waiting for transfers between devices: 7.17 us -> 3.67 us  [square_device(): lax.all_to_all(pieces, 'tensor', split_axis=0, concat_axis=0, tiled=True,...]
    ppermute x3, waiting for transfers between devices: 0.01 us -> 2.29 us  [to_peer(): return lax.ppermute(x, ('groups', 'tensor'), pairs)]
    ppermute x1, waiting for transfers between devices: 1.21 us -> 0.01 us  [square_device(): low_other = lax.ppermute(low_mine, 'pool', cores)]
    ppermute x3, starting transfers between devices: 3.49 us -> 4.41 us  [to_peer(): return lax.ppermute(x, ('groups', 'tensor'), pairs)]
  transfers between devices with their start and end apart: 10 -> 10, of which waited for: 6 -> 7; matrix products, arithmetic and copies ran while one was open for 0% -> 0% of each run, Pallas kernels for 17% -> 17%
where the time goes in v5:
time: 59.1 us; the launch traced here: 58.6 us
  starting transfers between devices  21.3 us (36%)
  waiting for transfers between devices  15.1 us (26%)
  local copies, waits for them, and re-layouts  11.3 us (19%)
  Pallas kernels  10.8 us (18%)
    unnamed x28, local copies, waits for them, and re-layouts  11.3 us
    pallas_call x8, Pallas kernels, call(): pl.pallas_call(kernel, grid_spec=pltpu.PrefetchScalarGridSpec(num_scalar_...  10.8 us
    ppermute x3, waiting for transfers between devices, along_z(): return lax.ppermute(x, 'tensor', [(i, i ^ 2 * step) for i in range(peers)])  7.97 us
    ppermute x3, starting transfers between devices, along_z(): return lax.ppermute(x, 'tensor', [(i, i ^ 2 * step) for i in range(peers)])  7.17 us
    all_to_all x1, starting transfers between devices, square_device(): lax.all_to_all(pieces, 'tensor', split_axis=0, concat_axis=0, tiled=True,...  5.9 us
    ppermute x3, starting transfers between devices, to_peer(): return lax.ppermute(x, ('groups', 'tensor'), pairs)  4.41 us
    all_to_all x1, starting transfers between devices, square_device(): lax.all_to_all(send, ('groups', 'tensor'), split_axis=0, concat_axis=0, t...  3.73 us
    all_to_all x1, waiting for transfers between devices, square_device(): lax.all_to_all(pieces, 'tensor', split_axis=0, concat_axis=0, tiled=True,...  3.67 us
  transfers between devices with their start and end apart: 10, of which 7 were waited for; matrix products, arithmetic and copies ran while one was open for 0% of the time, Pallas kernels for 17%

profile of v5, /device:TPU:0, one launch (start us, length us, event | category | flops | bytes accessed | tf_op | source)
XLA Modules:
  0.0 58.6 jit_solution(1383404867100483342)
XLA Ops:
  0.0 1.2 %copy-done = bf16[1024,512]{1,0:T(8,128)(2,1)S(1)} copy-done((bf16[1024,512]{1,0:T(8,128)(2,1)S(1)}, bf16[1024,512]{1,0:T(8,128)(2,1)}, u32[]{:S(2)}) %copy-start) | copy-done | bytes 1048600
  1.3 4.1 %collective-permute-start = (bf16[512,512]{1,0:T(8,128)(2,1)S(1)}, bf16[512,512]{1,0:T(8,128)(2,1)S(1)}, u32[]{:S(2)}, u32[]{:S(2)}) collective-permute-start(bf16[512,512]{1,0:T(8,128)(2,1)S(1)} %constant_dynamic-slice_fusion.rest_0_), channel_id=1, source_target_pairs={{0,8},{2,10},{4,12},{6,14},{8,0},{10,2},{12,4},{14,6},{1,9},{3,11}... | collective-permute-start | bytes 1572872 | tf_op jit(solution)/shard_map/ppermute | solution.py:187
  5.4 1.6 %collective-permute-start.1 = (bf16[512,512]{1,0:T(8,128)(2,1)S(1)}, bf16[512,512]{1,0:T(8,128)(2,1)}, u32[]{:S(2)}, u32[]{:S(2)}) collective-permute-start(bf16[512,512]{1,0:T(8,128)(2,1)S(1)} %constant_dynamic-slice_fusion.rest_0_), channel_id=1, source_target_pairs={{0,4},{2,6},{4,0},{6,2},{8,12},{10,14},{12,8},{14,10},{1,5},{3,7},... | collective-permute-start | bytes 1572872 | tf_op jit(solution)/shard_map/ppermute | solution.py:187
  6.9 1.6 %copy-done.1 = bf16[128,8192]{1,0:T(8,128)(2,1)S(1)} copy-done((bf16[128,8192]{1,0:T(8,128)(2,1)S(1)}, bf16[128,8192]{1,0:T(8,128)(2,1)}, u32[]{:S(2)}) %copy-start.1) | copy-done | bytes 2097176
  8.5 0.7 %copy-done.7 = bf16[8192]{0:T(1024)(128)(2,1)S(1)} copy-done((bf16[8192]{0:T(1024)(128)(2,1)S(1)}, bf16[8192]{0:T(1024)(128)(2,1)}, u32[]{:S(2)}) %copy-start.7) | copy-done | bytes 16408
  9.3 1.9 %norm_send.1 = bf16[4,64,2048]{2,1,0:T(8,128)(2,1)} custom-call(bf16[128,8192]{1,0:T(8,128)(2,1)S(1)} %copy-done.1, bf16[8192]{0:T(1024)(128)(2,1)S(1)} %copy-done.7), custom_call_target="tpu_custom_call" | custom-call | flops 3145728 | bytes 2097152 | tf_op jit(solution)/shard_map/norm_send/pallas_call | solution.py:147
  11.2 3.7 %all-to-all-start = ((bf16[4,64,2048]{2,1,0:T(8,128)(2,1)}), bf16[4,64,2048]{2,1,0:T(8,128)(2,1)S(1)}, u32[]{:S(2)}, u32[]{:S(2)}) async-start(bf16[4,64,2048]{2,1,0:T(8,128)(2,1)} %norm_send.1), calls=%async_computation | async-start | bytes 2097152 | tf_op jit(solution)/shard_map/all_to_all | solution.py:198
  14.9 3.4 %copy-done.9 = bf16[128,1,512,64]{2,3,1,0:T(8,128)(2,1)S(1)} copy-done((bf16[128,1,512,64]{2,3,1,0:T(8,128)(2,1)S(1)}, bf16[128,1,512,64]{2,3,1,0:T(8,128)(2,1)}, u32[]{:S(2)}) %copy-start.9) | copy-done | bytes 8388632
  18.3 1.2 %copy-done.10 = bf16[128,1,4096]{2,0,1:T(8,128)(2,1)S(1)} copy-done((bf16[128,1,4096]{2,0,1:T(8,128)(2,1)S(1)}, bf16[128,1,4096]{2,0,1:T(8,128)(2,1)}, u32[]{:S(2)}) %copy-start.10) | copy-done | bytes 1048600
  19.5 0.7 %copy-done.11 = s32[8]{0:T(128)S(1)} copy-done((s32[8]{0:T(128)S(1)}, s32[8]{0:T(128)}, u32[]{:S(2)}) %copy-start.11) | copy-done | bytes 56
  20.2 0.7 %copy-done.12 = s32[128]{0:T(128)S(1)} copy-done((s32[128]{0:T(128)S(1)}, s32[128]{0:T(128)}, u32[]{:S(2)}) %copy-start.12) | copy-done | bytes 536
  20.8 2.5 %pick_panels.1 = bf16[8,72,512]{2,1,0:T(8,128)(2,1)} custom-call(s32[8]{0:T(128)S(1)} %copy-done.11, s32[128]{0:T(128)S(1)} %copy-done.12, bf16[128,64,512]{2,1,0:T(8,128)(2,1)S(1)} %bitcast.4, bf16[128,4096]{1,0:T(8,128)(2,1)S(1)} %bitcast.5), custom_call_target="tpu_custom_call" | custom-call | flops 68719476736 | bytes 3145728 | tf_op jit(solution)/shard_map/pick_panels/pallas_call | solution.py:147
  23.3 5.3 %collective-permute-done.rest_2_ = bf16[512,512]{1,0:T(8,128)(2,1)S(1)} collective-permute-done((bf16[512,512]{1,0:T(8,128)(2,1)S(1)}, bf16[512,512]{1,0:T(8,128)(2,1)S(1)}, u32[]{:S(2)}, u32[]{:S(2)}) %collective-permute-start) | collective-permute-done | bytes 524320 | tf_op jit(solution)/shard_map/ppermute | solution.py:187
  28.6 0.3 collective-permute-done.1.rest_1_
  28.9 1.5 %collective-permute-start.3 = (bf16[512,512]{1,0:T(8,128)(2,1)S(1)}, bf16[512,512]{1,0:T(8,128)(2,1)}, u32[]{:S(2)}, u32[]{:S(2)}) collective-permute-start(bf16[512,512]{1,0:T(8,128)(2,1)S(1)} %collective-permute-done.rest_2_), channel_id=1, source_target_pairs={{0,4},{2,6},{4,0},{6,2},{8,12},{10,14},{12,8},{14,10},{1,5},{3,7},... | collective-permute-start | bytes 1572872 | tf_op jit(solution)/shard_map/ppermute | solution.py:187
  30.4 1.2 %collective-permute-done.2.other = bf16[4,64,2048]{2,1,0:T(8,128)(2,1)S(1)} collective-permute-done((bf16[4,64,2048]{2,1,0:T(8,128)(2,1)S(1)}, bf16[4,64,2048]{2,1,0:T(8,128)(2,1)S(1)}, u32[]{:S(2)}, u32[]{:S(2)}) %collective-permute-start.2) | collective-permute-done | bytes 1048608 | tf_op jit(solution)/shard_map/ppermute | solution.py:216
  31.6 2.0 %early_rows.1 = (f32[512,512]{1,0:T(8,128)S(1)}, bf16[512,512]{1,0:T(8,128)(2,1)S(1)}) custom-call(bf16[4,64,2048]{2,1,0:T(8,128)(2,1)S(1)} %all-to-all-done.mine, bf16[4,64,2048]{2,1,0:T(8,128)(2,1)S(1)} %collective-permute-done.2.other, bf16[512,512]{1,0:T(8,128)(2,1)S(1)} %constant_dynamic-slice_fusion.rest_0_, ...), custom_call_target="tpu_custom_call" | custom-call | flops 805306368 | bytes 4194304 | tf_op jit(solution)/shard_map/early_rows/pallas_call | solution.py:147
  33.7 1.0 %copy-done.3 = f32[512,512]{1,0:T(8,128)} copy-done((f32[512,512]{1,0:T(8,128)}, f32[512,512]{1,0:T(8,128)S(1)}, u32[]{:S(2)}) %copy-start.3) | copy-done | bytes 1048600
  34.7 0.8 %copy-done.5 = bf16[512,512]{1,0:T(8,128)(2,1)} copy-done((bf16[512,512]{1,0:T(8,128)(2,1)}, bf16[512,512]{1,0:T(8,128)(2,1)S(1)}, u32[]{:S(2)}) %copy-start.5) | copy-done | bytes 524312
  35.5 5.9 %all-to-all-start.1 = ((bf16[8,72,512]{2,1,0:T(8,128)(2,1)}), bf16[8,72,512]{2,1,0:T(8,128)(2,1)S(1)}, u32[]{:S(2)}, u32[]{:S(2)}) async-start(bf16[8,72,512]{2,1,0:T(8,128)(2,1)} %pick_panels.1), calls=%async_computation.1 | async-start | bytes 1179648 | tf_op jit(solution)/shard_map/all_to_all | solution.py:243
  41.4 0.0 copy-start.2
  41.4 2.3 %collective-permute-done.3.weight = bf16[512,512]{1,0:T(8,128)(2,1)} collective-permute-done((bf16[512,512]{1,0:T(8,128)(2,1)S(1)}, bf16[512,512]{1,0:T(8,128)(2,1)}, u32[]{:S(2)}, u32[]{:S(2)}) %collective-permute-start.3) | collective-permute-done | bytes 524320 | tf_op jit(solution)/shard_map/ppermute | solution.py:187
  43.8 2.1 %late_rows.1 = (bf16[128,512]{1,0:T(8,128)(2,1)}, bf16[128,512]{1,0:T(8,128)(2,1)}, bf16[128,512]{1,0:T(8,128)(2,1)S(1)}, f32[128,512]{1,0:T(8,128)S(1)}) custom-call(bf16[512,512]{1,0:T(8,128)(2,1)S(1)} %copy-done.6, bf16[512,512]{1,0:T(8,128)(2,1)} %collective-permute-done.3.weight, f32[512,512]{1,0:T(8,128)S(1)} %copy-done.4), custom_call_target="tpu_custom_call" | custom-call | flops 268435456 | bytes 4194304 | tf_op jit(solution)/shard_map/late_rows/pallas_call | solution.py:147
  45.9 3.8 %collective-permute-start.4 = (bf16[128,512]{1,0:T(8,128)(2,1)}, bf16[128,512]{1,0:T(8,128)(2,1)S(1)}, u32[]{:S(2)}, u32[]{:S(2)}) collective-permute-start(bf16[128,512]{1,0:T(8,128)(2,1)} %get-tuple-element.46), channel_id=1, source_target_pairs={{0,18},{2,16},{4,22},{6,20},{8,26},{10,24},{12,30},{14,28},{16,2},... | collective-permute-start | bytes 393224 | tf_op jit(solution)/shard_map/ppermute | solution.py:181
  49.7 0.6 collective-permute-start.6
  50.3 0.9 %norm_half.1.acts = bf16[128,4096]{1,0:T(8,128)(2,1)S(1)} custom-call(s32[128]{0:T(128)S(1)} %tick.1.token, bf16[128,8192]{1,0:T(8,128)(2,1)S(1)} %copy-done.2, bf16[8192]{0:T(1024)(128)(2,1)S(1)} %copy-done.8), custom_call_target="tpu_custom_call" | custom-call | flops 6291456 | bytes 4194304 | tf_op jit(solution)/shard_map/norm_half/pallas_call | solution.py:147
  51.3 3.7 %all-to-all-done.1.pieces = bf16[8,72,512]{2,1,0:T(8,128)(2,1)S(1)} async-done(((bf16[8,72,512]{2,1,0:T(8,128)(2,1)}), bf16[8,72,512]{2,1,0:T(8,128)(2,1)S(1)}, u32[]{:S(2)}, u32[]{:S(2)}) %all-to-all-start.1) | async-done | bytes 589856 | tf_op jit(solution)/shard_map/all_to_all | solution.py:243
  54.9 0.4 low_rank.1.low_mine
  55.3 0.1 collective-permute-start.7
  55.4 0.6 %collective-permute-done.4.far0 = bf16[128,512]{1,0:T(8,128)(2,1)S(1)} collective-permute-done((bf16[128,512]{1,0:T(8,128)(2,1)}, bf16[128,512]{1,0:T(8,128)(2,1)S(1)}, u32[]{:S(2)}, u32[]{:S(2)}) %collective-permute-start.4) | collective-permute-done | bytes 131104 | tf_op jit(solution)/shard_map/ppermute | solution.py:181
  56.0 1.7 %collective-permute-done.5.far1 = bf16[128,512]{1,0:T(8,128)(2,1)S(1)} collective-permute-done((bf16[128,512]{1,0:T(8,128)(2,1)}, bf16[128,512]{1,0:T(8,128)(2,1)S(1)}, u32[]{:S(2)}, u32[]{:S(2)}) %collective-permute-start.5) | collective-permute-done | bytes 131104 | tf_op jit(solution)/shard_map/ppermute | solution.py:181
  57.7 0.9 %final.1 = bf16[128,512]{1,0:T(8,128)(2,1)} custom-call(f32[128,512]{1,0:T(8,128)S(1)} %get-tuple-element.45.own, bf16[128,512]{1,0:T(8,128)(2,1)S(1)} %collective-permute-done.4.far0, bf16[128,512]{1,0:T(8,128)(2,1)S(1)} %collective-permute-done.5.far1, bf16[128,512]{1,0:T(8,128)(2,1)S(1)} %collective-permute-done.6.far2, f32[128,64]{1,0:T(8,128)S(1)} %low_rank.1.low_mine, ...), custom_call_target="tpu_custom_call" | custom-call | flops 16777216 | bytes 3145728 | tf_op jit(solution)/shard_map/final/pallas_call | solution.py:147
  (25 shorter events, 0.1 us)
Async XLA Ops:
  0.0 1.2 %copy-start = (bf16[1024,512]{1,0:T(8,128)(2,1)S(1)}, bf16[1024,512]{1,0:T(8,128)(2,1)}, u32[]{:S(2)}) copy-start(bf16[1024,512]{1,0:T(8,128)(2,1)} %param.9) | copy-start | bytes 3145732
  1.3 27.4 %collective-permute-start = (bf16[512,512]{1,0:T(8,128)(2,1)S(1)}, bf16[512,512]{1,0:T(8,128)(2,1)S(1)}, u32[]{:S(2)}, u32[]{:S(2)}) collective-permute-start(bf16[512,512]{1,0:T(8,128)(2,1)S(1)} %constant_dynamic-slice_fusion.rest_0_), channel_id=1, source_target_pairs={{0,8},{2,10},{4,12},{6,14},{8,0},{10,2},{12,4},{14,6},{1,9},{3,11}... | collective-permute-start | bytes 1572872 | tf_op jit(solution)/shard_map/ppermute | solution.py:187
  5.4 23.6 %collective-permute-start.1 = (bf16[512,512]{1,0:T(8,128)(2,1)S(1)}, bf16[512,512]{1,0:T(8,128)(2,1)}, u32[]{:S(2)}, u32[]{:S(2)}) collective-permute-start(bf16[512,512]{1,0:T(8,128)(2,1)S(1)} %constant_dynamic-slice_fusion.rest_0_), channel_id=1, source_target_pairs={{0,4},{2,6},{4,0},{6,2},{8,12},{10,14},{12,8},{14,10},{1,5},{3,7},... | collective-permute-start | bytes 1572872 | tf_op jit(solution)/shard_map/ppermute | solution.py:187
  6.9 1.6 %copy-start.1 = (bf16[128,8192]{1,0:T(8,128)(2,1)S(1)}, bf16[128,8192]{1,0:T(8,128)(2,1)}, u32[]{:S(2)}) copy-start(bf16[128,8192]{1,0:T(8,128)(2,1)} %hidden.3) | copy-start | bytes 6291460
  8.5 0.7 %copy-start.7 = (bf16[8192]{0:T(1024)(128)(2,1)S(1)}, bf16[8192]{0:T(1024)(128)(2,1)}, u32[]{:S(2)}) copy-start(bf16[8192]{0:T(1024)(128)(2,1)} %gain.1) | copy-start | bytes 49156
  11.2 17.7 %all-to-all-start = ((bf16[4,64,2048]{2,1,0:T(8,128)(2,1)}), bf16[4,64,2048]{2,1,0:T(8,128)(2,1)S(1)}, u32[]{:S(2)}, u32[]{:S(2)}) async-start(bf16[4,64,2048]{2,1,0:T(8,128)(2,1)} %norm_send.1), calls=%async_computation | async-start | bytes 2097152 | tf_op jit(solution)/shard_map/all_to_all | solution.py:198
  14.9 3.4 %copy-start.9 = (bf16[128,1,512,64]{2,3,1,0:T(8,128)(2,1)S(1)}, bf16[128,1,512,64]{2,3,1,0:T(8,128)(2,1)}, u32[]{:S(2)}) copy-start(bf16[128,1,512,64]{2,3,1,0:T(8,128)(2,1)} %param.10) | copy-start | bytes 25165828
  18.3 1.2 %copy-start.10 = (bf16[128,1,4096]{2,0,1:T(8,128)(2,1)S(1)}, bf16[128,1,4096]{2,0,1:T(8,128)(2,1)}, u32[]{:S(2)}) copy-start(bf16[128,1,4096]{2,0,1:T(8,128)(2,1)} %param.11) | copy-start | bytes 3145732
  19.5 0.7 %copy-start.11 = (s32[8]{0:T(128)S(1)}, s32[8]{0:T(128)}, u32[]{:S(2)}) copy-start(s32[8]{0:T(128)} %seg.1) | copy-start | bytes 100
  20.2 0.7 %copy-start.12 = (s32[128]{0:T(128)S(1)}, s32[128]{0:T(128)}, u32[]{:S(2)}) copy-start(s32[128]{0:T(128)} %token_) | copy-start | bytes 1540
  20.8 20.5 %copy-start.13 = (s32[128]{0:T(128)S(1)}, s32[128]{0:T(128)}, u32[]{:S(2)}) copy-start(s32[128]{0:T(128)} %token_) | copy-start | bytes 1540
  28.9 2.7 %collective-permute-start.2 = (bf16[4,64,2048]{2,1,0:T(8,128)(2,1)S(1)}, bf16[4,64,2048]{2,1,0:T(8,128)(2,1)S(1)}, u32[]{:S(2)}, u32[]{:S(2)}) collective-permute-start(bf16[4,64,2048]{2,1,0:T(8,128)(2,1)S(1)} %all-to-all-done.mine), channel_id=1, source_target_pairs={{0,1},{1,0},{2,3},{3,2},{4,5},{5,4},{6,7},{7,6},{8,9},{9,8},{10,11... | collective-permute-start | bytes 3145736 | tf_op jit(solution)/shard_map/ppermute | solution.py:216
  28.9 14.8 %collective-permute-start.3 = (bf16[512,512]{1,0:T(8,128)(2,1)S(1)}, bf16[512,512]{1,0:T(8,128)(2,1)}, u32[]{:S(2)}, u32[]{:S(2)}) collective-permute-start(bf16[512,512]{1,0:T(8,128)(2,1)S(1)} %collective-permute-done.rest_2_), channel_id=1, source_target_pairs={{0,4},{2,6},{4,0},{6,2},{8,12},{10,14},{12,8},{14,10},{1,5},{3,7},... | collective-permute-start | bytes 1572872 | tf_op jit(solution)/shard_map/ppermute | solution.py:187
  33.6 1.0 %copy-start.3 = (f32[512,512]{1,0:T(8,128)}, f32[512,512]{1,0:T(8,128)S(1)}, u32[]{:S(2)}) copy-start(f32[512,512]{1,0:T(8,128)S(1)} %get-tuple-element.39.early) | copy-start | bytes 3145732
  34.7 0.8 %copy-start.5 = (bf16[512,512]{1,0:T(8,128)(2,1)}, bf16[512,512]{1,0:T(8,128)(2,1)S(1)}, u32[]{:S(2)}) copy-start(bf16[512,512]{1,0:T(8,128)(2,1)S(1)} %get-tuple-element.33.last) | copy-start | bytes 1572868
  35.5 19.5 %all-to-all-start.1 = ((bf16[8,72,512]{2,1,0:T(8,128)(2,1)}), bf16[8,72,512]{2,1,0:T(8,128)(2,1)S(1)}, u32[]{:S(2)}, u32[]{:S(2)}) async-start(bf16[8,72,512]{2,1,0:T(8,128)(2,1)} %pick_panels.1), calls=%async_computation.1 | async-start | bytes 1179648 | tf_op jit(solution)/shard_map/all_to_all | solution.py:243
  41.4 2.4 %copy-start.4 = (f32[512,512]{1,0:T(8,128)S(1)}, f32[512,512]{1,0:T(8,128)}, u32[]{:S(2)}) copy-start(f32[512,512]{1,0:T(8,128)} %copy-done.3) | copy-start | bytes 3145732
  41.4 2.4 %copy-start.6 = (bf16[512,512]{1,0:T(8,128)(2,1)S(1)}, bf16[512,512]{1,0:T(8,128)(2,1)}, u32[]{:S(2)}) copy-start(bf16[512,512]{1,0:T(8,128)(2,1)} %copy-done.5) | copy-start | bytes 1572868
  41.4 8.9 %copy-start.2 = (bf16[128,8192]{1,0:T(8,128)(2,1)S(1)}, bf16[128,8192]{1,0:T(8,128)(2,1)}, u32[]{:S(2)}) copy-start(bf16[128,8192]{1,0:T(8,128)(2,1)} %hidden.3) | copy-start | bytes 6291460
  41.4 8.9 %copy-start.8 = (bf16[8192]{0:T(1024)(128)(2,1)S(1)}, bf16[8192]{0:T(1024)(128)(2,1)}, u32[]{:S(2)}) copy-start(bf16[8192]{0:T(1024)(128)(2,1)} %gain.1) | copy-start | bytes 49156
  45.9 10.2 %collective-permute-start.4 = (bf16[128,512]{1,0:T(8,128)(2,1)}, bf16[128,512]{1,0:T(8,128)(2,1)S(1)}, u32[]{:S(2)}, u32[]{:S(2)}) collective-permute-start(bf16[128,512]{1,0:T(8,128)(2,1)} %get-tuple-element.46), channel_id=1, source_target_pairs={{0,18},{2,16},{4,22},{6,20},{8,26},{10,24},{12,30},{14,28},{16,2},... | collective-permute-start | bytes 393224 | tf_op jit(solution)/shard_map/ppermute | solution.py:181
  49.7 8.0 %collective-permute-start.5 = (bf16[128,512]{1,0:T(8,128)(2,1)}, bf16[128,512]{1,0:T(8,128)(2,1)S(1)}, u32[]{:S(2)}, u32[]{:S(2)}) collective-permute-start(bf16[128,512]{1,0:T(8,128)(2,1)} %get-tuple-element.47), channel_id=1, source_target_pairs={{0,2},{2,0},{4,6},{6,4},{8,10},{10,8},{12,14},{14,12},{16,18},{18,... | collective-permute-start | bytes 393224 | tf_op jit(solution)/shard_map/ppermute | solution.py:181
  49.7 8.0 %collective-permute-start.6 = (bf16[128,512]{1,0:T(8,128)(2,1)S(1)}, bf16[128,512]{1,0:T(8,128)(2,1)S(1)}, u32[]{:S(2)}, u32[]{:S(2)}) collective-permute-start(bf16[128,512]{1,0:T(8,128)(2,1)S(1)} %get-tuple-element.48), channel_id=1, source_target_pairs={{0,16},{2,18},{4,20},{6,22},{8,24},{10,26},{12,28},{14,30},{16,0},... | collective-permute-start | bytes 393224 | tf_op jit(solution)/shard_map/ppermute | solution.py:181
  55.3 2.4 %collective-permute-start.7 = (f32[128,64]{1,0:T(8,128)S(1)}, f32[128,64]{1,0:T(8,128)S(1)}, u32[]{:S(2)}, u32[]{:S(2)}) collective-permute-start(f32[128,64]{1,0:T(8,128)S(1)} %low_rank.1.low_mine), channel_id=1, source_target_pairs={{0,1},{1,0},{2,3},{3,2},{4,5},{5,4},{6,7},{7,6},{8,9},{9,8},{10,11... | collective-permute-start | bytes 98312 | tf_op jit(solution)/shard_map/ppermute | solution.py:251

commit v6 on v5

--- a/solution.py
+++ b/solution.py
@@ -18,7 +18,7 @@
 def panel_order(peers):
     planes = peers // 2
     inner = [*range(planes // 2, -1, -1), *range(planes // 2 + 1, planes)]
-    return [2 * z + x for z in inner for x in range(2)]
+    return [2 * z + x for z in inner for x in (1, 0)]
 
 
 def gather_kernel(seg, slot_of, down, up, out, sem):
@@ -30,7 +30,7 @@
     col = lax.broadcasted_iota(jnp.int32, (2 * PAD_ROWS, up.shape[0]), 1)
     hot = jnp.zeros((2 * PAD_ROWS, up.shape[0]), jnp.float32)
     for k in range(peers):
-        slot = slot_of[seg[panel_order(peers)[k]]]
+        slot = slot_of[seg[panel_order(peers)[k] ^ lax.axis_index("pool")]]
         copy = pltpu.make_async_copy(down.at[slot], out.at[k, pl.ds(0, rank)], sem.at[k])
         copy.start()
         copies.append(copy)
@@ -122,18 +122,19 @@
     feats = pieces.shape[2]
     total = jnp.zeros(out.shape, jnp.float32)
     for k, t in enumerate(panel_order(pieces.shape[0])):
-        x = acts[:, t * feats : (t + 1) * feats]
+        first = (t ^ lax.axis_index("pool")) * feats
+        x = acts[:, pl.ds(pl.multiple_of(first, feats), feats)]
         total += lax.dot_general(x, pieces[k, :rank, :], (((1,), (1,)), ((), ())), preferred_element_type=jnp.float32)
     out[...] = total
 
 
-def final_kernel(up_rows, own, far0, far1, far2, low_mine, low_other, pieces, out):
+def final_kernel(up_rows, own, far0, far1, far2, low_mine, low_other, pieces, out, up):
     rank = low_mine.shape[1]
-    order = panel_order(pieces.shape[0])
-    up = [pieces[order.index(t), rank : rank + up_rows, :].astype(jnp.float32) for t in range(len(order))]
+    for k, t in enumerate(panel_order(pieces.shape[0])):
+        first = (t ^ lax.axis_index("pool")) * up_rows
+        up[pl.ds(pl.multiple_of(first, up_rows), up_rows), :] = pieces[k, rank:, :].astype(jnp.float32)
     low = (low_mine[...] + low_other[...]).astype(jnp.bfloat16)
-    up = jnp.concatenate(up, axis=0).astype(jnp.bfloat16)
-    total = jnp.dot(low, up, preferred_element_type=jnp.float32) + own[...]
+    total = jnp.dot(low, up[...].astype(jnp.bfloat16), preferred_element_type=jnp.float32) + own[...]
     for part in (far0, far1, far2):
         total += part[...].astype(jnp.float32)
     out[...] = total.astype(jnp.bfloat16)
@@ -240,8 +241,13 @@
     )
     parts = [to_peer(x, *peer) for x, peer in zip(late[:3], PEERS)]
 
+    panel_groups = [
+        [(a * peers + (k ^ core)) * 2 + core for k in panel_order(peers)]
+        for a in range(groups)
+        for core in range(2)
+    ]
     pieces = lax.all_to_all(
-        pieces, "tensor", split_axis=0, concat_axis=0, tiled=True, axis_index_groups=[panel_order(peers)]
+        pieces, ("groups", "tensor", "pool"), split_axis=0, concat_axis=0, tiled=True, axis_index_groups=panel_groups
     )
     low_mine = call(
         rank_kernel, [], [acts, pieces], [whole(acts.shape), whole(piece_shape)],
@@ -254,7 +260,7 @@
         [late[3], *parts, low_mine, low_other, pieces],
         [whole((tokens, cols))] * 4 + [whole((tokens, rank))] * 2 + [whole(piece_shape)],
         jax.ShapeDtypeStruct((tokens, cols), bf16), whole((tokens, cols)),
-        name="final", flops=4 * tokens * rank * cols, nbytes=3 << 20,
+        scratch=[pltpu.VMEM((rank, cols), f32)], name="final", flops=4 * tokens * rank * cols, nbytes=3 << 20,
     )
 
 

time: 59.1 us -> 58.1 us (0.983)
  starting transfers between devices: 21.3 us -> 20.7 us
    ppermute x3, waiting for transfers between devices: 2.29 us -> 0.76 us  [to_peer(): return lax.ppermute(x, ('groups', 'tensor'), pairs)]
    all_to_all x1, waiting for transfers between devices: 3.67 us -> 4.27 us  [square_device(): lax.all_to_all(pieces, ('groups', 'tensor', 'pool'), split_axis=0, concat...]
where the time goes in v6:
time: 58.1 us; the launch traced here: 57.6 us
  starting transfers between devices  20.7 us (36%)
  waiting for transfers between devices  14.6 us (25%)
  local copies, waits for them, and re-layouts  11.3 us (19%)
  Pallas kernels  10.8 us (19%)
    unnamed x28, local copies, waits for them, and re-layouts  11.3 us
    pallas_call x8, Pallas kernels, call(): pl.pallas_call(kernel, grid_spec=pltpu.PrefetchScalarGridSpec(num_scalar_...  10.8 us
    ppermute x3, waiting for transfers between devices, along_z(): return lax.ppermute(x, 'tensor', [(i, i ^ 2 * step) for i in range(peers)])  7.96 us
    ppermute x3, starting transfers between devices, along_z(): return lax.ppermute(x, 'tensor', [(i, i ^ 2 * step) for i in range(peers)])  7.17 us
    all_to_all x1, starting transfers between devices, square_device(): lax.all_to_all(pieces, ('groups', 'tensor', 'pool'), split_axis=0, concat...  5.9 us
    all_to_all x1, waiting for transfers between devices, square_device(): lax.all_to_all(pieces, ('groups', 'tensor', 'pool'), split_axis=0, concat...  4.27 us
    ppermute x3, starting transfers between devices, to_peer(): return lax.ppermute(x, ('groups', 'tensor'), pairs)  3.85 us
    all_to_all x1, starting transfers between devices, square_device(): lax.all_to_all(send, ('groups', 'tensor'), split_axis=0, concat_axis=0, t...  3.73 us
  transfers between devices with their start and end apart: 10, of which 7 were waited for; matrix products, arithmetic and copies ran while one was open for 0% of the time, Pallas kernels for 17%

profile of v6, /device:TPU:0, one launch (start us, length us, event | category | flops | bytes accessed | tf_op | source)
XLA Modules:
  0.0 57.6 jit_solution(13859877944305543192)
XLA Ops:
  0.0 1.2 %copy-done = bf16[1024,512]{1,0:T(8,128)(2,1)S(1)} copy-done((bf16[1024,512]{1,0:T(8,128)(2,1)S(1)}, bf16[1024,512]{1,0:T(8,128)(2,1)}, u32[]{:S(2)}) %copy-start) | copy-done | bytes 1048600
  1.3 4.1 %collective-permute-start = (bf16[512,512]{1,0:T(8,128)(2,1)S(1)}, bf16[512,512]{1,0:T(8,128)(2,1)S(1)}, u32[]{:S(2)}, u32[]{:S(2)}) collective-permute-start(bf16[512,512]{1,0:T(8,128)(2,1)S(1)} %constant_dynamic-slice_fusion.rest_0_), channel_id=1, source_target_pairs={{0,8},{2,10},{4,12},{6,14},{8,0},{10,2},{12,4},{14,6},{1,9},{3,11}... | collective-permute-start | bytes 1572872 | tf_op jit(solution)/shard_map/ppermute | solution.py:188
  5.4 1.6 %collective-permute-start.1 = (bf16[512,512]{1,0:T(8,128)(2,1)S(1)}, bf16[512,512]{1,0:T(8,128)(2,1)}, u32[]{:S(2)}, u32[]{:S(2)}) collective-permute-start(bf16[512,512]{1,0:T(8,128)(2,1)S(1)} %constant_dynamic-slice_fusion.rest_0_), channel_id=1, source_target_pairs={{0,4},{2,6},{4,0},{6,2},{8,12},{10,14},{12,8},{14,10},{1,5},{3,7},... | collective-permute-start | bytes 1572872 | tf_op jit(solution)/shard_map/ppermute | solution.py:188
  6.9 1.6 %copy-done.1 = bf16[128,8192]{1,0:T(8,128)(2,1)S(1)} copy-done((bf16[128,8192]{1,0:T(8,128)(2,1)S(1)}, bf16[128,8192]{1,0:T(8,128)(2,1)}, u32[]{:S(2)}) %copy-start.1) | copy-done | bytes 2097176
  8.5 0.7 %copy-done.7 = bf16[8192]{0:T(1024)(128)(2,1)S(1)} copy-done((bf16[8192]{0:T(1024)(128)(2,1)S(1)}, bf16[8192]{0:T(1024)(128)(2,1)}, u32[]{:S(2)}) %copy-start.7) | copy-done | bytes 16408
  9.3 1.9 %norm_send.1 = bf16[4,64,2048]{2,1,0:T(8,128)(2,1)} custom-call(bf16[128,8192]{1,0:T(8,128)(2,1)S(1)} %copy-done.1, bf16[8192]{0:T(1024)(128)(2,1)S(1)} %copy-done.7), custom_call_target="tpu_custom_call" | custom-call | flops 3145728 | bytes 2097152 | tf_op jit(solution)/shard_map/norm_send/pallas_call | solution.py:148
  11.2 3.7 %all-to-all-start = ((bf16[4,64,2048]{2,1,0:T(8,128)(2,1)}), bf16[4,64,2048]{2,1,0:T(8,128)(2,1)S(1)}, u32[]{:S(2)}, u32[]{:S(2)}) async-start(bf16[4,64,2048]{2,1,0:T(8,128)(2,1)} %norm_send.1), calls=%async_computation | async-start | bytes 2097152 | tf_op jit(solution)/shard_map/all_to_all | solution.py:199
  14.9 3.4 %copy-done.9 = bf16[128,1,512,64]{2,3,1,0:T(8,128)(2,1)S(1)} copy-done((bf16[128,1,512,64]{2,3,1,0:T(8,128)(2,1)S(1)}, bf16[128,1,512,64]{2,3,1,0:T(8,128)(2,1)}, u32[]{:S(2)}) %copy-start.9) | copy-done | bytes 8388632
  18.3 1.2 %copy-done.10 = bf16[128,1,4096]{2,0,1:T(8,128)(2,1)S(1)} copy-done((bf16[128,1,4096]{2,0,1:T(8,128)(2,1)S(1)}, bf16[128,1,4096]{2,0,1:T(8,128)(2,1)}, u32[]{:S(2)}) %copy-start.10) | copy-done | bytes 1048600
  19.5 0.7 %copy-done.11 = s32[8]{0:T(128)S(1)} copy-done((s32[8]{0:T(128)S(1)}, s32[8]{0:T(128)}, u32[]{:S(2)}) %copy-start.11) | copy-done | bytes 56
  20.2 0.7 %copy-done.12 = s32[128]{0:T(128)S(1)} copy-done((s32[128]{0:T(128)S(1)}, s32[128]{0:T(128)}, u32[]{:S(2)}) %copy-start.12) | copy-done | bytes 536
  20.8 2.5 %pick_panels.1 = bf16[8,72,512]{2,1,0:T(8,128)(2,1)} custom-call(s32[8]{0:T(128)S(1)} %copy-done.11, s32[128]{0:T(128)S(1)} %copy-done.12, bf16[128,64,512]{2,1,0:T(8,128)(2,1)S(1)} %bitcast.4, bf16[128,4096]{1,0:T(8,128)(2,1)S(1)} %bitcast.5), custom_call_target="tpu_custom_call" | custom-call | flops 68719476736 | bytes 3145728 | tf_op jit(solution)/shard_map/pick_panels/pallas_call | solution.py:148
  23.3 5.3 %collective-permute-done.rest_2_ = bf16[512,512]{1,0:T(8,128)(2,1)S(1)} collective-permute-done((bf16[512,512]{1,0:T(8,128)(2,1)S(1)}, bf16[512,512]{1,0:T(8,128)(2,1)S(1)}, u32[]{:S(2)}, u32[]{:S(2)}) %collective-permute-start) | collective-permute-done | bytes 524320 | tf_op jit(solution)/shard_map/ppermute | solution.py:188
  28.6 0.3 collective-permute-done.1.rest_1_
  28.9 1.5 %collective-permute-start.3 = (bf16[512,512]{1,0:T(8,128)(2,1)S(1)}, bf16[512,512]{1,0:T(8,128)(2,1)}, u32[]{:S(2)}, u32[]{:S(2)}) collective-permute-start(bf16[512,512]{1,0:T(8,128)(2,1)S(1)} %collective-permute-done.rest_2_), channel_id=1, source_target_pairs={{0,4},{2,6},{4,0},{6,2},{8,12},{10,14},{12,8},{14,10},{1,5},{3,7},... | collective-permute-start | bytes 1572872 | tf_op jit(solution)/shard_map/ppermute | solution.py:188
  30.4 1.2 %collective-permute-done.2.other = bf16[4,64,2048]{2,1,0:T(8,128)(2,1)S(1)} collective-permute-done((bf16[4,64,2048]{2,1,0:T(8,128)(2,1)S(1)}, bf16[4,64,2048]{2,1,0:T(8,128)(2,1)S(1)}, u32[]{:S(2)}, u32[]{:S(2)}) %collective-permute-start.2) | collective-permute-done | bytes 1048608 | tf_op jit(solution)/shard_map/ppermute | solution.py:217
  31.6 2.0 %early_rows.1 = (f32[512,512]{1,0:T(8,128)S(1)}, bf16[512,512]{1,0:T(8,128)(2,1)S(1)}) custom-call(bf16[4,64,2048]{2,1,0:T(8,128)(2,1)S(1)} %all-to-all-done.mine, bf16[4,64,2048]{2,1,0:T(8,128)(2,1)S(1)} %collective-permute-done.2.other, bf16[512,512]{1,0:T(8,128)(2,1)S(1)} %constant_dynamic-slice_fusion.rest_0_, ...), custom_call_target="tpu_custom_call" | custom-call | flops 805306368 | bytes 4194304 | tf_op jit(solution)/shard_map/early_rows/pallas_call | solution.py:148
  33.7 1.0 %copy-done.3 = f32[512,512]{1,0:T(8,128)} copy-done((f32[512,512]{1,0:T(8,128)}, f32[512,512]{1,0:T(8,128)S(1)}, u32[]{:S(2)}) %copy-start.3) | copy-done | bytes 1048600
  34.7 0.8 %copy-done.5 = bf16[512,512]{1,0:T(8,128)(2,1)} copy-done((bf16[512,512]{1,0:T(8,128)(2,1)}, bf16[512,512]{1,0:T(8,128)(2,1)S(1)}, u32[]{:S(2)}) %copy-start.5) | copy-done | bytes 524312
  35.5 5.9 %all-to-all-start.1 = ((bf16[8,72,512]{2,1,0:T(8,128)(2,1)}), bf16[8,72,512]{2,1,0:T(8,128)(2,1)S(1)}, u32[]{:S(2)}, u32[]{:S(2)}) async-start(bf16[8,72,512]{2,1,0:T(8,128)(2,1)} %pick_panels.1), calls=%async_computation.1 | async-start | bytes 1179648 | tf_op jit(solution)/shard_map/all_to_all | solution.py:249
  41.4 0.0 copy-start.2
  41.4 2.3 %collective-permute-done.3.weight = bf16[512,512]{1,0:T(8,128)(2,1)} collective-permute-done((bf16[512,512]{1,0:T(8,128)(2,1)S(1)}, bf16[512,512]{1,0:T(8,128)(2,1)}, u32[]{:S(2)}, u32[]{:S(2)}) %collective-permute-start.3) | collective-permute-done | bytes 524320 | tf_op jit(solution)/shard_map/ppermute | solution.py:188
  43.8 2.1 %late_rows.1 = (bf16[128,512]{1,0:T(8,128)(2,1)}, bf16[128,512]{1,0:T(8,128)(2,1)}, bf16[128,512]{1,0:T(8,128)(2,1)S(1)}, f32[128,512]{1,0:T(8,128)S(1)}) custom-call(bf16[512,512]{1,0:T(8,128)(2,1)S(1)} %copy-done.6, bf16[512,512]{1,0:T(8,128)(2,1)} %collective-permute-done.3.weight, f32[512,512]{1,0:T(8,128)S(1)} %copy-done.4), custom_call_target="tpu_custom_call" | custom-call | flops 268435456 | bytes 4194304 | tf_op jit(solution)/shard_map/late_rows/pallas_call | solution.py:148
  45.9 3.3 %collective-permute-start.4 = (bf16[128,512]{1,0:T(8,128)(2,1)}, bf16[128,512]{1,0:T(8,128)(2,1)S(1)}, u32[]{:S(2)}, u32[]{:S(2)}) collective-permute-start(bf16[128,512]{1,0:T(8,128)(2,1)} %get-tuple-element.46), channel_id=1, source_target_pairs={{0,18},{2,16},{4,22},{6,20},{8,26},{10,24},{12,30},{14,28},{16,2},... | collective-permute-start | bytes 393224 | tf_op jit(solution)/shard_map/ppermute | solution.py:182
  49.2 0.6 collective-permute-start.6
  49.7 0.9 %norm_half.1.acts = bf16[128,4096]{1,0:T(8,128)(2,1)S(1)} custom-call(s32[128]{0:T(128)S(1)} %tick.1.token, bf16[128,8192]{1,0:T(8,128)(2,1)S(1)} %copy-done.2, bf16[8192]{0:T(1024)(128)(2,1)S(1)} %copy-done.8), custom_call_target="tpu_custom_call" | custom-call | flops 6291456 | bytes 4194304 | tf_op jit(solution)/shard_map/norm_half/pallas_call | solution.py:148
  50.7 4.3 %all-to-all-done.1.pieces = bf16[8,72,512]{2,1,0:T(8,128)(2,1)S(1)} async-done(((bf16[8,72,512]{2,1,0:T(8,128)(2,1)}), bf16[8,72,512]{2,1,0:T(8,128)(2,1)S(1)}, u32[]{:S(2)}, u32[]{:S(2)}) %all-to-all-start.1) | async-done | bytes 589856 | tf_op jit(solution)/shard_map/all_to_all | solution.py:249
  55.0 0.4 low_rank.1.low_mine
  55.4 0.1 collective-permute-start.7
  55.5 0.8 %collective-permute-done.5.far1 = bf16[128,512]{1,0:T(8,128)(2,1)S(1)} collective-permute-done((bf16[128,512]{1,0:T(8,128)(2,1)}, bf16[128,512]{1,0:T(8,128)(2,1)S(1)}, u32[]{:S(2)}, u32[]{:S(2)}) %collective-permute-start.5) | collective-permute-done | bytes 131104 | tf_op jit(solution)/shard_map/ppermute | solution.py:182
  56.2 0.5 collective-permute-done.7.low_other
  56.7 0.9 %final.1 = bf16[128,512]{1,0:T(8,128)(2,1)} custom-call(f32[128,512]{1,0:T(8,128)S(1)} %get-tuple-element.45.own, bf16[128,512]{1,0:T(8,128)(2,1)S(1)} %collective-permute-done.4.far0, bf16[128,512]{1,0:T(8,128)(2,1)S(1)} %collective-permute-done.5.far1, bf16[128,512]{1,0:T(8,128)(2,1)S(1)} %collective-permute-done.6.far2, f32[128,64]{1,0:T(8,128)S(1)} %low_rank.1.low_mine, ...), custom_call_target="tpu_custom_call" | custom-call | flops 16777216 | bytes 3145728 | tf_op jit(solution)/shard_map/final/pallas_call | solution.py:148
  (25 shorter events, 0.1 us)
Async XLA Ops:
  0.0 1.2 %copy-start = (bf16[1024,512]{1,0:T(8,128)(2,1)S(1)}, bf16[1024,512]{1,0:T(8,128)(2,1)}, u32[]{:S(2)}) copy-start(bf16[1024,512]{1,0:T(8,128)(2,1)} %param.9) | copy-start | bytes 3145732
  1.3 27.4 %collective-permute-start = (bf16[512,512]{1,0:T(8,128)(2,1)S(1)}, bf16[512,512]{1,0:T(8,128)(2,1)S(1)}, u32[]{:S(2)}, u32[]{:S(2)}) collective-permute-start(bf16[512,512]{1,0:T(8,128)(2,1)S(1)} %constant_dynamic-slice_fusion.rest_0_), channel_id=1, source_target_pairs={{0,8},{2,10},{4,12},{6,14},{8,0},{10,2},{12,4},{14,6},{1,9},{3,11}... | collective-permute-start | bytes 1572872 | tf_op jit(solution)/shard_map/ppermute | solution.py:188
  5.4 23.6 %collective-permute-start.1 = (bf16[512,512]{1,0:T(8,128)(2,1)S(1)}, bf16[512,512]{1,0:T(8,128)(2,1)}, u32[]{:S(2)}, u32[]{:S(2)}) collective-permute-start(bf16[512,512]{1,0:T(8,128)(2,1)S(1)} %constant_dynamic-slice_fusion.rest_0_), channel_id=1, source_target_pairs={{0,4},{2,6},{4,0},{6,2},{8,12},{10,14},{12,8},{14,10},{1,5},{3,7},... | collective-permute-start | bytes 1572872 | tf_op jit(solution)/shard_map/ppermute | solution.py:188
  6.9 1.6 %copy-start.1 = (bf16[128,8192]{1,0:T(8,128)(2,1)S(1)}, bf16[128,8192]{1,0:T(8,128)(2,1)}, u32[]{:S(2)}) copy-start(bf16[128,8192]{1,0:T(8,128)(2,1)} %hidden.3) | copy-start | bytes 6291460
  8.5 0.7 %copy-start.7 = (bf16[8192]{0:T(1024)(128)(2,1)S(1)}, bf16[8192]{0:T(1024)(128)(2,1)}, u32[]{:S(2)}) copy-start(bf16[8192]{0:T(1024)(128)(2,1)} %gain.1) | copy-start | bytes 49156
  11.2 17.7 %all-to-all-start = ((bf16[4,64,2048]{2,1,0:T(8,128)(2,1)}), bf16[4,64,2048]{2,1,0:T(8,128)(2,1)S(1)}, u32[]{:S(2)}, u32[]{:S(2)}) async-start(bf16[4,64,2048]{2,1,0:T(8,128)(2,1)} %norm_send.1), calls=%async_computation | async-start | bytes 2097152 | tf_op jit(solution)/shard_map/all_to_all | solution.py:199
  14.9 3.4 %copy-start.9 = (bf16[128,1,512,64]{2,3,1,0:T(8,128)(2,1)S(1)}, bf16[128,1,512,64]{2,3,1,0:T(8,128)(2,1)}, u32[]{:S(2)}) copy-start(bf16[128,1,512,64]{2,3,1,0:T(8,128)(2,1)} %param.10) | copy-start | bytes 25165828
  18.3 1.2 %copy-start.10 = (bf16[128,1,4096]{2,0,1:T(8,128)(2,1)S(1)}, bf16[128,1,4096]{2,0,1:T(8,128)(2,1)}, u32[]{:S(2)}) copy-start(bf16[128,1,4096]{2,0,1:T(8,128)(2,1)} %param.11) | copy-start | bytes 3145732
  19.5 0.7 %copy-start.11 = (s32[8]{0:T(128)S(1)}, s32[8]{0:T(128)}, u32[]{:S(2)}) copy-start(s32[8]{0:T(128)} %seg.1) | copy-start | bytes 100
  20.2 0.7 %copy-start.12 = (s32[128]{0:T(128)S(1)}, s32[128]{0:T(128)}, u32[]{:S(2)}) copy-start(s32[128]{0:T(128)} %token_) | copy-start | bytes 1540
  20.8 20.5 %copy-start.13 = (s32[128]{0:T(128)S(1)}, s32[128]{0:T(128)}, u32[]{:S(2)}) copy-start(s32[128]{0:T(128)} %token_) | copy-start | bytes 1540
  28.9 2.7 %collective-permute-start.2 = (bf16[4,64,2048]{2,1,0:T(8,128)(2,1)S(1)}, bf16[4,64,2048]{2,1,0:T(8,128)(2,1)S(1)}, u32[]{:S(2)}, u32[]{:S(2)}) collective-permute-start(bf16[4,64,2048]{2,1,0:T(8,128)(2,1)S(1)} %all-to-all-done.mine), channel_id=1, source_target_pairs={{0,1},{1,0},{2,3},{3,2},{4,5},{5,4},{6,7},{7,6},{8,9},{9,8},{10,11... | collective-permute-start | bytes 3145736 | tf_op jit(solution)/shard_map/ppermute | solution.py:217
  28.9 14.8 %collective-permute-start.3 = (bf16[512,512]{1,0:T(8,128)(2,1)S(1)}, bf16[512,512]{1,0:T(8,128)(2,1)}, u32[]{:S(2)}, u32[]{:S(2)}) collective-permute-start(bf16[512,512]{1,0:T(8,128)(2,1)S(1)} %collective-permute-done.rest_2_), channel_id=1, source_target_pairs={{0,4},{2,6},{4,0},{6,2},{8,12},{10,14},{12,8},{14,10},{1,5},{3,7},... | collective-permute-start | bytes 1572872 | tf_op jit(solution)/shard_map/ppermute | solution.py:188
  33.6 1.0 %copy-start.3 = (f32[512,512]{1,0:T(8,128)}, f32[512,512]{1,0:T(8,128)S(1)}, u32[]{:S(2)}) copy-start(f32[512,512]{1,0:T(8,128)S(1)} %get-tuple-element.39.early) | copy-start | bytes 3145732
  34.7 0.8 %copy-start.5 = (bf16[512,512]{1,0:T(8,128)(2,1)}, bf16[512,512]{1,0:T(8,128)(2,1)S(1)}, u32[]{:S(2)}) copy-start(bf16[512,512]{1,0:T(8,128)(2,1)S(1)} %get-tuple-element.33.last) | copy-start | bytes 1572868
  35.5 19.5 %all-to-all-start.1 = ((bf16[8,72,512]{2,1,0:T(8,128)(2,1)}), bf16[8,72,512]{2,1,0:T(8,128)(2,1)S(1)}, u32[]{:S(2)}, u32[]{:S(2)}) async-start(bf16[8,72,512]{2,1,0:T(8,128)(2,1)} %pick_panels.1), calls=%async_computation.1 | async-start | bytes 1179648 | tf_op jit(solution)/shard_map/all_to_all | solution.py:249
  41.4 2.4 %copy-start.4 = (f32[512,512]{1,0:T(8,128)S(1)}, f32[512,512]{1,0:T(8,128)}, u32[]{:S(2)}) copy-start(f32[512,512]{1,0:T(8,128)} %copy-done.3) | copy-start | bytes 3145732
  41.4 2.4 %copy-start.6 = (bf16[512,512]{1,0:T(8,128)(2,1)S(1)}, bf16[512,512]{1,0:T(8,128)(2,1)}, u32[]{:S(2)}) copy-start(bf16[512,512]{1,0:T(8,128)(2,1)} %copy-done.5) | copy-start | bytes 1572868
  41.4 8.4 %copy-start.2 = (bf16[128,8192]{1,0:T(8,128)(2,1)S(1)}, bf16[128,8192]{1,0:T(8,128)(2,1)}, u32[]{:S(2)}) copy-start(bf16[128,8192]{1,0:T(8,128)(2,1)} %hidden.3) | copy-start | bytes 6291460
  41.4 8.4 %copy-start.8 = (bf16[8192]{0:T(1024)(128)(2,1)S(1)}, bf16[8192]{0:T(1024)(128)(2,1)}, u32[]{:S(2)}) copy-start(bf16[8192]{0:T(1024)(128)(2,1)} %gain.1) | copy-start | bytes 49156
  45.9 9.6 %collective-permute-start.4 = (bf16[128,512]{1,0:T(8,128)(2,1)}, bf16[128,512]{1,0:T(8,128)(2,1)S(1)}, u32[]{:S(2)}, u32[]{:S(2)}) collective-permute-start(bf16[128,512]{1,0:T(8,128)(2,1)} %get-tuple-element.46), channel_id=1, source_target_pairs={{0,18},{2,16},{4,22},{6,20},{8,26},{10,24},{12,30},{14,28},{16,2},... | collective-permute-start | bytes 393224 | tf_op jit(solution)/shard_map/ppermute | solution.py:182
  49.2 7.1 %collective-permute-start.5 = (bf16[128,512]{1,0:T(8,128)(2,1)}, bf16[128,512]{1,0:T(8,128)(2,1)S(1)}, u32[]{:S(2)}, u32[]{:S(2)}) collective-permute-start(bf16[128,512]{1,0:T(8,128)(2,1)} %get-tuple-element.47), channel_id=1, source_target_pairs={{0,2},{2,0},{4,6},{6,4},{8,10},{10,8},{12,14},{14,12},{16,18},{18,... | collective-permute-start | bytes 393224 | tf_op jit(solution)/shard_map/ppermute | solution.py:182
  49.2 7.1 %collective-permute-start.6 = (bf16[128,512]{1,0:T(8,128)(2,1)S(1)}, bf16[128,512]{1,0:T(8,128)(2,1)S(1)}, u32[]{:S(2)}, u32[]{:S(2)}) collective-permute-start(bf16[128,512]{1,0:T(8,128)(2,1)S(1)} %get-tuple-element.48), channel_id=1, source_target_pairs={{0,16},{2,18},{4,20},{6,22},{8,24},{10,26},{12,28},{14,30},{16,0},... | collective-permute-start | bytes 393224 | tf_op jit(solution)/shard_map/ppermute | solution.py:182
  55.4 1.3 %collective-permute-start.7 = (f32[128,64]{1,0:T(8,128)S(1)}, f32[128,64]{1,0:T(8,128)S(1)}, u32[]{:S(2)}, u32[]{:S(2)}) collective-permute-start(f32[128,64]{1,0:T(8,128)S(1)} %low_rank.1.low_mine), channel_id=1, source_target_pairs={{0,1},{1,0},{2,3},{3,2},{4,5},{5,4},{6,7},{7,6},{8,9},{9,8},{10,11... | collective-permute-start | bytes 98312 | tf_op jit(solution)/shard_map/ppermute | solution.py:257
